TPU v7x, 32 devices: a whole 2x2x4 slice. The times are simulated.
32 devices in a mesh: dp: 8 (over z, x), seq: 4 (over y, core).
Axes of the slice: x: 2, y: 2, z: 4, core: 2. Of those that a mesh axis runs over, the one named last changes fastest.
Arguments:
- short_in: bfloat16 [2, 32, 256, 768], P(None, 'dp', 'seq'), may hold values from -6 to 6
- long_in: bfloat16 [2, 16, 512, 768], P(None, 'dp', 'seq'), may hold values from -6 to 6
- short_cot: bfloat16 [2, 32, 256, 768], P(None, 'dp', 'seq'), may hold values from -6 to 6
- long_cot: bfloat16 [2, 16, 512, 768], P(None, 'dp', 'seq'), may hold values from -6 to 6
- short_len: int32 [2, 8, 4], P(None, 'dp'), may hold values from 0 to 256, as said below
- long_len: int32 [2, 8, 2], P(None, 'dp'), may hold values from 0 to 512, as said below
- wide_master: float32 [768, 6144], P('dp')
- down_master: float32 [3072, 768], P('dp'), may hold values from -0.109375 to 0.109375
- vector_master: float32 [768, 12], P('dp')
- wide_moment: float32 [768, 6144], P('dp'), may hold values from -256 to 256
- down_moment: float32 [3072, 768], P('dp'), may hold values from -256 to 256
- vector_moment: float32 [768, 12], P('dp'), may hold values from -256 to 256
- wide_average: float32 [768, 6144], P('dp'), may hold values from -0.21875 to 0.21875
- down_average: float32 [3072, 768], P('dp'), may hold values from -0.109375 to 0.109375
- vector_average: float32 [768, 12], P('dp'), may hold values from -6 to 6
Outputs:
- short_out: bfloat16 [2, 32, 256, 768], P(None, 'dp', 'seq')
- long_out: bfloat16 [2, 16, 512, 768], P(None, 'dp', 'seq')
- short_back: bfloat16 [2, 32, 256, 768], P(None, 'dp', 'seq')
- long_back: bfloat16 [2, 16, 512, 768], P(None, 'dp', 'seq')
- wide_grad: float32 [768, 6144], P('dp')
- down_grad: float32 [3072, 768], P('dp')
- vector_grad: float32 [768, 12], P('dp')
- wide_velocity: float32 [768, 6144], P('dp')
- down_velocity: float32 [3072, 768], P('dp')
- vector_velocity: float32 [768, 12], P('dp')
- wide_averaged: float32 [768, 6144], P('dp')
- down_averaged: float32 [3072, 768], P('dp')
- vector_averaged: float32 [768, 12], P('dp')
- wide_updated: float32 [768, 6144], P('dp')
- down_updated: float32 [3072, 768], P('dp')
- vector_updated: float32 [768, 12], P('dp')
- wide_copy: bfloat16 [768, 6144], P('dp')
- down_copy: bfloat16 [3072, 768], P('dp')
- vector_copy: bfloat16 [768, 12], P('dp')
Inputs may be any that keep to these rules, and one draw needn't show every extreme that they name: `short_len`: 0 marks an empty slot; in each micro-batch every index of dp has at least half of its slots live and one sequence of exactly 256 tokens. `long_len`: 0 marks an empty slot; in each micro-batch every index of dp has at least half of its slots live and one sequence of exactly 512 tokens.
All inputs are finite; a program needn't handle non-finite values.
Results may differ from a plain program's by a relative error of at most 0.015.
Values may be sent and summed in bfloat16 or wider, within the bound.
A program may use at most 256 MiB of HBM per device.

v0:
```python
import jax
import jax.numpy as jnp
from jax import lax
from jax.sharding import PartitionSpec as P

D = 768
HEAD_DIM = 64
FF = 3072


norm_eps = 1e-12
mask_fill = -10000.0
learning_rate = 0.0002
momentum_rate = 0.9
decay_weight = 0.0001
average_rate = 0.9


def norm_forward(inputs, gain, shift):
    centred = inputs - jnp.mean(inputs, axis=-1, keepdims=True)
    inverse = lax.rsqrt(jnp.mean(centred * centred, axis=-1, keepdims=True) + norm_eps)
    normed = centred * inverse
    return (normed * gain + shift, normed, inverse)


def norm_backward(grad_out, normed, inverse, gain):
    scaled = grad_out * gain
    grad_in = inverse * (
        scaled
        - jnp.mean(scaled, axis=-1, keepdims=True)
        - normed * jnp.mean(scaled * normed, axis=-1, keepdims=True)
    )
    return (grad_in, jnp.sum(grad_out * normed, axis=0), jnp.sum(grad_out, axis=0))


def transpose_dot(left, right):
    return jnp.einsum("ra,rb->ab", left, right, preferred_element_type=jnp.float32)


def right_dot(left, right):
    return jnp.einsum("ra,ba->rb", left, right, preferred_element_type=jnp.float32)


def weight_grads(factor_list):
    products = []
    for kind in range(4):
        left = jnp.concatenate([factors[kind][0] for factors in factor_list], axis=0)
        right = jnp.concatenate([factors[kind][1] for factors in factor_list], axis=0)
        products.append(transpose_dot(left, right))
    return products


def micro_step(tokens, cotangent, lengths, weights, spread):
    wide_w, down_w, vector_w = weights
    seq_count, local_len, model_width = tokens.shape
    row_count = seq_count * local_len
    parts_count = lax.axis_size("seq") if spread else 1
    full_len = local_len * parts_count
    head_width = model_width // parts_count
    local_heads = head_width // HEAD_DIM
    vector = vector_w.astype(jnp.float32)
    flat_rows = tokens.reshape(row_count, model_width)
    proj_bias = jnp.concatenate(
        [vector[:, 0], jnp.zeros((model_width,), jnp.float32), vector[:, 1]]
    )
    projected = (
        jnp.dot(flat_rows, wide_w[:, : 3 * model_width], preferred_element_type=jnp.float32)
        + proj_bias
    )
    stacked = projected.astype(jnp.bfloat16).reshape(seq_count, local_len, 3, model_width)
    if spread:
        headed = lax.all_to_all(stacked, "seq", split_axis=3, concat_axis=1, tiled=True)
    else:
        headed = stacked
    headed = headed.reshape(seq_count, full_len, 3, local_heads, HEAD_DIM)
    queries = headed[:, :, 0]
    key_rows = headed[:, :, 1]
    values = headed[:, :, 2]
    key_live = (jnp.arange(full_len)[None, :] < lengths[:, None])[:, None, None, :]
    score_scale = HEAD_DIM ** (-0.5)
    raw_scores = (
        jnp.einsum("bqhd,bkhd->bhqk", queries, key_rows, preferred_element_type=jnp.float32)
        * score_scale
    )
    scores = jnp.where(key_live, raw_scores, mask_fill)
    row_top = jnp.max(scores, axis=-1, keepdims=True)
    exponent = jnp.exp(scores - row_top)
    row_total = jnp.sum(exponent, axis=-1, keepdims=True)
    log_total = row_top + jnp.log(row_total)
    probs = (exponent / row_total).astype(jnp.bfloat16)
    attended = jnp.einsum("bhqk,bkhd->bqhd", probs, values, preferred_element_type=jnp.float32)
    attended = attended.astype(jnp.bfloat16).reshape(seq_count, full_len, head_width)
    if spread:
        gathered = lax.all_to_all(attended, "seq", split_axis=1, concat_axis=2, tiled=True)
    else:
        gathered = attended
    attn_rows = gathered.reshape(row_count, model_width)
    branch = (
        jnp.dot(
            attn_rows,
            wide_w[:, 3 * model_width : 4 * model_width],
            preferred_element_type=jnp.float32,
        )
        + vector[:, 2]
    )
    first, normed_one, inverse_one = norm_forward(
        flat_rows.astype(jnp.float32) + branch, vector[:, 3], vector[:, 4]
    )
    first_low = first.astype(jnp.bfloat16)
    bias_one = jnp.transpose(vector[:, 8:]).reshape(-1)
    inner_pre = (
        jnp.dot(first_low, wide_w[:, 4 * model_width :], preferred_element_type=jnp.float32)
        + bias_one
    )
    active = jax.nn.gelu(inner_pre, approximate=False).astype(jnp.bfloat16)
    branch_two = jnp.dot(active, down_w, preferred_element_type=jnp.float32) + vector[:, 5]
    result, normed_two, inverse_two = norm_forward(first + branch_two, vector[:, 6], vector[:, 7])
    output = result.astype(jnp.bfloat16).reshape(tokens.shape)
    offset = lax.axis_index("seq") * local_len if spread else 0
    position = offset + jnp.arange(local_len)
    live_rows = (position[None, :] < lengths[:, None]).astype(jnp.float32).reshape(row_count, 1)
    grad_out = cotangent.reshape(row_count, model_width).astype(jnp.float32) * live_rows
    grad_mid, grad_gain_two, grad_shift_two = norm_backward(
        grad_out, normed_two, inverse_two, vector[:, 6]
    )
    grad_mid_low = grad_mid.astype(jnp.bfloat16)
    grad_active = right_dot(grad_mid_low, down_w)
    normal_cdf = 0.5 * (1.0 + jax.scipy.special.erf(inner_pre * 0.5**0.5))
    normal_pdf = jnp.exp(-0.5 * inner_pre * inner_pre) * (2.0 * jnp.pi) ** (-0.5)
    grad_inner = (grad_active * (normal_cdf + inner_pre * normal_pdf)).astype(jnp.bfloat16)
    grad_first = grad_mid + right_dot(grad_inner, wide_w[:, 4 * model_width :])
    grad_resid, grad_gain_one, grad_shift_one = norm_backward(
        grad_first, normed_one, inverse_one, vector[:, 3]
    )
    grad_resid_low = grad_resid.astype(jnp.bfloat16)
    grad_attended = right_dot(grad_resid_low, wide_w[:, 3 * model_width : 4 * model_width])
    grad_attended = grad_attended.astype(jnp.bfloat16).reshape(seq_count, local_len, model_width)
    if spread:
        grad_headed = lax.all_to_all(grad_attended, "seq", split_axis=2, concat_axis=1, tiled=True)
    else:
        grad_headed = grad_attended
    grad_heads = grad_headed.reshape(seq_count, full_len, local_heads, HEAD_DIM)
    again_scores = jnp.where(
        key_live,
        jnp.einsum("bqhd,bkhd->bhqk", queries, key_rows, preferred_element_type=jnp.float32)
        * score_scale,
        mask_fill,
    )
    prob_exact = jnp.exp(again_scores - log_total)
    grad_probs = jnp.einsum(
        "bqhd,bkhd->bhqk", grad_heads, values, preferred_element_type=jnp.float32
    )
    grad_scores = prob_exact * (
        grad_probs - jnp.sum(prob_exact * grad_probs, axis=-1, keepdims=True)
    )
    grad_scores = jnp.where(key_live, grad_scores, 0.0).astype(jnp.bfloat16)
    grad_query = (
        jnp.einsum("bhqk,bkhd->bqhd", grad_scores, key_rows, preferred_element_type=jnp.float32)
        * score_scale
    )
    grad_key = (
        jnp.einsum("bhqk,bqhd->bkhd", grad_scores, queries, preferred_element_type=jnp.float32)
        * score_scale
    )
    grad_value = jnp.einsum(
        "bhqk,bqhd->bkhd", probs, grad_heads, preferred_element_type=jnp.float32
    )
    grad_stack = jnp.stack([grad_query, grad_key, grad_value], axis=2)
    grad_stack = grad_stack.astype(jnp.bfloat16).reshape(seq_count, full_len, 3, head_width)
    if spread:
        grad_local = lax.all_to_all(grad_stack, "seq", split_axis=1, concat_axis=3, tiled=True)
    else:
        grad_local = grad_stack
    grad_proj = grad_local.reshape(row_count, 3 * model_width)
    grad_input = grad_resid + right_dot(grad_proj, wide_w[:, : 3 * model_width])
    back = grad_input.astype(jnp.bfloat16).reshape(tokens.shape)
    proj_sums = jnp.sum(grad_proj.astype(jnp.float32), axis=0)
    grad_bias_one = jnp.sum(grad_inner.astype(jnp.float32), axis=0)
    grad_columns = jnp.stack(
        [
            proj_sums[:model_width],
            proj_sums[2 * model_width :],
            jnp.sum(grad_resid_low.astype(jnp.float32), axis=0),
            grad_gain_one,
            grad_shift_one,
            jnp.sum(grad_mid_low.astype(jnp.float32), axis=0),
            grad_gain_two,
            grad_shift_two,
        ],
        axis=1,
    )
    grad_vector = jnp.concatenate(
        [grad_columns, jnp.transpose(grad_bias_one.reshape(-1, model_width))], axis=1
    )
    factors = (
        (flat_rows, grad_proj),
        (attn_rows, grad_resid_low),
        (first_low, grad_inner),
        (active, grad_mid_low),
    )
    return (output, back, factors, grad_vector)


def update(master, reduced_grad, moment, average):
    step_grad = reduced_grad + decay_weight * master
    velocity = momentum_rate * moment + step_grad
    updated = master - learning_rate * (step_grad + momentum_rate * velocity)
    averaged = average_rate * average + (1.0 - average_rate) * updated
    return (velocity, averaged, updated, updated.astype(jnp.bfloat16))


def body(
    short_in,
    long_in,
    short_cot,
    long_cot,
    short_len,
    long_len,
    wide_master,
    down_master,
    vector_master,
    wide_moment,
    down_moment,
    vector_moment,
    wide_average,
    down_average,
    vector_average,
):
    weights = (
        lax.all_gather(wide_master.astype(jnp.bfloat16), "dp", axis=0, tiled=True),
        lax.all_gather(down_master.astype(jnp.bfloat16), "dp", axis=0, tiled=True),
        lax.all_gather(vector_master.astype(jnp.bfloat16), "dp", axis=0, tiled=True),
    )
    own_rows = wide_master.shape[0]
    sums = (
        jnp.zeros((own_rows, 3 * D), jnp.float32),
        jnp.zeros((own_rows, D), jnp.float32),
        jnp.zeros((own_rows, FF), jnp.float32),
        jnp.zeros(down_master.shape, jnp.float32),
        jnp.zeros(vector_master.shape, jnp.float32),
    )
    factor_list = []
    vector_total = jnp.zeros(weights[2].shape, jnp.float32)
    bucket_results = []
    for bucket_index, (tokens, cotangent, lengths) in enumerate(
        ((short_in, short_cot, short_len), (long_in, long_cot, long_len))
    ):
        outputs = []
        backs = []
        for micro_index in range(tokens.shape[0]):
            micro_tokens = tokens[micro_index]
            micro_cot = cotangent[micro_index]
            micro_len = lengths[micro_index, 0]
            if bucket_index == 0:
                own_count = micro_tokens.shape[0] // lax.axis_size("seq")
                whole_tokens, whole_cot = (
                    lax.all_to_all(micro_tokens, "seq", split_axis=0, concat_axis=1, tiled=True),
                    lax.all_to_all(micro_cot, "seq", split_axis=0, concat_axis=1, tiled=True),
                )
                own_len = lax.dynamic_slice_in_dim(
                    micro_len, lax.axis_index("seq") * own_count, own_count
                )
                whole_out, whole_back, factors, grad_vector = micro_step(
                    whole_tokens, whole_cot, own_len, weights, False
                )
                output, back = (
                    lax.all_to_all(whole_out, "seq", split_axis=1, concat_axis=0, tiled=True),
                    lax.all_to_all(whole_back, "seq", split_axis=1, concat_axis=0, tiled=True),
                )
            else:
                output, back, factors, grad_vector = micro_step(
                    micro_tokens, micro_cot, micro_len, weights, True
                )
            factor_list.append(factors)
            vector_total = vector_total + grad_vector
            outputs.append(output)
            backs.append(back)
        bucket_results.append((jnp.stack(outputs), jnp.stack(backs)))
    products = weight_grads(factor_list)
    sums = (
        lax.psum_scatter(products[0], "dp", scatter_dimension=0, tiled=True),
        lax.psum_scatter(products[1], "dp", scatter_dimension=0, tiled=True),
        lax.psum_scatter(products[2], "dp", scatter_dimension=0, tiled=True),
        lax.psum_scatter(products[3], "dp", scatter_dimension=0, tiled=True),
        lax.psum_scatter(vector_total, "dp", scatter_dimension=0, tiled=True),
    )
    reduced = (
        lax.psum(sums[0].astype(jnp.bfloat16), "seq").astype(jnp.float32),
        lax.psum(sums[1].astype(jnp.bfloat16), "seq").astype(jnp.float32),
        lax.psum(sums[2].astype(jnp.bfloat16), "seq").astype(jnp.float32),
        lax.psum(sums[3].astype(jnp.bfloat16), "seq").astype(jnp.float32),
        lax.psum(sums[4].astype(jnp.bfloat16), "seq").astype(jnp.float32),
    )
    wide_reduced = jnp.concatenate([reduced[0], reduced[1], reduced[2]], axis=1)
    down_reduced = reduced[3]
    vector_reduced = reduced[4]
    wide_new = update(wide_master, wide_reduced, wide_moment, wide_average)
    down_new = update(down_master, down_reduced, down_moment, down_average)
    vector_new = update(vector_master, vector_reduced, vector_moment, vector_average)
    return (
        bucket_results[0][0],
        bucket_results[1][0],
        bucket_results[0][1],
        bucket_results[1][1],
        wide_reduced,
        down_reduced,
        vector_reduced,
        wide_new[0],
        down_new[0],
        vector_new[0],
        wide_new[1],
        down_new[1],
        vector_new[1],
        wide_new[2],
        down_new[2],
        vector_new[2],
        wide_new[3],
        down_new[3],
        vector_new[3],
    )


def solution(mesh):
    return jax.shard_map(
        body,
        mesh=mesh,
        in_specs=(
            P(None, "dp", "seq", None),
            P(None, "dp", "seq", None),
            P(None, "dp", "seq", None),
            P(None, "dp", "seq", None),
            P(None, "dp", None),
            P(None, "dp", None),
            P("dp", None),
            P("dp", None),
            P("dp", None),
            P("dp", None),
            P("dp", None),
            P("dp", None),
            P("dp", None),
            P("dp", None),
            P("dp", None),
        ),
        out_specs=(
            P(None, "dp", "seq", None),
            P(None, "dp", "seq", None),
            P(None, "dp", "seq", None),
            P(None, "dp", "seq", None),
            P("dp", None),
            P("dp", None),
            P("dp", None),
            P("dp", None),
            P("dp", None),
            P("dp", None),
            P("dp", None),
            P("dp", None),
            P("dp", None),
            P("dp", None),
            P("dp", None),
            P("dp", None),
            P("dp", None),
            P("dp", None),
            P("dp", None),
        ),
        check_vma=False,
    )
```

profile of v0, /device:TPU:0, one launch (start us, length us, event | category | flops | bytes accessed | tf_op | source)
XLA Modules:
  0.0 1123.0 jit_solution(16164182160932773514)
XLA Ops:
  11.2 4.4 all-to-all-start.8
  20.8 32.3 %all-gather = bf16[8,96,12]{1,2,0:T(8,128)(2,1)S(1)} all-gather(bf16[1,96,12]{1,2,0:T(8,128)(2,1)S(1)} %convert_bitcast_fusion), channel_id=1, replica_groups=mesh['dp'=8,'seq'=4] {'dp'}, dimensions={0}, use_global_device_ids=true | all-gather | bytes 20736 | tf_op jit(solution)/shard_map/all_gather | solution.py:232
  58.9 3.5 all-to-all-start.10
  65.1 4.7 all-to-all-done.10
  69.8 3.5 all-to-all-start.2
  75.5 5.2 all-to-all-done.2
  80.7 3.5 all-to-all-start
  84.2 67.5 %all-gather.4.cloned.1.call-done = bf16[768,6144]{1,0:T(8,128)(2,1)} async-done(((bf16[96,6144]{1,0:T(8,128)(2,1)}), bf16[768,6144]{1,0:T(8,128)(2,1)}) %all-gather.4.cloned.1.call-update) | async-done | bytes 9437200 | tf_op jit(solution)/shard_map/all_gather | solution.py:230
  155.4 3.6 fusion.42
  160.9 5.0 copy.368
  170.9 5.0 copy.375
  175.8 4.5 all-to-all-start.4
  180.4 4.1 fusion.40
  196.6 3.8 all-to-all-start.6
  209.4 6.8 all-to-all-done.6
  230.6 3.5 all-to-all-start.7
  245.2 3.9 all-to-all-start.5
  251.8 6.2 all-to-all-done.5
  267.0 10.8 fusion.66
  277.8 4.5 fusion.382
  282.6 9.5 fusion.63
  295.0 9.8 fusion.69
  306.5 9.6 fusion.60
  343.6 3.6 convert_reduce_fusion.11
  359.6 4.1 all-to-all-start.14
  372.7 4.0 fusion.177
  376.7 6.7 fusion.241
  383.4 6.7 fusion.247
  393.3 4.1 all-to-all-start.12
  414.6 4.9 fusion.316
  419.5 11.7 %fusion.269 = bf16[2,3,64,512]{3,2,1,0:T(8,128)(2,1)S(1)} fusion(f32[2,3,512,512]{2,3,1,0:T(8,128)} %fusion.316, f32[2,3,512,512]{2,3,1,0:T(8,128)} %copy-done.1, f32[2,3,512]{2,1,0:T(4,128)S(1)} %copy-done.104, pred[2,512]{1,0:T(4,128)(4,1)S(1)} %copy-done.85, bf16[2,512,3,3,64]{1,4,3,0,2:T(8,128)(2,1)S(1)} %copy-done.18), kind=kOutput, calls=%fused_computation.309 | convolution fusion | flops 219024896 | bytes 25989120 | tf_op jit(solution)/shard_map/bhqk,bkhd->bqhd/dot_general | solution.py:158
  431.7 11.9 %fusion.266 = bf16[2,3,64,512]{3,2,1,0:T(8,128)(2,1)S(1)} fusion(f32[2,3,512,512]{2,3,1,0:T(8,128)} %fusion.316, f32[2,3,512,512]{2,3,1,0:T(8,128)} %copy-done.1, f32[2,3,512]{2,1,0:T(4,128)S(1)} %copy-done.104, pred[2,512]{1,0:T(4,128)(4,1)S(1)} %copy-done.85, bf16[2,512,3,3,64]{1,4,3,0,2:T(8,128)(2,1)S(1)} %copy-done.18), kind=kOutput, calls=%fused_computation.308 | convolution fusion | flops 219024896 | bytes 25989120 | tf_op jit(solution)/shard_map/bhqk,bqhd->bkhd/dot_general | solution.py:162
  447.4 3.7 all-to-all-start.13
  451.1 3.7 fusion.318
  454.8 11.6 %fusion.275 = bf16[2,3,64,512]{3,2,1,0:T(8,128)(2,1)S(1)} fusion(f32[2,3,512,512]{2,3,1,0:T(8,128)} %fusion.318, f32[2,3,512,512]{2,3,1,0:T(8,128)} %copy-done, f32[2,3,512]{2,1,0:T(4,128)} %log_add_fusion, pred[2,512]{1,0:T(4,128)(4,1)S(1)} %copy-done.83, bf16[2,512,3,3,64]{1,4,3,0,2:T(8,128)(2,1)S(1)} %copy-done.17), kind=kOutput, calls=%fused_computation.311 | convolution fusion | flops 219024896 | bytes 25989120 | tf_op jit(solution)/shard_map/bhqk,bkhd->bqhd/dot_general | solution.py:158
  467.5 11.8 %fusion.272 = bf16[2,3,64,512]{3,2,1,0:T(8,128)(2,1)S(1)} fusion(f32[2,3,512,512]{2,3,1,0:T(8,128)} %fusion.318, f32[2,3,512,512]{2,3,1,0:T(8,128)} %copy-done, f32[2,3,512]{2,1,0:T(4,128)} %log_add_fusion, pred[2,512]{1,0:T(4,128)(4,1)S(1)} %copy-done.83, bf16[2,512,3,3,64]{1,4,3,0,2:T(8,128)(2,1)S(1)} %copy-done.17), kind=kOutput, calls=%fused_computation.310 | convolution fusion | flops 219024896 | bytes 25989120 | tf_op jit(solution)/shard_map/bhqk,bqhd->bkhd/dot_general | solution.py:162
  480.4 4.9 pad_maximum_fusion.1
  485.3 4.4 all-to-all-start.15
  492.0 6.9 fusion.253
  498.9 6.9 fusion.259
  514.9 3.6 copy.413
  520.8 7.7 fusion.28
  528.6 9.9 fusion.4
  538.6 10.5 fusion.12
  552.2 4.7 reduce.54
  558.7 4.1 all-to-all-start.3
  578.0 4.7 reduce.55
  607.6 4.3 all-to-all-start.1
  611.9 3.7 fusion.282
  617.1 4.7 reduce.56
  623.6 4.1 all-to-all-start.11
  627.7 3.7 fusion.283
  632.9 4.7 reduce.57
  639.4 4.1 all-to-all-start.9
  665.5 3.3 reshape.976
  670.8 3.3 reshape.978
  685.0 4.5 fusion.280
  693.1 130.0 %reduce-scatter.12.cloned.1.call-done = f32[96,3072]{1,0:T(8,128)} async-done(((f32[768,3072]{1,0:T(8,128)}), f32[96,3072]{1,0:T(8,128)}) %reduce-scatter.12.cloned.1.call-update) | async-done | bytes 1179664 | tf_op jit(solution)/shard_map/reduce_scatter | solution.py:283
  825.3 164.3 %reduce-scatter.14.cloned.1.call-done = f32[384,768]{1,0:T(8,128)} async-done(((f32[3072,768]{1,0:T(8,128)}), f32[384,768]{1,0:T(8,128)}) %reduce-scatter.14.cloned.1.call-update) | async-done | bytes 1179664 | tf_op jit(solution)/shard_map/reduce_scatter | solution.py:284
  991.8 3.5 fusion.281
  996.2 58.1 %reduce-scatter.16.cloned.1.call-done = f32[96,12]{1,0:T(8,128)} async-done(((f32[768,12]{1,0:T(8,128)}), f32[96,12]{1,0:T(8,128)}) %reduce-scatter.16.cloned.1.call-update) | async-done | bytes 4624
  1055.2 5.7 psum.39
  1062.8 41.7 %all-reduce.3.cloned.1.call-done = (bf16[96,3072]{1,0:T(8,128)(2,1)}, bf16[96,768]{1,0:T(8,128)(2,1)}, bf16[96,2304]{1,0:T(8,128)(2,1)}, bf16[384,768]{1,0:T(8,128)(2,1)}) async-done(((bf16[96,3072]{1,0:T(8,128)(2,1)}, bf16[96,768]{1,0:T(8,128)(2,1)}, bf16[96,2304]{1,0:T(8,128)(2,1)}, bf16[384,768]{1,0:T(8,128)(2,1)}), (bf16[96,3072]{1,0:T(8,128)(2,1)}, bf16[96,768]{1,0:T(8,128)(2,1)}, ...) | async-done | bytes 1769488 | tf_op jit(solution)/shard_map/psum | solution.py:290
  1110.4 3.4 fusion.366
  (572 shorter events, 287.5 us)
Async XLA Ops:
  7.2 144.5 %all-gather.4.cloned.1.call-start = ((), (), s32[]{:S(2)}) async-start(), calls=%async_computation.21 | async-start | bytes 10616832 | tf_op jit(solution)/shard_map/all_gather | solution.py:230
  10.2 10.6 copy-start.89
  10.2 43.7 %copy-start.132 = (s32[2,1,2]{2,1,0:T(1,128)S(1)}, s32[2,1,2]{2,1,0:T(1,128)}, u32[]{:S(2)}) copy-start(s32[2,1,2]{2,1,0:T(1,128)} %param.20) | copy-start | bytes 52
  10.2 45.1 %copy-start.14 = (bf16[2,2,128,768]{3,2,1,0:T(8,128)(2,1)S(1)}, bf16[2,2,128,768]{3,2,1,0:T(8,128)(2,1)}, u32[]{:S(2)}) copy-start(bf16[2,2,128,768]{3,2,1,0:T(8,128)(2,1)} %param.18) | copy-start | bytes 2359300
  11.2 46.8 %copy-start.44 = (bf16[2,4,64,768]{3,2,1,0:T(8,128)(2,1)S(1)}, bf16[2,4,64,768]{3,2,1,0:T(8,128)(2,1)}, u32[]{:S(2)}) copy-start(bf16[2,4,64,768]{3,2,1,0:T(8,128)(2,1)} %param.15) | copy-start | bytes 2359300
  11.2 47.7 %all-to-all-start.8 = ((bf16[4,64,768]{2,1,0:T(8,128)(2,1)}), bf16[4,64,768]{2,1,0:T(8,128)(2,1)S(1)}, u32[]{:S(2)}, u32[]{:S(2)}) async-start(bf16[4,64,768]{2,1,0:T(8,128)(2,1)} %get-tuple-element.113), calls=%async_computation.8 | async-start | bytes 786432 | tf_op jit(solution)/shard_map/all_to_all | solution.py:258
  15.5 262.2 %all-gather.6.cloned.1.call-start = ((), (), s32[]{:S(2)}) async-start(), calls=%async_computation.22 | async-start | bytes 5308416 | tf_op jit(solution)/shard_map/all_gather | solution.py:231
  16.4 47.7 %copy-start.45 = (bf16[2,2,128,768]{3,2,1,0:T(8,128)(2,1)S(1)}, bf16[2,2,128,768]{3,2,1,0:T(8,128)(2,1)}, u32[]{:S(2)}) copy-start(bf16[2,2,128,768]{3,2,1,0:T(8,128)(2,1)} %param.16) | copy-start | bytes 2359300
  53.9 20.3 %copy-start.75 = (f32[768]{0:T(1024)}, f32[768]{0:T(1024)S(1)}, u32[]{:S(2)}) copy-start(f32[768]{0:T(1024)S(1)} %get-tuple-element.53) | copy-start | bytes 9220
  58.9 92.7 %copy-start.25 = (bf16[4,64,768]{2,1,0:T(8,128)(2,1)}, bf16[4,64,768]{2,1,0:T(8,128)(2,1)S(1)}, u32[]{:S(2)}) copy-start(bf16[4,64,768]{2,1,0:T(8,128)(2,1)S(1)} %all-to-all-done.8) | copy-start | bytes 1179652
  58.9 10.9 all-to-all-start.10
  69.8 10.9 all-to-all-start.2
  80.7 74.1 %copy-start.65 = (bf16[4,64,768]{2,1,0:T(8,128)(2,1)}, bf16[4,64,768]{2,1,0:T(8,128)(2,1)S(1)}, u32[]{:S(2)}) copy-start(bf16[4,64,768]{2,1,0:T(8,128)(2,1)S(1)} %all-to-all-done.2) | copy-start | bytes 1179652
  80.7 95.1 %all-to-all-start = ((bf16[4,64,768]{2,1,0:T(8,128)(2,1)}), bf16[4,64,768]{2,1,0:T(8,128)(2,1)S(1)}, u32[]{:S(2)}, u32[]{:S(2)}) async-start(bf16[4,64,768]{2,1,0:T(8,128)(2,1)} %get-tuple-element.117), calls=%async_computation | async-start | bytes 786432 | tf_op jit(solution)/shard_map/all_to_all | solution.py:257
  155.4 38.5 %copy-start.21 = (bf16[256,2304]{0,1:T(8,128)(2,1)}, bf16[256,2304]{0,1:T(8,128)(2,1)S(1)}, u32[]{:S(2)}) copy-start(bf16[256,2304]{0,1:T(8,128)(2,1)S(1)} %copy.364) | copy-start | bytes 3538948
  175.8 20.8 %all-to-all-start.4 = ((bf16[2,128,3,768]{1,0,2,3:T(2,128)(2,1)}), bf16[2,128,3,768]{1,0,2,3:T(2,128)(2,1)}, u32[]{:S(2)}, u32[]{:S(2)}) async-start(bf16[2,128,3,768]{1,0,2,3:T(2,128)(2,1)} %copy.368), calls=%async_computation.4 | async-start | bytes 2359296 | tf_op jit(solution)/shard_map/all_to_all | solution.py:72
  196.4 9.8 copy-start.93
  196.6 19.6 %all-to-all-start.6 = ((bf16[2,128,3,768]{1,0,2,3:T(2,128)(2,1)}), bf16[2,128,3,768]{1,0,2,3:T(2,128)(2,1)S(1)}, u32[]{:S(2)}, u32[]{:S(2)}) async-start(bf16[2,128,3,768]{1,0,2,3:T(2,128)(2,1)} %copy.375), calls=%async_computation.6 | async-start | bytes 2359296 | tf_op jit(solution)/shard_map/all_to_all | solution.py:72
  209.4 11.4 %copy-start.82 = (pred[2,512]{1,0:T(4,128)(4,1)S(1)}, pred[2,512]{1,0:T(4,128)(4,1)}, u32[]{:S(2)}) copy-start(pred[2,512]{1,0:T(4,128)(4,1)} %get-tuple-element.209) | copy-start | bytes 3076
  230.6 14.6 %all-to-all-start.7 = ((bf16[2,512,192]{2,0,1:T(2,128)(2,1)}), bf16[2,512,192]{2,0,1:T(2,128)(2,1)S(1)}, u32[]{:S(2)}, u32[]{:S(2)}) async-start(bf16[2,512,192]{2,0,1:T(2,128)(2,1)} %copy.379), calls=%async_computation.7 | async-start | bytes 1048576 | tf_op jit(solution)/shard_map/all_to_all | solution.py:94
  244.1 16.0 %copy-start.129 = (f32[768]{0:T(1024)S(1)}, f32[768]{0:T(1024)}, u32[]{:S(2)}) copy-start(f32[768]{0:T(1024)} %get-tuple-element.58) | copy-start | bytes 9220
  245.2 12.7 %all-to-all-start.5 = ((bf16[2,512,192]{2,0,1:T(2,128)(2,1)}), bf16[2,512,192]{2,0,1:T(2,128)(2,1)S(1)}, u32[]{:S(2)}, u32[]{:S(2)}) async-start(bf16[2,512,192]{2,0,1:T(2,128)(2,1)} %copy.372), calls=%async_computation.5 | async-start | bytes 1048576 | tf_op jit(solution)/shard_map/all_to_all | solution.py:94
  264.3 13.5 %copy-start.32 = (f32[256,768]{1,0:T(8,128)}, f32[256,768]{1,0:T(8,128)S(1)}, u32[]{:S(2)}) copy-start(f32[256,768]{1,0:T(8,128)S(1)} %get-tuple-element.170) | copy-start | bytes 2359300
  277.8 14.3 %slice-start.3 = ((s8[4718592]{0:T(1024)(128)(4,1)}), s8[4194304]{0:T(1024)(128)(4,1)S(1)}, s32[]{:S(2)}) async-start(s8[4718592]{0:T(1024)(128)(4,1)} %bitcast.462), calls=%async_computation.32 | async-start | bytes 8388608
  277.8 17.1 %slice-start = ((s8[9437184]{0:T(1024)(128)(4,1)}), s8[4194304]{0:T(1024)(128)(4,1)S(1)}, s32[]{:S(2)}) async-start(s8[9437184]{0:T(1024)(128)(4,1)} %bitcast.460), calls=%async_computation.29 | async-start | bytes 8388608
  282.6 9.6 copy-start.96
  282.6 9.6 copy-start.112
  282.6 9.6 copy-start.127
  282.6 9.6 slice-start.4
  282.6 12.3 %slice-start.1 = ((s8[9437184]{0:T(1024)(128)(4,1)}), s8[4194304]{0:T(1024)(128)(4,1)S(1)}, s32[]{:S(2)}) async-start(s8[9437184]{0:T(1024)(128)(4,1)} %bitcast.460), calls=%async_computation.30 | async-start | bytes 8388608
  282.6 12.3 %slice-start.2 = ((s8[9437184]{0:T(1024)(128)(4,1)}), s8[1048576]{0:T(1024)(128)(4,1)S(1)}, s32[]{:S(2)}) async-start(s8[9437184]{0:T(1024)(128)(4,1)} %bitcast.460), calls=%async_computation.31 | async-start | bytes 2097152
  295.0 9.8 copy-start.114
  306.5 9.7 copy-start.110
  322.0 17.7 %copy-start.61 = (bf16[256,768]{1,0:T(8,128)(2,1)}, bf16[256,768]{1,0:T(8,128)(2,1)S(1)}, u32[]{:S(2)}) copy-start(bf16[256,768]{1,0:T(8,128)(2,1)S(1)} %get-tuple-element.100) | copy-start | bytes 1179652
  324.3 10.9 copy-start.63
  354.5 9.3 copy-start.52
  359.6 33.7 %all-to-all-start.14 = ((bf16[2,128,768]{1,0,2:T(2,128)(2,1)}), bf16[2,128,768]{1,0,2:T(2,128)(2,1)}, u32[]{:S(2)}, u32[]{:S(2)}) async-start(bf16[2,128,768]{1,0,2:T(2,128)(2,1)} %copy.403), calls=%async_computation.14 | async-start | bytes 786432 | tf_op jit(solution)/shard_map/all_to_all | solution.py:139
  363.7 325.8 %reduce-scatter.10.cloned.1.call-start = ((), (), s32[]{:S(2)}) async-start(), calls=%async_computation.24 | async-start | bytes 2654208 | tf_op jit(solution)/shard_map/reduce_scatter | solution.py:282
  363.8 8.8 copy-start.49
  390.1 11.4 %copy-start.5 = (bf16[2,3,512,512]{2,3,1,0:T(8,128)(2,1)S(1)}, bf16[2,3,512,512]{2,3,1,0:T(8,128)(2,1)}, u32[]{:S(2)}) copy-start(bf16[2,3,512,512]{2,3,1,0:T(8,128)(2,1)} %copy-done.4) | copy-start | bytes 9437188
  393.3 13.1 %all-to-all-start.12 = ((bf16[2,128,768]{1,0,2:T(2,128)(2,1)}), bf16[2,128,768]{1,0,2:T(2,128)(2,1)}, u32[]{:S(2)}, u32[]{:S(2)}) async-start(bf16[2,128,768]{1,0,2:T(2,128)(2,1)} %copy.391), calls=%async_computation.12 | async-start | bytes 786432 | tf_op jit(solution)/shard_map/all_to_all | solution.py:139
  447.4 37.9 %all-to-all-start.13 = ((bf16[2,512,3,192]{3,0,2,1:T(2,128)(2,1)}), bf16[2,512,3,192]{3,0,2,1:T(2,128)(2,1)S(1)}, u32[]{:S(2)}, u32[]{:S(2)}) async-start(bf16[2,512,3,192]{3,0,2,1:T(2,128)(2,1)} %pad_maximum_fusion), calls=%async_computation.13 | async-start | bytes 3145728 | tf_op jit(solution)/shard_map/all_to_all | solution.py:171
  480.4 9.3 copy-start.20
  485.3 29.6 %all-to-all-start.15 = ((bf16[2,512,3,192]{3,0,2,1:T(2,128)(2,1)}), bf16[2,512,3,192]{3,0,2,1:T(2,128)(2,1)}, u32[]{:S(2)}, u32[]{:S(2)}) async-start(bf16[2,512,3,192]{3,0,2,1:T(2,128)(2,1)} %pad_maximum_fusion.1), calls=%async_computation.15 | async-start | bytes 3145728 | tf_op jit(solution)/shard_map/all_to_all | solution.py:171
  489.7 201.5 %reduce-scatter.8.cloned.1.call-start = ((), (), s32[]{:S(2)}) async-start(), calls=%async_computation.23 | async-start | bytes 7962624 | tf_op jit(solution)/shard_map/reduce_scatter | solution.py:281
  528.6 294.6 %reduce-scatter.12.cloned.1.call-start = ((), (), s32[]{:S(2)}) async-start(), calls=%async_computation.25 | async-start | bytes 10616832 | tf_op jit(solution)/shard_map/reduce_scatter | solution.py:283
  538.5 451.0 %reduce-scatter.14.cloned.1.call-start = ((), (), s32[]{:S(2)}) async-start(), calls=%async_computation.26 | async-start | bytes 10616832 | tf_op jit(solution)/shard_map/reduce_scatter | solution.py:284
  549.1 13.8 %copy-start.98 = (f32[768]{0:T(1024)S(1)}, f32[768]{0:T(1024)}, u32[]{:S(2)}) copy-start(f32[768]{0:T(1024)} %get-tuple-element.43) | copy-start | bytes 9220
  549.1 14.3 %copy-start.97 = (f32[768]{0:T(1024)S(1)}, f32[768]{0:T(1024)}, u32[]{:S(2)}) copy-start(f32[768]{0:T(1024)} %get-tuple-element.44) | copy-start | bytes 9220
  549.1 14.9 %copy-start.100 = (f32[768]{0:T(1024)S(1)}, f32[768]{0:T(1024)}, u32[]{:S(2)}) copy-start(f32[768]{0:T(1024)} %get-tuple-element.51) | copy-start | bytes 9220
  549.1 15.5 %copy-start.99 = (f32[768]{0:T(1024)S(1)}, f32[768]{0:T(1024)}, u32[]{:S(2)}) copy-start(f32[768]{0:T(1024)} %get-tuple-element.156) | copy-start | bytes 9220
  558.7 48.9 %all-to-all-start.3 = ((bf16[4,2,24576]{2,1,0:T(2,128)(2,1)}), bf16[4,2,24576]{2,1,0:T(2,128)(2,1)}, u32[]{:S(2)}, u32[]{:S(2)}) async-start(bf16[4,2,24576]{2,1,0:T(2,128)(2,1)} %reshape.971), calls=%async_computation.3 | async-start | bytes 786432 | tf_op jit(solution)/shard_map/all_to_all | solution.py:267
  564.6 23.2 %copy-start.101 = (f32[768]{0:T(1024)S(1)}, f32[768]{0:T(1024)}, u32[]{:S(2)}) copy-start(f32[768]{0:T(1024)} %get-tuple-element.108) | copy-start | bytes 9220
  607.6 16.0 %all-to-all-start.1 = ((bf16[4,2,24576]{2,1,0:T(2,128)(2,1)}), bf16[4,2,24576]{2,1,0:T(2,128)(2,1)}, u32[]{:S(2)}, u32[]{:S(2)}) async-start(bf16[4,2,24576]{2,1,0:T(2,128)(2,1)} %reshape.973), calls=%async_computation.1 | async-start | bytes 786432 | tf_op jit(solution)/shard_map/all_to_all | solution.py:267
  623.6 15.8 %all-to-all-start.11 = ((bf16[4,2,24576]{2,1,0:T(2,128)(2,1)}), bf16[4,2,24576]{2,1,0:T(2,128)(2,1)}, u32[]{:S(2)}, u32[]{:S(2)}) async-start(bf16[4,2,24576]{2,1,0:T(2,128)(2,1)} %reshape.975), calls=%async_computation.11 | async-start | bytes 786432 | tf_op jit(solution)/shard_map/all_to_all | solution.py:268
  631.4 18.9 %copy-start.106 = (f32[768,1]{0,1:T(1,128)S(1)}, f32[768,1]{0,1:T(1,128)}, u32[]{:S(2)}) copy-start(f32[768,1]{0,1:T(1,128)} %stack.187) | copy-start | bytes 9220
  639.4 31.4 %all-to-all-start.9 = ((bf16[4,2,24576]{2,1,0:T(2,128)(2,1)}), bf16[4,2,24576]{2,1,0:T(2,128)(2,1)}, u32[]{:S(2)}, u32[]{:S(2)}) async-start(bf16[4,2,24576]{2,1,0:T(2,128)(2,1)} %reshape.977), calls=%async_computation.9 | async-start | bytes 786432 | tf_op jit(solution)/shard_map/all_to_all | solution.py:268
  643.5 410.8 %reduce-scatter.16.cloned.1.call-start = ((), (), s32[]{:S(2)}) async-start(), calls=%async_computation.27 | async-start | bytes 442368
  684.8 419.7 %all-reduce.3.cloned.1.call-start = ((), (), s32[]{:S(2)}) async-start(), calls=%async_computation.28 | async-start | bytes 3538944 | tf_op jit(solution)/shard_map/psum | solution.py:290
  991.7 69.1 %copy-start.90 = (f32[96,12]{0,1:T(8,128)S(1)}, f32[96,12]{0,1:T(8,128)}, u32[]{:S(2)}) copy-start(f32[96,12]{0,1:T(8,128)} %param.23) | copy-start | bytes 13828
  991.8 70.4 %copy-start.119 = (f32[96,12]{0,1:T(8,128)S(1)}, f32[96,12]{0,1:T(8,128)}, u32[]{:S(2)}) copy-start(f32[96,12]{0,1:T(8,128)} %param.29) | copy-start | bytes 13828
  991.8 112.7 %copy-start.29 = (f32[384,768]{1,0:T(8,128)S(1)}, f32[384,768]{1,0:T(8,128)}, u32[]{:S(2)}) copy-start(f32[384,768]{1,0:T(8,128)} %param.22) | copy-start | bytes 3538948
  991.8 112.7 %copy-start.38 = (f32[384,768]{1,0:T(8,128)S(1)}, f32[384,768]{1,0:T(8,128)}, u32[]{:S(2)}) copy-start(f32[384,768]{1,0:T(8,128)} %param.25) | copy-start | bytes 3538948
  1062.2 45.5 %copy-start.88 = (f32[96,12]{0,1:T(8,128)}, f32[96,12]{0,1:T(8,128)S(1)}, u32[]{:S(2)}) copy-start(f32[96,12]{0,1:T(8,128)S(1)} %get-tuple-element.66) | copy-start | bytes 13828
  (111 other events, 379.6 us)
Sparse Core Ops, SparseCore 0:
  10.8 140.8 all-gather.3
  154.4 78.0 all-gather.5
  376.8 68.0 reduce-scatter.9
  528.7 128.0 reduce-scatter.7
  660.6 162.4 reduce-scatter.11
  827.0 162.5 reduce-scatter.13
  993.7 60.5 reduce-scatter.15
  1058.8 45.6 all-reduce.2
where the time goes:
time: 1130 us; the launch traced here: 1120 us
  waiting for transfers between devices  485 us (43%)
  matrix products  251 us (22%)
  local copies, waits for them, and re-layouts  169 us (15%)
  other arithmetic  99.7 us (9%)
  starting transfers between devices  63.9 us (6%)
  blocking collectives  38 us (3%)
  between operations  16.5 us (1%)
    reduce_scatter x1, waiting for transfers between devices, body(): lax.psum_scatter(products[3], 'dp', scatter_dimension=0, tiled=True)  164 us
    reduce_scatter x1, waiting for transfers between devices, body(): lax.psum_scatter(products[2], 'dp', scatter_dimension=0, tiled=True)  130 us
    all_gather x1, waiting for transfers between devices, body(): lax.all_gather(wide_master.astype(jnp.bfloat16), 'dp', axis=0, tiled=True)  67.5 us
    unnamed x9, waiting for transfers between devices  58.2 us
    unnamed x321, local copies, waits for them, and re-layouts  49.1 us
    dot_general x16, matrix products, right_dot(): jnp.einsum('ra,ba->rb', left, right, preferred_element_type=jnp.float32)  44.5 us
    psum x1, waiting for transfers between devices, body(): lax.psum(sums[2].astype(jnp.bfloat16), 'seq').astype(jnp.float32)  41.7 us
    dot_general x4, matrix products, micro_step(): jnp.dot(first_low, wide_w[:, 4 * model_width:], preferred_element_type=jn...  39.7 us
  transfers between devices with their start and end apart: 24, of which 9 were waited for; matrix products, arithmetic and copies ran while one was open for 37% of the time, Pallas kernels for 0%

commit v1 on v0

v1 whole, which is shorter than its diff:
```python
import jax
import jax.numpy as jnp
from jax import lax
from jax.experimental import pallas as pl
from jax.experimental.pallas import tpu as pltpu
from jax.sharding import PartitionSpec as P

D = 768
HEAD_DIM = 64
FF = 3072
PAIR = 128
LONG_L = 512
SHORT_L = 256
VMEM_BYTES = 56 * 1024 * 1024

norm_eps = 1e-12
mask_fill = -10000.0
learning_rate = 0.0002
momentum_rate = 0.9
decay_weight = 0.0001
average_rate = 0.9
score_scale = HEAD_DIM ** (-0.5)
f32 = jnp.float32
bf16 = jnp.bfloat16


def params():
    return pltpu.CompilerParams(vmem_limit_bytes=VMEM_BYTES)


def dot_nn(a, b):
    return lax.dot_general(a, b, (((1,), (0,)), ((), ())), preferred_element_type=f32)


def dot_nt(a, b):
    return lax.dot_general(a, b, (((1,), (1,)), ((), ())), preferred_element_type=f32)


SEQS = ((0, 128, LONG_L, 0), (128, 64, SHORT_L, 1), (192, 64, SHORT_L, 2))


def attn_forward_kernel(lens_ref, q_ref, k_ref, v_ref, o_ref, long_ref, short_ref):
    for first, rows, length, index in SEQS:
        q = q_ref[:, first : first + rows, :].reshape(length, PAIR)
        k = k_ref[:, first : first + rows, :].reshape(length, PAIR)
        v = v_ref[:, first : first + rows, :].reshape(length, PAIR)
        v_t = jnp.transpose(v)
        head_lane = lax.broadcasted_iota(jnp.int32, (length, PAIR), 1) // HEAD_DIM
        live = lax.broadcasted_iota(jnp.int32, (length, length), 0) < lens_ref[index]
        parts = []
        for h in range(2):
            k_h = jnp.where(head_lane == h, k, jnp.zeros_like(k))
            scores = jnp.where(live, dot_nt(k_h, q) * score_scale, mask_fill)
            top = jnp.max(scores, axis=0, keepdims=True)
            exponent = jnp.exp(scores - top)
            total = jnp.sum(exponent, axis=0, keepdims=True)
            probs = (exponent * (1.0 / total)).astype(bf16)
            if index == 0:
                long_ref[h] = probs
            else:
                short_ref[h, index - 1] = probs
            parts.append(dot_nn(v_t[h * HEAD_DIM : (h + 1) * HEAD_DIM], probs))
        o = jnp.transpose(jnp.concatenate(parts, axis=0))
        o_ref[:, first : first + rows, :] = o.astype(bf16).reshape(4, rows, PAIR)


def attn_forward(lens, qkv):
    pairs = D // PAIR
    col = lambda base: pl.BlockSpec((4, 256, PAIR), lambda i, base=base: (0, 0, base + i))
    return pl.pallas_call(
        attn_forward_kernel,
        grid=(pairs,),
        in_specs=[
            pl.BlockSpec(memory_space=pltpu.SMEM),
            col(0),
            col(pairs),
            col(2 * pairs),
        ],
        out_specs=[
            pl.BlockSpec((4, 256, PAIR), lambda i: (0, 0, i)),
            pl.BlockSpec((2, LONG_L, LONG_L), lambda i: (i, 0, 0)),
            pl.BlockSpec((2, 2, SHORT_L, SHORT_L), lambda i: (i, 0, 0, 0)),
        ],
        out_shape=[
            jax.ShapeDtypeStruct((4, 256, D), bf16),
            jax.ShapeDtypeStruct((2 * pairs, LONG_L, LONG_L), bf16),
            jax.ShapeDtypeStruct((2 * pairs, 2, SHORT_L, SHORT_L), bf16),
        ],
        compiler_params=params(),
        name="attn_forward",
    )(lens, qkv, qkv, qkv)


def attn_backward_kernel(
    lens_ref, q_ref, k_ref, v_ref, do_ref, o_ref, long_ref, short_ref, dq_ref, dk_ref, dv_ref, sum_ref
):
    sum_q = jnp.zeros((1, PAIR), f32)
    sum_v = jnp.zeros((1, PAIR), f32)
    for first, rows, length, index in SEQS:
        q = q_ref[:, first : first + rows, :].reshape(length, PAIR)
        k = k_ref[:, first : first + rows, :].reshape(length, PAIR)
        v = v_ref[:, first : first + rows, :].reshape(length, PAIR)
        do = do_ref[:, first : first + rows, :].reshape(length, PAIR)
        o = o_ref[:, first : first + rows, :].reshape(length, PAIR)
        k_t = jnp.transpose(k)
        inner = jnp.transpose(do.astype(f32) * o.astype(f32))
        head_lane = lax.broadcasted_iota(jnp.int32, (length, PAIR), 1) // HEAD_DIM
        live = lax.broadcasted_iota(jnp.int32, (length, length), 0) < lens_ref[index]
        dq_parts = []
        dk = jnp.zeros((length, PAIR), f32)
        dv = jnp.zeros((length, PAIR), f32)
        for h in range(2):
            keep = head_lane == h
            v_h = jnp.where(keep, v, jnp.zeros_like(v))
            do_h = jnp.where(keep, do, jnp.zeros_like(do))
            q_h = jnp.where(keep, q, jnp.zeros_like(q))
            probs = long_ref[h] if index == 0 else short_ref[h, index - 1]
            delta = jnp.sum(inner[h * HEAD_DIM : (h + 1) * HEAD_DIM], axis=0, keepdims=True)
            d_probs = dot_nt(v_h, do)
            d_scores = jnp.where(live, probs.astype(f32) * (d_probs - delta), 0.0).astype(bf16)
            dv = dv + dot_nn(probs, do_h)
            dk = dk + dot_nn(d_scores, q_h)
            dq_parts.append(dot_nn(k_t[h * HEAD_DIM : (h + 1) * HEAD_DIM], d_scores))
        dq = (jnp.transpose(jnp.concatenate(dq_parts, axis=0)) * score_scale).astype(bf16)
        dk = (dk * score_scale).astype(bf16)
        dv = dv.astype(bf16)
        sum_q = sum_q + jnp.sum(dq.astype(f32), axis=0, keepdims=True)
        sum_v = sum_v + jnp.sum(dv.astype(f32), axis=0, keepdims=True)
        dq_ref[:, first : first + rows, :] = dq.reshape(4, rows, PAIR)
        dk_ref[:, first : first + rows, :] = dk.reshape(4, rows, PAIR)
        dv_ref[:, first : first + rows, :] = dv.reshape(4, rows, PAIR)
    sum_ref[0:1, :] = sum_q
    sum_ref[1:2, :] = sum_v
    sum_ref[2:8, :] = jnp.zeros((6, PAIR), f32)


def attn_backward(lens, qkv, d_attended, attended, long_probs, short_probs):
    pairs = D // PAIR
    col = lambda base: pl.BlockSpec((4, 256, PAIR), lambda i, base=base: (0, 0, base + i))
    return pl.pallas_call(
        attn_backward_kernel,
        grid=(pairs,),
        in_specs=[
            pl.BlockSpec(memory_space=pltpu.SMEM),
            col(0),
            col(pairs),
            col(2 * pairs),
            col(0),
            col(0),
            pl.BlockSpec((2, LONG_L, LONG_L), lambda i: (i, 0, 0)),
            pl.BlockSpec((2, 2, SHORT_L, SHORT_L), lambda i: (i, 0, 0, 0)),
        ],
        out_specs=[col(0), col(0), col(0), pl.BlockSpec((8, PAIR), lambda i: (0, i))],
        out_shape=[jax.ShapeDtypeStruct((4, 256, D), bf16)] * 3 + [jax.ShapeDtypeStruct((8, D), f32)],
        compiler_params=params(),
        name="attn_backward",
    )(lens, qkv, qkv, qkv, d_attended, attended, long_probs, short_probs)


def gelu_pair(u):
    a = jnp.abs(u)
    t = 1.0 / (1.0 + (0.3275911 * 0.5**0.5) * a)
    e = jnp.exp(-0.5 * u * u)
    poly = t * (0.254829592 + t * (-0.284496736 + t * (1.421413741 + t * (-1.453152027 + t * 1.061405429))))
    tail = 0.5 * poly * e
    cdf = jnp.where(u < 0.0, tail, 1.0 - tail)
    pdf = e * (0.5 / jnp.pi) ** 0.5
    return u * cdf, cdf + u * pdf


def row_mean(v):
    return jnp.mean(v, axis=-1, keepdims=True)


def middle_kernel(
    lens_ref,
    o_ref,
    x_ref,
    cot_ref,
    wo_ref,
    w1_ref,
    w2_ref,
    vec_ref,
    out_ref,
    y1b_ref,
    g_ref,
    dfb_ref,
    dub_ref,
    dab_ref,
    dob_ref,
    dh_ref,
    sum_ref,
    slope_ref,
):
    r = pl.program_id(0)
    rows = o_ref.shape[0]

    @pl.when(r == 0)
    def _():
        sum_ref[...] = jnp.zeros_like(sum_ref)

    def add(index, v):
        sum_ref[index : index + 1, :] += jnp.sum(v, axis=0, keepdims=True)

    vec = lambda i: vec_ref[i : i + 1, :]
    h = x_ref[...].astype(f32) + (dot_nn(o_ref[...], wo_ref[...]) + vec(2))
    centred = h - row_mean(h)
    inv1 = lax.rsqrt(row_mean(centred * centred) + norm_eps)
    norm1 = centred * inv1
    y1 = norm1 * vec(3) + vec(4)
    y1b = y1.astype(bf16)
    y1b_ref[...] = y1b
    z = y1 + vec(5)
    for c in range(FF // D):
        cols = slice(c * D, (c + 1) * D)
        act, slope = gelu_pair(dot_nn(y1b, w1_ref[:, cols]) + vec(8 + c))
        act = act.astype(bf16)
        g_ref[:, cols] = act
        slope_ref[:, cols] = slope
        z = z + dot_nn(act, w2_ref[cols, :])
    centred2 = z - row_mean(z)
    inv2 = lax.rsqrt(row_mean(centred2 * centred2) + norm_eps)
    norm2 = centred2 * inv2
    out_ref[...] = (norm2 * vec(6) + vec(7)).astype(bf16)

    j = lax.broadcasted_iota(jnp.int32, (rows, 1), 0)
    long_end = lens_ref[0] - r * 128
    short_end = [lens_ref[i] - r * 64 + first for i, first in ((1, 128), (2, 192))]
    live = j < jnp.where(j < 128, long_end, jnp.where(j < 192, short_end[0], short_end[1]))
    dr = jnp.where(live, cot_ref[...].astype(f32), 0.0)
    e2 = dr * vec(6)
    dz = inv2 * (e2 - row_mean(e2) - norm2 * row_mean(e2 * norm2))
    dfb = dz.astype(bf16)
    dfb_ref[...] = dfb
    add(6, dr * norm2)
    add(7, dr)
    add(5, dfb.astype(f32))
    dy1 = dz
    for c in range(FF // D):
        cols = slice(c * D, (c + 1) * D)
        dub = (dot_nt(dfb, w2_ref[cols, :]) * slope_ref[:, cols]).astype(bf16)
        dub_ref[:, cols] = dub
        add(8 + c, dub.astype(f32))
        dy1 = dy1 + dot_nt(dub, w1_ref[:, cols])
    add(3, dy1 * norm1)
    add(4, dy1)
    e1 = dy1 * vec(3)
    dh = inv1 * (e1 - row_mean(e1) - norm1 * row_mean(e1 * norm1))
    dab = dh.astype(bf16)
    dh_ref[...] = dh
    dab_ref[...] = dab
    add(2, dab.astype(f32))
    dob_ref[...] = dot_nt(dab, wo_ref[...]).astype(bf16)


def middle(lens, attended, tokens, cotangent, w_o, w_1, w_2, vec):
    n = tokens.shape[0]
    rows = 256
    row = lambda width: pl.BlockSpec((rows, width), lambda i: (i, 0))
    whole = lambda a: pl.BlockSpec(a.shape, lambda i: (0, 0), pipeline_mode=pl.Buffered(1))
    shape = jax.ShapeDtypeStruct
    return pl.pallas_call(
        middle_kernel,
        grid=(n // rows,),
        in_specs=[
            pl.BlockSpec(memory_space=pltpu.SMEM),
            row(D),
            row(D),
            row(D),
            whole(w_o),
            whole(w_1),
            whole(w_2),
            whole(vec),
        ],
        out_specs=[
            row(D),
            row(D),
            row(FF),
            row(D),
            row(FF),
            row(D),
            row(D),
            row(D),
            pl.BlockSpec((16, D), lambda i: (0, 0)),
        ],
        out_shape=[
            shape((n, D), bf16),
            shape((n, D), bf16),
            shape((n, FF), bf16),
            shape((n, D), bf16),
            shape((n, FF), bf16),
            shape((n, D), bf16),
            shape((n, D), bf16),
            shape((n, D), f32),
            shape((16, D), f32),
        ],
        scratch_shapes=[pltpu.VMEM((rows, FF), f32)],
        compiler_params=params(),
        name="middle",
    )(lens, attended, tokens, cotangent, w_o, w_1, w_2, vec)


def transpose_dot(left, right):
    return jnp.einsum("ra,rb->ab", left, right, preferred_element_type=f32)


def right_dot(left, right):
    return jnp.einsum("ra,ba->rb", left, right, preferred_element_type=f32)


def flip(v, axis, bit):
    n = lax.axis_size(axis)
    return lax.ppermute(v, axis, [(i, i ^ bit) for i in range(n)])


def half_of(v, dim, which):
    size = v.shape[dim] // 2
    return lax.dynamic_slice_in_dim(v, which * size, size, dim)


def halve(v, axis, bit, dim):
    mine = (lax.axis_index(axis) // bit) % 2
    other = flip(half_of(v, dim, 1 - mine), axis, bit)
    return (half_of(v, dim, mine).astype(f32) + other.astype(f32)).astype(bf16)


def double(v, axis, bit, dim):
    mine = (lax.axis_index(axis) // bit) % 2
    other = flip(v, axis, bit)
    return jnp.where(
        mine == 0, jnp.concatenate([v, other], axis=dim), jnp.concatenate([other, v], axis=dim)
    )


def reduce_rows(grad):
    rows, cols = grad.shape
    dp = lax.axis_size("dp")
    v = grad.reshape(dp, rows // dp, cols)
    v = halve(v, "seq", 1, 2)
    v = halve(v, "seq", 2, 2)
    bit = 1
    while bit < dp:
        blocks = v.shape[0]
        v = v.reshape(blocks // 2, 2, v.shape[1], v.shape[2]) if v.ndim == 3 else v
        v = halve(v, "dp", bit, 1)[:, 0]
        bit *= 2
    v = v[0]
    v = double(v, "seq", 2, 1)
    v = double(v, "seq", 1, 1)
    return v.astype(f32)


def update(master, reduced_grad, moment, average):
    step_grad = reduced_grad + decay_weight * master
    velocity = momentum_rate * moment + step_grad
    updated = master - learning_rate * (step_grad + momentum_rate * velocity)
    averaged = average_rate * average + (1.0 - average_rate) * updated
    return (velocity, averaged, updated, updated.astype(jnp.bfloat16))


def spread_rows(long_part, short_part):
    long_blocks = long_part.reshape(4, 128, D)
    short_blocks = jnp.transpose(short_part, (1, 0, 2, 3)).reshape(4, 128, D)
    return jnp.concatenate([long_blocks, short_blocks], axis=1)


def exchange(v):
    return lax.all_to_all(v, "seq", split_axis=0, concat_axis=0, tiled=True)


def collect_rows(v):
    long_part = v[:, :128].reshape(2, 2, 128, D)
    short_part = jnp.transpose(v[:, 128:].reshape(4, 2, 64, D), (1, 0, 2, 3))
    return short_part, long_part


def body(
    short_in,
    long_in,
    short_cot,
    long_cot,
    short_len,
    long_len,
    wide_master,
    down_master,
    vector_master,
    wide_moment,
    down_moment,
    vector_moment,
    wide_average,
    down_average,
    vector_average,
):
    s = lax.axis_index("seq")
    lens = jnp.stack([long_len[s // 2, 0, s % 2], short_len[0, 0, s], short_len[1, 0, s]])
    tokens = exchange(spread_rows(long_in, short_in))
    cotangent = exchange(spread_rows(long_cot, short_cot))
    wide_w = lax.all_gather(wide_master.astype(bf16), "dp", axis=0, tiled=True)
    down_w = lax.all_gather(down_master.astype(bf16), "dp", axis=0, tiled=True)
    vector_w = lax.all_gather(vector_master.astype(bf16), "dp", axis=0, tiled=True)
    vec = jnp.transpose(vector_w.astype(f32))
    w_qkv = wide_w[:, : 3 * D]
    w_o = wide_w[:, 3 * D : 4 * D]
    w_1 = wide_w[:, 4 * D :]

    rows = tokens.reshape(1024, D)
    proj_bias = jnp.concatenate([vec[0], jnp.zeros((D,), f32), vec[1]])
    qkv = (jnp.dot(rows, w_qkv, preferred_element_type=f32) + proj_bias).astype(bf16)
    qkv = qkv.reshape(4, 256, 3 * D)
    attended, long_probs, short_probs = attn_forward(lens, qkv)
    flat_attended = attended.reshape(1024, D)
    out, y1b, act, dfb, dub, dab, dob, dh, sums = middle(
        lens, flat_attended, rows, cotangent.reshape(1024, D), w_o, w_1, down_w, vec
    )
    d_down = transpose_dot(act, dfb).astype(bf16)
    d_one = transpose_dot(y1b, dub).astype(bf16)
    d_o = transpose_dot(flat_attended, dab).astype(bf16)
    dq, dk, dv, qv_sums = attn_backward(
        lens, qkv, dob.reshape(4, 256, D), attended, long_probs, short_probs
    )
    d_qkv = jnp.concatenate([dq, dk, dv], axis=2).reshape(1024, 3 * D)
    d_wqkv = transpose_dot(rows, d_qkv).astype(bf16)
    back = (dh + right_dot(d_qkv, w_qkv)).astype(bf16).reshape(4, 256, D)

    vector_total = jnp.concatenate([qv_sums[:2], sums[2:12]], axis=0)
    vector_sum = jnp.transpose(lax.psum(vector_total, ("dp", "seq")))
    own_rows = vector_master.shape[0]
    vector_reduced = lax.dynamic_slice_in_dim(vector_sum, lax.axis_index("dp") * own_rows, own_rows, 0)
    wide_reduced = jnp.concatenate([reduce_rows(d_wqkv), reduce_rows(d_o), reduce_rows(d_one)], axis=1)
    down_reduced = reduce_rows(d_down)

    short_out, long_out = collect_rows(exchange(out.reshape(4, 256, D)))
    short_back, long_back = collect_rows(exchange(back))
    wide_new = update(wide_master, wide_reduced, wide_moment, wide_average)
    down_new = update(down_master, down_reduced, down_moment, down_average)
    vector_new = update(vector_master, vector_reduced, vector_moment, vector_average)
    return (
        short_out,
        long_out,
        short_back,
        long_back,
        wide_reduced,
        down_reduced,
        vector_reduced,
        wide_new[0],
        down_new[0],
        vector_new[0],
        wide_new[1],
        down_new[1],
        vector_new[1],
        wide_new[2],
        down_new[2],
        vector_new[2],
        wide_new[3],
        down_new[3],
        vector_new[3],
    )


def solution(mesh):
    tok = P(None, "dp", "seq", None)
    lengths = P(None, "dp", None)
    state = P("dp", None)
    return jax.shard_map(
        body,
        mesh=mesh,
        in_specs=(tok,) * 4 + (lengths,) * 2 + (state,) * 9,
        out_specs=(tok,) * 4 + (state,) * 15,
        check_vma=False,
    )
```

time: 1130 us -> 576 us (0.51)
  waiting for transfers between devices: 485 us -> 230 us
  matrix products: 251 us -> 34.5 us
  local copies, waits for them, and re-layouts: 169 us -> 45.3 us
  Pallas kernels: 0 us -> 78.9 us
  other arithmetic: 99.7 us -> 39 us
  blocking collectives: 38 us -> 84.8 us
  starting transfers between devices: 63.9 us -> 41.9 us
    reduce_scatter x4 -> x0, waiting for transfers between devices: 294 us -> none  [the longest x1 164 us: body(): lax.psum_scatter(products[3], 'dp', scatter_dimension=0, tiled=True)]
    dot_general x60 -> x6, matrix products: 251 us -> 34.5 us  [the longest x4 19.1 us: transpose_dot(): return jnp.einsum('ra,rb->ab', left, right, preferred_element_type=f32)]
    ppermute x0 -> x28, waiting for transfers between devices: none -> 90.1 us  [flip(): return lax.ppermute(v, axis, [(i, i ^ bit) for i in range(n)])]
    pallas_call x0 -> x3, Pallas kernels: none -> 78.9 us  [the longest x1 43.2 us: middle(): pl.pallas_call(middle_kernel, grid=(n // rows,), in_specs=[pl.BlockSpec(m...]
    all_gather x2, waiting for transfers between devices: 67.5 us -> 136 us  [the longest x1 89.5 us: body(): wide_w = lax.all_gather(wide_master.astype(bf16), 'dp', axis=0, tiled=True)]
    unnamed x9 -> x2, waiting for transfers between devices: 58.2 us -> 0.03 us
    psum x1, blocking collectives: 5.67 us -> 52.6 us  [body(): vector_sum = jnp.transpose(lax.psum(vector_total, ('dp', 'seq')))]
    all_to_all x16 -> x4, starting transfers between devices: 63.4 us -> 16.7 us  [exchange(): return lax.all_to_all(v, 'seq', split_axis=0, concat_axis=0, tiled=True)]
  transfers between devices with their start and end apart: 24 -> 34, of which waited for: 9 -> 18; matrix products, arithmetic and copies ran while one was open for 37% -> 15% of each run, Pallas kernels for 0% -> 6%
where the time goes in v1:
time: 576 us; the launch traced here: 569 us
  waiting for transfers between devices  230 us (40%)
  blocking collectives  84.8 us (15%)
  Pallas kernels  78.9 us (14%)
  local copies, waits for them, and re-layouts  45.3 us (8%)
  starting transfers between devices  41.9 us (7%)
  other arithmetic  39 us (7%)
  matrix products  34.5 us (6%)
  between operations  15.3 us (3%)
    ppermute x28, waiting for transfers between devices, flip(): return lax.ppermute(v, axis, [(i, i ^ bit) for i in range(n)])  90.1 us
    all_gather x1, waiting for transfers between devices, body(): wide_w = lax.all_gather(wide_master.astype(bf16), 'dp', axis=0, tiled=True)  89.5 us
    psum x1, blocking collectives, body(): vector_sum = jnp.transpose(lax.psum(vector_total, ('dp', 'seq')))  52.6 us
    all_gather x1, waiting for transfers between devices, body(): down_w = lax.all_gather(down_master.astype(bf16), 'dp', axis=0, tiled=True)  46.5 us
    pallas_call x1, Pallas kernels, middle(): pl.pallas_call(middle_kernel, grid=(n // rows,), in_specs=[pl.BlockSpec(m...  43.2 us
    all_gather x1, blocking collectives, body(): lax.all_gather(vector_master.astype(bf16), 'dp', axis=0, tiled=True)  32.3 us
    ppermute x28, starting transfers between devices, flip(): return lax.ppermute(v, axis, [(i, i ^ bit) for i in range(n)])  25.2 us
    unnamed x96, local copies, waits for them, and re-layouts  20 us
  transfers between devices with their start and end apart: 34, of which 18 were waited for; matrix products, arithmetic and copies ran while one was open for 15% of the time, Pallas kernels for 6%

profile of v1, /device:TPU:0, one launch (start us, length us, event | category | flops | bytes accessed | tf_op | source)
XLA Modules:
  0.0 569.4 jit_solution(3266363668972784422)
XLA Ops:
  7.3 2.9 convert_element_type.231
  14.0 4.4 all-to-all-start
  19.7 32.3 %all-gather = bf16[8,96,12]{1,2,0:T(8,128)(2,1)S(1)} all-gather(bf16[1,96,12]{1,2,0:T(8,128)(2,1)S(1)} %convert_bitcast_fusion), channel_id=1, replica_groups=mesh['dp'=8,'seq'=4] {'dp'}, dimensions={0}, use_global_device_ids=true | all-gather | bytes 20736 | tf_op jit(solution)/shard_map/all_gather | solution.py:400
  51.9 2.4 pad_maximum_fusion.1
  54.3 3.6 all-to-all-start.1
  57.9 2.5 pad_add_fusion.lens_ref
  60.7 1.6 copy.83
  62.2 89.5 %all-gather.4.cloned.1.call-done = bf16[768,6144]{1,0:T(8,128)(2,1)} async-done(((bf16[96,6144]{1,0:T(8,128)(2,1)}), bf16[768,6144]{1,0:T(8,128)(2,1)}) %all-gather.4.cloned.1.call-update) | async-done | bytes 9437200 | tf_op jit(solution)/shard_map/all_gather | solution.py:398
  151.8 8.4 %add_convert_fusion = bf16[1024,2304]{1,0:T(8,128)(2,1)} fusion(bf16[1024,768]{1,0:T(8,128)(2,1)} %bitcast.88, f32[2304]{0:T(1024)S(1)} %pad_maximum_fusion.3, bf16[768,6144]{1,0:T(8,128)(2,1)} %all-gather.4.cloned.1.call-done), kind=kOutput, calls=%fused_computation | convolution fusion | flops 3628597248 | bytes 9839616 | tf_op jit(solution)/shard_map/dot_general | solution.py:408
  160.2 18.7 %attn_forward.1 = (bf16[4,256,768]{2,1,0:T(8,128)(2,1)}, bf16[12,512,512]{2,1,0:T(8,128)(2,1)}, bf16[12,2,256,256]{3,2,1,0:T(8,128)(2,1)}) custom-call(s32[3]{0:T(128)} %pad_add_fusion.lens_ref, bf16[4,256,2304]{2,1,0:T(8,128)(2,1)} %bitcast.79, bf16[4,256,2304]{2,1,0:T(8,128)(2,1)} %bitcast.80, bf16[4,256,2304]{2,1,0:T(8,128)(2,1)} %bitcast.81), custom_call_target="tpu_custom_call" | custom-call | tf_op jit(solution)/shard_map/attn_forward/pallas_call | solution.py:70
  178.9 4.9 slice.48.w1_ref
  183.8 2.4 slice.47.wo_ref
  186.1 46.5 %all-gather.6.cloned.1.call-done.w2_ref = bf16[3072,768]{1,0:T(8,128)(2,1)} async-done(((bf16[384,768]{1,0:T(8,128)(2,1)}), bf16[3072,768]{1,0:T(8,128)(2,1)}) %all-gather.6.cloned.1.call-update) | async-done | bytes 4718608 | tf_op jit(solution)/shard_map/all_gather | solution.py:399
  232.6 43.2 %middle.1 = (bf16[1024,768]{1,0:T(8,128)(2,1)}, bf16[1024,768]{1,0:T(8,128)(2,1)}, bf16[1024,3072]{1,0:T(8,128)(2,1)}, bf16[1024,768]{1,0:T(8,128)(2,1)}, bf16[1...) custom-call(s32[3]{0:T(128)} %pad_add_fusion.lens_ref, ...), custom_call_target="tpu_custom_call" | custom-call | tf_op jit(solution)/shard_map/middle/pallas_call | solution.py:262
  275.8 7.7 %convolution_convert_fusion = bf16[3072,768]{1,0:T(8,128)(2,1)S(1)} fusion(bf16[1024,3072]{1,0:T(8,128)(2,1)} %get-tuple-element.47, bf16[1024,768]{1,0:T(8,128)(2,1)} %get-tuple-element.48), kind=kOutput, calls=%fused_computation.2 | convolution fusion | flops 4834197504 | bytes 12582912 | tf_op jit(solution)/shard_map/ra,rb->ab/dot_general | solution.py:304
  283.6 2.0 constant_dynamic-slice_fusion.7
  285.5 4.3 copy.105
  289.8 16.9 %attn_backward.1 = (bf16[4,256,768]{2,1,0:T(8,128)(2,1)}, bf16[4,256,768]{2,1,0:T(8,128)(2,1)}, bf16[4,256,768]{2,1,0:T(8,128)(2,1)}, f32[8,768]{1,0:T(8,128)}) custom-call(s32[3]{0:T(128)} %pad_add_fusion.lens_ref, bf16[4,256,2304]{2,1,0:T(8,128)(2,1)} %bitcast.82, bf16[4,256,2304]{2,1,0:T(8,128)(2,1)} %bitcast.83, bf16[4,256,2304]{2,1,0:T(8,128)(2,1)} %bitcast.84, ...), custom_call_target="tpu_custom_call" | custom-call | tf_op jit(solution)/shard_map/attn_backward/pallas_call | solution.py:140
  306.8 1.6 constant_dynamic-update-slice_fusion.2
  310.3 4.4 bitcast_convert_fusion
  318.6 1.4 convolution_convert_fusion.2
  320.7 5.4 convolution_convert_fusion.1
  326.5 1.6 collective-permute-start.8
  328.1 1.6 constant_dynamic-slice_fusion.11
  329.7 8.0 %collective-permute-done.8 = bf16[8,96,192]{2,1,0:T(8,128)(2,1)S(1)} collective-permute-done((bf16[8,96,192]{2,1,0:T(8,128)(2,1)S(1)}, bf16[8,96,192]{2,1,0:T(8,128)(2,1)S(1)}, u32[]{:S(2)}, u32[]{:S(2)}) %collective-permute-start.8) | collective-permute-done | bytes 294944 | tf_op jit(solution)/shard_map/ppermute | solution.py:313
  338.5 7.0 %add_convert_fusion.4 = bf16[1024,768]{1,0:T(8,128)(2,1)} fusion(f32[1024,768]{1,0:T(8,128)S(1)} %copy-done.36, bf16[1024,2304]{1,0:T(8,128)(2,1)S(1)} %bitcast.122, bf16[768,6144]{1,0:T(8,128)(2,1)} %all-gather.4.cloned.1.call-done), kind=kOutput, calls=%fused_computation.7 | convolution fusion | flops 3625451520 | bytes 12976128 | tf_op jit(solution)/shard_map/ra,ba->rb/dot_general | solution.py:308
  346.3 4.4 all-to-all-start.3
  350.7 52.6 %psum.7 = f32[12,768]{1,0:T(8,128)S(1)} all-reduce(f32[12,768]{1,0:T(8,128)S(1)} %pad_maximum_fusion.2), channel_id=1, replica_groups=mesh['dp'=8,'seq'=4] {'dp','seq'}, use_global_device_ids=true, to_apply=%region_0.1 | all-reduce | flops 9216 | bytes 73728 | tf_op jit(solution)/shard_map/psum | solution.py:426
  403.4 1.5 collective-permute-start.10
  405.5 2.5 collective-permute-done.10
  408.1 1.5 collective-permute-start.11
  410.3 2.6 copy.104
  413.2 2.3 collective-permute-start.12
  415.6 2.4 add_convert_fusion.3
  419.2 1.4 constant_dynamic-slice_fusion.18
  420.8 4.4 all-to-all-start.2
  425.2 2.5 fusion.16
  427.7 2.5 add_convert_fusion.1
  431.4 2.0 collective-permute-start.22
  433.3 12.3 %collective-permute-done.1 = bf16[8,96,576]{2,1,0:T(8,128)(2,1)} collective-permute-done((bf16[8,96,576]{2,1,0:T(8,128)(2,1)}, bf16[8,96,576]{2,1,0:T(8,128)(2,1)}, u32[]{:S(2)}, u32[]{:S(2)}) %collective-permute-start.1) | collective-permute-done | bytes 884768 | tf_op jit(solution)/shard_map/ppermute | solution.py:313
  445.6 1.8 add_convert_fusion.7
  448.1 3.0 add_convert_fusion.2
  453.8 2.6 collective-permute-done.2
  457.3 1.7 collective-permute-start.3
  459.0 3.5 all-to-all-done.2
  462.4 2.4 fusion.17
  467.7 1.6 collective-permute-start.4
  469.4 5.5 collective-permute-done.4
  475.0 12.7 %collective-permute-done.22 = bf16[8,384,192]{1,2,0:T(8,128)(2,1)} collective-permute-done((bf16[8,384,192]{1,2,0:T(8,128)(2,1)}, bf16[8,384,192]{1,2,0:T(8,128)(2,1)}, u32[]{:S(2)}, u32[]{:S(2)}) %collective-permute-start.22) | collective-permute-done | bytes 1179680 | tf_op jit(solution)/shard_map/ppermute | solution.py:313
  487.7 1.7 add_convert_fusion.5
  490.2 19.2 %collective-permute-done.15 = bf16[8,96,768]{2,1,0:T(8,128)(2,1)} collective-permute-done((bf16[8,96,768]{2,1,0:T(8,128)(2,1)}, bf16[8,96,768]{2,1,0:T(8,128)(2,1)}, u32[]{:S(2)}, u32[]{:S(2)}) %collective-permute-start.15) | collective-permute-done | bytes 1179680 | tf_op jit(solution)/shard_map/ppermute | solution.py:313
  509.4 1.6 add_convert_fusion.6
  511.0 1.5 collective-permute-start.16
  513.2 1.4 collective-permute-start.24
  514.8 6.2 %collective-permute-done.16 = bf16[4,1,96,768]{3,2,0,1:T(8,128)(2,1)} collective-permute-done((bf16[4,1,96,768]{3,2,0,1:T(8,128)(2,1)S(1)}, bf16[4,1,96,768]{3,2,0,1:T(8,128)(2,1)}, u32[]{:S(2)}, u32[]{:S(2)}) %collective-permute-start.16) | collective-permute-done | bytes 589856 | tf_op jit(solution)/shard_map/ppermute | solution.py:313
  522.3 1.5 collective-permute-start.17
  523.9 1.4 collective-permute-done.24
  526.4 1.5 collective-permute-start.25
  527.9 5.9 %collective-permute-done.17 = bf16[2,1,96,768]{3,2,1,0:T(8,128)(2,1)S(1)} collective-permute-done((bf16[2,1,96,768]{3,2,1,0:T(8,128)(2,1)S(1)}, bf16[2,1,96,768]{3,2,1,0:T(8,128)(2,1)S(1)}, u32[]{:S(2)}, u32[]{:S(2)}) %collective-permute-start.17) | collective-permute-done | bytes 294944 | tf_op jit(solution)/shard_map/ppermute | solution.py:313
  534.5 7.8 %collective-permute-done.25 = bf16[1,1,384,192]{3,2,1,0:T(8,128)(2,1)S(1)} collective-permute-done((bf16[1,1,384,192]{3,2,1,0:T(8,128)(2,1)S(1)}, bf16[1,1,384,192]{3,2,1,0:T(8,128)(2,1)S(1)}, u32[]{:S(2)}, u32[]{:S(2)}) %collective-permute-start.25) | collective-permute-done | bytes 147488 | tf_op jit(solution)/shard_map/ppermute | solution.py:313
  544.8 4.4 collective-permute-done.26
  551.4 1.9 fusion.13
  556.5 3.4 fusion.15
  559.9 2.0 multiply_add_fusion
  (187 shorter events, 37.8 us)
Async XLA Ops:
  7.2 11.3 %copy-start = (s32[2,1,2]{2,1,0:T(1,128)S(1)}, s32[2,1,2]{2,1,0:T(1,128)}, u32[]{:S(2)}) copy-start(s32[2,1,2]{2,1,0:T(1,128)} %param.20) | copy-start | bytes 52
  7.2 3.0 copy-start.15
  7.2 144.5 %all-gather.4.cloned.1.call-start = ((), (), s32[]{:S(2)}) async-start(), calls=%async_computation.4 | async-start | bytes 10616832 | tf_op jit(solution)/shard_map/all_gather | solution.py:398
  10.2 222.4 %all-gather.6.cloned.1.call-start = ((), (), s32[]{:S(2)}) async-start(), calls=%async_computation.5 | async-start | bytes 5308416 | tf_op jit(solution)/shard_map/all_gather | solution.py:399
  14.0 4.4 copy-start.28
  14.0 5.0 copy-start.35
  14.0 5.6 copy-start.32
  14.0 40.3 %all-to-all-start = ((bf16[4,256,768]{1,2,0:T(8,128)(2,1)}), bf16[4,256,768]{1,2,0:T(8,128)(2,1)S(1)}, u32[]{:S(2)}, u32[]{:S(2)}) async-start(bf16[4,256,768]{1,2,0:T(8,128)(2,1)} %pad_maximum_fusion), calls=%async_computation | async-start | bytes 3145728 | tf_op jit(solution)/shard_map/all_to_all | solution.py:368
  54.3 7.9 %copy-start.10 = (bf16[4,256,768]{1,2,0:T(8,128)(2,1)}, bf16[4,256,768]{1,2,0:T(8,128)(2,1)S(1)}, u32[]{:S(2)}) copy-start(bf16[4,256,768]{1,2,0:T(8,128)(2,1)S(1)} %all-to-all-done) | copy-start | bytes 4718596
  54.3 131.8 %all-to-all-start.1 = ((bf16[4,256,768]{2,1,0:T(8,128)(2,1)}), bf16[4,256,768]{2,1,0:T(8,128)(2,1)S(1)}, u32[]{:S(2)}, u32[]{:S(2)}) async-start(bf16[4,256,768]{2,1,0:T(8,128)(2,1)} %pad_maximum_fusion.1), calls=%async_computation.1 | async-start | bytes 3145728 | tf_op jit(solution)/shard_map/all_to_all | solution.py:368
  60.5 99.7 %copy-start.29 = (f32[768,12]{0,1:T(8,128)}, f32[768,12]{0,1:T(8,128)S(1)}, u32[]{:S(2)}) copy-start(f32[768,12]{0,1:T(8,128)S(1)} %reshape.153) | copy-start | bytes 110596
  186.1 46.5 %copy-start.12 = (bf16[4,256,768]{2,1,0:T(8,128)(2,1)}, bf16[4,256,768]{2,1,0:T(8,128)(2,1)S(1)}, u32[]{:S(2)}) copy-start(bf16[4,256,768]{2,1,0:T(8,128)(2,1)S(1)} %all-to-all-done.1) | copy-start | bytes 4718596
  289.8 137.9 %collective-permute-start.21 = (bf16[8,384,384]{1,2,0:T(8,128)(2,1)}, bf16[8,384,384]{1,2,0:T(8,128)(2,1)}, u32[]{:S(2)}, u32[]{:S(2)}) collective-permute-start(bf16[8,384,384]{1,2,0:T(8,128)(2,1)} %copy.105), channel_id=1, source_target_pairs={{0,1},{1,0},{2,3},{3,2},{4,5},{5,4},{6,7},{7,6},{8,9},{9,8},{10,11... | collective-permute-start | bytes 7077896 | tf_op jit(solution)/shard_map/ppermute | solution.py:313
  309.9 10.8 %slice-start = ((s8[6291456]{0:T(1024)(128)(4,1)}), s8[4194304]{0:T(1024)(128)(4,1)S(1)}, s32[]{:S(2)}) async-start(s8[6291456]{0:T(1024)(128)(4,1)} %bitcast.125), calls=%async_computation.6 | async-start | bytes 8388608
  310.3 10.3 %slice-start.1 = ((s8[6291456]{0:T(1024)(128)(4,1)}), s8[2097152]{0:T(1024)(128)(4,1)S(1)}, s32[]{:S(2)}) async-start(s8[6291456]{0:T(1024)(128)(4,1)} %bitcast.125), calls=%async_computation.7 | async-start | bytes 4194304
  314.8 5.3 copy-start.17
  314.8 2.6 copy-start.9
  314.8 3.8 copy-start.38
  316.2 99.4 %collective-permute-start = (bf16[8,96,1152]{2,1,0:T(8,128)(2,1)}, bf16[8,96,1152]{2,1,0:T(8,128)(2,1)}, u32[]{:S(2)}, u32[]{:S(2)}) collective-permute-start(bf16[8,96,1152]{2,1,0:T(8,128)(2,1)} %constant_dynamic-slice_fusion.19), channel_id=1, source_target_pairs={{0,1},{1,0},{2,3},{3,2},{4,5},{5,4},{6,7},{7,6},{8,9},{9,8},{10,11... | collective-permute-start | bytes 5308424 | tf_op jit(solution)/shard_map/ppermute | solution.py:313
  320.1 6.0 %collective-permute-start.7 = (bf16[8,96,384]{2,1,0:T(8,128)(2,1)S(1)}, bf16[8,96,384]{2,1,0:T(8,128)(2,1)S(1)}, u32[]{:S(2)}, u32[]{:S(2)}) collective-permute-start(bf16[8,96,384]{2,1,0:T(8,128)(2,1)S(1)} %constant_dynamic-slice_fusion.15), channel_id=1, source_target_pairs={{0,1},{1,0},{2,3},{3,2},{4,5},{5,4},{6,7},{7,6},{8,9},{9,8},{10,11... | collective-permute-start | bytes 1769480 | tf_op jit(solution)/shard_map/ppermute | solution.py:313
  326.1 3.5 copy-start.14
  326.5 11.1 %collective-permute-start.8 = (bf16[8,96,192]{2,1,0:T(8,128)(2,1)S(1)}, bf16[8,96,192]{2,1,0:T(8,128)(2,1)S(1)}, u32[]{:S(2)}, u32[]{:S(2)}) collective-permute-start(bf16[8,96,192]{2,1,0:T(8,128)(2,1)S(1)} %constant_dynamic-slice_fusion.14), channel_id=1, source_target_pairs={{0,2},{1,3},{2,0},{3,1},{4,6},{5,7},{6,4},{7,5},{8,10},{9,11},{10,... | collective-permute-start | bytes 884744 | tf_op jit(solution)/shard_map/ppermute | solution.py:313
  328.1 10.4 %copy-start.36 = (f32[1024,768]{1,0:T(8,128)S(1)}, f32[1024,768]{1,0:T(8,128)}, u32[]{:S(2)}) copy-start(f32[1024,768]{1,0:T(8,128)} %get-tuple-element.37) | copy-start | bytes 9437188
  329.7 118.5 %collective-permute-start.14 = (bf16[8,96,1536]{2,1,0:T(8,128)(2,1)}, bf16[8,96,1536]{2,1,0:T(8,128)(2,1)}, u32[]{:S(2)}, u32[]{:S(2)}) collective-permute-start(bf16[8,96,1536]{2,1,0:T(8,128)(2,1)} %constant_dynamic-slice_fusion.11), channel_id=1, source_target_pairs={{0,1},{1,0},{2,3},{3,2},{4,5},{5,4},{6,7},{7,6},{8,9},{9,8},{10,11... | collective-permute-start | bytes 7077896 | tf_op jit(solution)/shard_map/ppermute | solution.py:313
  337.9 65.4 %collective-permute-start.9 = (bf16[4,1,96,192]{3,2,0,1:T(8,128)(2,1)S(1)}, bf16[4,1,96,192]{3,2,0,1:T(8,128)(2,1)S(1)}, u32[]{:S(2)}, u32[]{:S(2)}) collective-permute-start(bf16[4,1,96,192]{3,2,0,1:T(8,128)(2,1)S(1)} %dynamic-slice_bitcast_fusion.2), channel_id=1, source_target_pairs={{0,4},{4,0},{8,12},{12,8},{16,20},{20,16},{24,28},{28,24},{1,5},{5... | collective-permute-start | bytes 442376 | tf_op jit(solution)/shard_map/ppermute | solution.py:313
  338.5 7.7 %copy-start.30 = (f32[16,768]{1,0:T(8,128)S(1)}, f32[16,768]{1,0:T(8,128)}, u32[]{:S(2)}) copy-start(f32[16,768]{1,0:T(8,128)} %get-tuple-element.50) | copy-start | bytes 147460
  346.3 58.6 %copy-start.34 = (f32[96,12]{0,1:T(8,128)S(1)}, f32[96,12]{0,1:T(8,128)}, u32[]{:S(2)}) copy-start(f32[96,12]{0,1:T(8,128)} %param.26) | copy-start | bytes 13828
  346.3 63.4 %copy-start.33 = (f32[96,12]{0,1:T(8,128)S(1)}, f32[96,12]{0,1:T(8,128)}, u32[]{:S(2)}) copy-start(f32[96,12]{0,1:T(8,128)} %param.29) | copy-start | bytes 13828
  346.3 74.5 %all-to-all-start.3 = ((bf16[4,256,768]{2,1,0:T(8,128)(2,1)}), bf16[4,256,768]{2,1,0:T(8,128)(2,1)}, u32[]{:S(2)}, u32[]{:S(2)}) async-start(bf16[4,256,768]{2,1,0:T(8,128)(2,1)} %bitcast.112), calls=%async_computation.3 | async-start | bytes 3145728 | tf_op jit(solution)/shard_map/all_to_all | solution.py:368
  403.4 4.7 collective-permute-start.10
  405.5 7.3 %copy-start.31 = (f32[96,12]{0,1:T(8,128)}, f32[96,12]{0,1:T(8,128)S(1)}, u32[]{:S(2)}) copy-start(f32[96,12]{0,1:T(8,128)S(1)} %get-tuple-element.111) | copy-start | bytes 13828
  408.1 5.1 collective-permute-start.11
  413.2 7.4 %collective-permute-start.12 = (bf16[96,192]{1,0:T(8,128)(2,1)S(1)}, bf16[96,192]{1,0:T(8,128)(2,1)S(1)}, u32[]{:S(2)}, u32[]{:S(2)}) collective-permute-start(bf16[96,192]{1,0:T(8,128)(2,1)S(1)} %fusion.9), channel_id=1, source_target_pairs={{0,2},{1,3},{2,0},{3,1},{4,6},{5,7},{6,4},{7,5},{8,10},{9,11},{10,... | collective-permute-start | bytes 110600 | tf_op jit(solution)/shard_map/ppermute | solution.py:313
  420.6 25.0 %collective-permute-start.1 = (bf16[8,96,576]{2,1,0:T(8,128)(2,1)}, bf16[8,96,576]{2,1,0:T(8,128)(2,1)}, u32[]{:S(2)}, u32[]{:S(2)}) collective-permute-start(bf16[8,96,576]{2,1,0:T(8,128)(2,1)} %constant_dynamic-slice_fusion.18), channel_id=1, source_target_pairs={{0,2},{1,3},{2,0},{3,1},{4,6},{5,7},{6,4},{7,5},{8,10},{9,11},{10,... | collective-permute-start | bytes 2654216 | tf_op jit(solution)/shard_map/ppermute | solution.py:313
  420.7 48.7 %collective-permute-start.13 = (bf16[96,384]{1,0:T(8,128)(2,1)S(1)}, bf16[96,384]{1,0:T(8,128)(2,1)S(1)}, u32[]{:S(2)}, u32[]{:S(2)}) collective-permute-start(bf16[96,384]{1,0:T(8,128)(2,1)S(1)} %maximum_select_fusion.7), channel_id=1, source_target_pairs={{0,1},{1,0},{2,3},{3,2},{4,5},{5,4},{6,7},{7,6},{8,9},{9,8},{10,11... | collective-permute-start | bytes 221192 | tf_op jit(solution)/shard_map/ppermute | solution.py:313
  420.8 41.6 %all-to-all-start.2 = ((bf16[4,256,768]{2,1,0:T(8,128)(2,1)}), bf16[4,256,768]{2,1,0:T(8,128)(2,1)}, u32[]{:S(2)}, u32[]{:S(2)}) async-start(bf16[4,256,768]{2,1,0:T(8,128)(2,1)} %bitcast.15), calls=%async_computation.2 | async-start | bytes 3145728 | tf_op jit(solution)/shard_map/all_to_all | solution.py:368
  425.2 2.5 copy-start.6
  430.2 15.4 %copy-start.8 = (bf16[8,96,1152]{2,1,0:T(8,128)(2,1)S(1)}, bf16[8,96,1152]{2,1,0:T(8,128)(2,1)}, u32[]{:S(2)}) copy-start(bf16[8,96,1152]{2,1,0:T(8,128)(2,1)} %copy-done.7) | copy-start | bytes 5308420
  431.4 56.4 %collective-permute-start.22 = (bf16[8,384,192]{1,2,0:T(8,128)(2,1)}, bf16[8,384,192]{1,2,0:T(8,128)(2,1)}, u32[]{:S(2)}, u32[]{:S(2)}) collective-permute-start(bf16[8,384,192]{1,2,0:T(8,128)(2,1)} %constant_dynamic-slice_fusion.5), channel_id=1, source_target_pairs={{0,2},{1,3},{2,0},{3,1},{4,6},{5,7},{6,4},{7,5},{8,10},{9,11},{10,... | collective-permute-start | bytes 3538952 | tf_op jit(solution)/shard_map/ppermute | solution.py:313
  447.4 8.9 %collective-permute-start.2 = (bf16[4,1,96,576]{3,2,0,1:T(8,128)(2,1)S(1)}, bf16[4,1,96,576]{3,2,0,1:T(8,128)(2,1)S(1)}, u32[]{:S(2)}, u32[]{:S(2)}) collective-permute-start(bf16[4,1,96,576]{3,2,0,1:T(8,128)(2,1)S(1)} %dynamic-slice_bitcast_fusion.1), channel_id=1, source_target_pairs={{0,4},{4,0},{8,12},{12,8},{16,20},{20,16},{24,28},{28,24},{1,5},{5... | collective-permute-start | bytes 1327112 | tf_op jit(solution)/shard_map/ppermute | solution.py:313
  451.2 6.1 %copy-start.4 = (bf16[8,96,1536]{2,1,0:T(8,128)(2,1)}, bf16[8,96,1536]{2,1,0:T(8,128)(2,1)S(1)}, u32[]{:S(2)}) copy-start(bf16[8,96,1536]{2,1,0:T(8,128)(2,1)S(1)} %add_convert_fusion.2) | copy-start | bytes 7077892
  452.4 57.0 %collective-permute-start.15 = (bf16[8,96,768]{2,1,0:T(8,128)(2,1)}, bf16[8,96,768]{2,1,0:T(8,128)(2,1)}, u32[]{:S(2)}, u32[]{:S(2)}) collective-permute-start(bf16[8,96,768]{2,1,0:T(8,128)(2,1)} %constant_dynamic-slice_fusion.10), channel_id=1, source_target_pairs={{0,2},{1,3},{2,0},{3,1},{4,6},{5,7},{6,4},{7,5},{8,10},{9,11},{10,... | collective-permute-start | bytes 3538952 | tf_op jit(solution)/shard_map/ppermute | solution.py:313
  457.3 9.4 %collective-permute-start.3 = (bf16[2,1,96,576]{3,2,1,0:T(8,128)(2,1)S(1)}, bf16[2,1,96,576]{3,2,1,0:T(8,128)(2,1)}, u32[]{:S(2)}, u32[]{:S(2)}) collective-permute-start(bf16[2,1,96,576]{3,2,1,0:T(8,128)(2,1)S(1)} %constant_dynamic-slice_fusion.17), channel_id=1, source_target_pairs={{0,8},{4,12},{8,0},{12,4},{16,24},{20,28},{24,16},{28,20},{1,9},{5... | collective-permute-start | bytes 663560 | tf_op jit(solution)/shard_map/ppermute | solution.py:313
  467.7 7.2 %collective-permute-start.4 = (bf16[1,1,96,576]{3,2,1,0:T(8,128)(2,1)S(1)}, bf16[1,1,96,576]{3,2,1,0:T(8,128)(2,1)S(1)}, u32[]{:S(2)}, u32[]{:S(2)}) collective-permute-start(bf16[1,1,96,576]{3,2,1,0:T(8,128)(2,1)S(1)} %constant_dynamic-slice_fusion.16), channel_id=1, source_target_pairs={{0,16},{4,20},{8,24},{12,28},{16,0},{20,4},{24,8},{28,12},{1,17},{... | collective-permute-start | bytes 331784 | tf_op jit(solution)/shard_map/ppermute | solution.py:313
  474.9 34.5 %copy-start.5 = (bf16[8,96,1536]{2,1,0:T(8,128)(2,1)S(1)}, bf16[8,96,1536]{2,1,0:T(8,128)(2,1)}, u32[]{:S(2)}) copy-start(bf16[8,96,1536]{2,1,0:T(8,128)(2,1)} %copy-done.4) | copy-start | bytes 7077892
  474.9 37.6 %collective-permute-start.5 = (bf16[96,576]{1,0:T(8,128)(2,1)S(1)}, bf16[96,576]{1,0:T(8,128)(2,1)S(1)}, u32[]{:S(2)}, u32[]{:S(2)}) collective-permute-start(bf16[96,576]{1,0:T(8,128)(2,1)S(1)} %fusion.8), channel_id=1, source_target_pairs={{0,2},{1,3},{2,0},{3,1},{4,6},{5,7},{6,4},{7,5},{8,10},{9,11},{10,... | collective-permute-start | bytes 331784 | tf_op jit(solution)/shard_map/ppermute | solution.py:313
  489.5 23.3 %collective-permute-start.23 = (bf16[4,1,384,192]{2,3,1,0:T(8,128)(2,1)S(1)}, bf16[4,1,384,192]{2,3,1,0:T(8,128)(2,1)S(1)}, u32[]{:S(2)}, u32[]{:S(2)}) collective-permute-start(bf16[4,1,384,192]{2,3,1,0:T(8,128)(2,1)S(1)} %constant_dynamic-slice_fusion.4), channel_id=1, source_target_pairs={{0,4},{4,0},{8,12},{12,8},{16,20},{20,16},{24,28},{28,24},{1,5},{5... | collective-permute-start | bytes 1769480 | tf_op jit(solution)/shard_map/ppermute | solution.py:313
  511.0 10.1 %collective-permute-start.16 = (bf16[4,1,96,768]{3,2,0,1:T(8,128)(2,1)S(1)}, bf16[4,1,96,768]{3,2,0,1:T(8,128)(2,1)}, u32[]{:S(2)}, u32[]{:S(2)}) collective-permute-start(bf16[4,1,96,768]{3,2,0,1:T(8,128)(2,1)S(1)} %dynamic-slice_bitcast_fusion), channel_id=1, source_target_pairs={{0,4},{4,0},{8,12},{12,8},{16,20},{20,16},{24,28},{28,24},{1,5},{5... | collective-permute-start | bytes 1769480 | tf_op jit(solution)/shard_map/ppermute | solution.py:313
  512.7 36.8 %collective-permute-start.6 = (bf16[96,1152]{1,0:T(8,128)(2,1)S(1)}, bf16[96,1152]{1,0:T(8,128)(2,1)}, u32[]{:S(2)}, u32[]{:S(2)}) collective-permute-start(bf16[96,1152]{1,0:T(8,128)(2,1)S(1)} %maximum_select_fusion.5), channel_id=1, source_target_pairs={{0,1},{1,0},{2,3},{3,2},{4,5},{5,4},{6,7},{7,6},{8,9},{9,8},{10,11... | collective-permute-start | bytes 663560 | tf_op jit(solution)/shard_map/ppermute | solution.py:313
  513.2 12.1 %collective-permute-start.24 = (bf16[2,1,384,192]{3,2,1,0:T(8,128)(2,1)S(1)}, bf16[2,1,384,192]{3,2,1,0:T(8,128)(2,1)}, u32[]{:S(2)}, u32[]{:S(2)}) collective-permute-start(bf16[2,1,384,192]{3,2,1,0:T(8,128)(2,1)S(1)} %copy.107), channel_id=1, source_target_pairs={{0,8},{4,12},{8,0},{12,4},{16,24},{20,28},{24,16},{28,20},{1,9},{5... | collective-permute-start | bytes 884744 | tf_op jit(solution)/shard_map/ppermute | solution.py:313
  522.3 11.5 %collective-permute-start.17 = (bf16[2,1,96,768]{3,2,1,0:T(8,128)(2,1)S(1)}, bf16[2,1,96,768]{3,2,1,0:T(8,128)(2,1)S(1)}, u32[]{:S(2)}, u32[]{:S(2)}) collective-permute-start(bf16[2,1,96,768]{3,2,1,0:T(8,128)(2,1)S(1)} %constant_dynamic-slice_fusion.9), channel_id=1, source_target_pairs={{0,8},{4,12},{8,0},{12,4},{16,24},{20,28},{24,16},{28,20},{1,9},{5... | collective-permute-start | bytes 884744 | tf_op jit(solution)/shard_map/ppermute | solution.py:313
  526.4 15.8 %collective-permute-start.25 = (bf16[1,1,384,192]{3,2,1,0:T(8,128)(2,1)S(1)}, bf16[1,1,384,192]{3,2,1,0:T(8,128)(2,1)S(1)}, u32[]{:S(2)}, u32[]{:S(2)}) collective-permute-start(bf16[1,1,384,192]{3,2,1,0:T(8,128)(2,1)S(1)} %constant_dynamic-slice_fusion.1), channel_id=1, source_target_pairs={{0,16},{4,20},{8,24},{12,28},{16,0},{20,4},{24,8},{28,12},{1,17},{... | collective-permute-start | bytes 442376 | tf_op jit(solution)/shard_map/ppermute | solution.py:313
  534.0 17.4 %copy-start.16 = (f32[384,768]{1,0:T(8,128)S(1)}, f32[384,768]{1,0:T(8,128)}, u32[]{:S(2)}) copy-start(f32[384,768]{1,0:T(8,128)} %param.22) | copy-start | bytes 3538948
  534.0 17.4 %copy-start.24 = (f32[384,768]{1,0:T(8,128)S(1)}, f32[384,768]{1,0:T(8,128)}, u32[]{:S(2)}) copy-start(f32[384,768]{1,0:T(8,128)} %param.25) | copy-start | bytes 3538948
  534.0 10.0 %collective-permute-start.18 = (bf16[1,1,96,768]{3,2,1,0:T(8,128)(2,1)S(1)}, bf16[1,1,96,768]{3,2,1,0:T(8,128)(2,1)S(1)}, u32[]{:S(2)}, u32[]{:S(2)}) collective-permute-start(bf16[1,1,96,768]{3,2,1,0:T(8,128)(2,1)S(1)} %constant_dynamic-slice_fusion.8), channel_id=1, source_target_pairs={{0,16},{4,20},{8,24},{12,28},{16,0},{20,4},{24,8},{28,12},{1,17},{... | collective-permute-start | bytes 442376 | tf_op jit(solution)/shard_map/ppermute | solution.py:313
  542.3 6.8 %collective-permute-start.26 = (bf16[384,192]{1,0:T(8,128)(2,1)S(1)}, bf16[384,192]{1,0:T(8,128)(2,1)S(1)}, u32[]{:S(2)}, u32[]{:S(2)}) collective-permute-start(bf16[384,192]{1,0:T(8,128)(2,1)S(1)} %fusion.6), channel_id=1, source_target_pairs={{0,2},{1,3},{2,0},{3,1},{4,6},{5,7},{6,4},{7,5},{8,10},{9,11},{10,... | collective-permute-start | bytes 442376 | tf_op jit(solution)/shard_map/ppermute | solution.py:313
  544.1 6.7 %collective-permute-start.19 = (bf16[96,768]{1,0:T(8,128)(2,1)S(1)}, bf16[96,768]{1,0:T(8,128)(2,1)S(1)}, u32[]{:S(2)}, u32[]{:S(2)}) collective-permute-start(bf16[96,768]{1,0:T(8,128)(2,1)S(1)} %fusion.7), channel_id=1, source_target_pairs={{0,2},{1,3},{2,0},{3,1},{4,6},{5,7},{6,4},{7,5},{8,10},{9,11},{10,... | collective-permute-start | bytes 442376 | tf_op jit(solution)/shard_map/ppermute | solution.py:313
  549.4 1.9 collective-permute-start.27
  550.8 2.5 copy-start.25
  550.9 3.7 collective-permute-start.20
  553.3 2.5 copy-start.3
  553.3 3.2 copy-start.18
  556.5 3.4 copy-start.19
  559.9 2.2 copy-start.1
  (11 other events, 17.0 us)
Sparse Core Ops, SparseCore 0:
  10.8 140.8 all-gather.3
  154.5 78.0 all-gather.5

commit v2 on v1

--- a/solution.py
+++ b/solution.py
@@ -300,6 +300,346 @@
     )(lens, attended, tokens, cotangent, w_o, w_1, w_2, vec)
 
 
+MESH = pl.DeviceIdType.MESH
+Z_CHIPS = 4
+
+
+def place():
+    dp = lax.axis_index("dp")
+    s = lax.axis_index("seq")
+    return dp, s, dp // 2, dp % 2, s // 2, s % 2
+
+
+def remote(src, dst, send, recv, device):
+    return pltpu.make_async_remote_copy(
+        src_ref=src, dst_ref=dst, send_sem=send, recv_sem=recv, device_id=device, device_id_type=MESH
+    )
+
+
+def greet():
+    dp, s = lax.axis_index("dp"), lax.axis_index("seq")
+    barrier = pltpu.get_barrier_semaphore()
+    for k in range(1, 8):
+        pl.semaphore_signal(barrier, inc=1, device_id=((dp + k) % 8, s), device_id_type=MESH)
+    for k in range(1, 4):
+        pl.semaphore_signal(barrier, inc=1, device_id=(dp, (s + k) % 4), device_id_type=MESH)
+    pl.semaphore_wait(barrier, 10)
+
+
+class Part:
+    def __init__(self, own, out, sems):
+        self.own, self.out = own, out
+        self.z_send, self.z_recv, self.x_send, self.x_recv, self.y_send, self.y_recv, self.c_send, self.c_recv = sems
+        self.dp, self.s, self.z, self.x, self.y, self.c = place()
+        self.rows, cols = own.shape
+        self.half_rows, self.half_cols = self.rows // 2, cols // 2
+
+    def cols(self, core):
+        return pl.ds(pl.multiple_of(core * self.half_cols, 128), self.half_cols)
+
+    def some(self, q):
+        return pl.ds(pl.multiple_of(q * self.half_rows, 16), self.half_rows)
+
+    def block(self, zs, x, core, q=None):
+        rows = slice(None) if q is None else self.some(q)
+        return self.out.at[zs * 2 + x, rows, self.cols(core)]
+
+    def source(self, zs, own, q=None):
+        if own:
+            rows = slice(None) if q is None else self.some(q)
+            return self.own.at[rows, self.cols(self.c)]
+        return self.block(zs, self.x, self.c, q)
+
+    def up(self, zs, own=False):
+        dst = self.block(zs, self.x, self.c)
+        return remote(self.source(zs, own), dst, self.z_send.at[zs, 0], self.z_recv.at[zs], (self.dp + 2, self.s))
+
+    def down(self, zs, own=False):
+        dst = self.block(zs, self.x, self.c)
+        return remote(self.source(zs, own), dst, self.z_send.at[zs, 1], self.z_recv.at[zs], (self.dp - 2, self.s))
+
+    def across(self, zs, own=False):
+        dst = self.block(zs, self.x, self.c, self.y)
+        device = (self.z * 2 + 1 - self.x, self.s)
+        return remote(self.source(zs, own, self.y), dst, self.x_send.at[zs], self.x_recv.at[zs], device)
+
+    def across_in(self, zs):
+        ref = self.block(zs, 1 - self.x, self.c, self.y)
+        return remote(ref, ref, self.x_send.at[zs], self.x_recv.at[zs], (self.dp, self.s))
+
+    def over(self, zs):
+        ref = self.block(zs, 1 - self.x, self.c, self.y)
+        return remote(ref, ref, self.y_send.at[zs], self.y_recv.at[zs], (self.dp, (1 - self.y) * 2 + self.c))
+
+    def over_in(self, zs):
+        ref = self.block(zs, 1 - self.x, self.c, 1 - self.y)
+        return remote(ref, ref, self.y_send.at[zs], self.y_recv.at[zs], (self.dp, self.s))
+
+    def share(self, kind, zs, core):
+        if kind == 0:
+            ref = self.block(zs, self.x, core)
+        else:
+            ref = self.block(zs, 1 - self.x, core, self.y if kind == 1 else 1 - self.y)
+        j = kind * Z_CHIPS + zs
+        return remote(ref, ref, self.c_send.at[j], self.c_recv.at[j], (self.dp, self.s + 1 - 2 * self.c))
+
+    def each(self, k, what):
+        if k == 0:
+            what(self.z)
+            return
+
+        @pl.when(self.z >= k)
+        def _():
+            what(self.z - k)
+
+        @pl.when(self.z + k < Z_CHIPS)
+        def _():
+            what(self.z + k)
+
+    def stage(self, k):
+        if k == 0:
+
+            @pl.when(self.z < Z_CHIPS - 1)
+            def _():
+                self.up(self.z, True).start()
+
+            @pl.when(self.z > 0)
+            def _():
+                self.down(self.z, True).start()
+
+            self.across(self.z, True).start()
+        elif k < Z_CHIPS:
+
+            @pl.when(self.z >= k)
+            def _():
+                zs = self.z - k
+                self.up(zs).wait_recv()
+
+                @pl.when(self.z < Z_CHIPS - 1)
+                def _():
+                    self.up(zs).start()
+
+                self.across(zs).start()
+                self.share(0, zs, self.c).start()
+
+            @pl.when(self.z + k < Z_CHIPS)
+            def _():
+                zs = self.z + k
+                self.down(zs).wait_recv()
+
+                @pl.when(self.z > 0)
+                def _():
+                    self.down(zs).start()
+
+                self.across(zs).start()
+                self.share(0, zs, self.c).start()
+
+        if 1 <= k <= Z_CHIPS:
+
+            def pass_x(zs):
+                self.across_in(zs).wait_recv()
+                self.over(zs).start()
+                self.share(1, zs, self.c).start()
+
+            self.each(k - 1, pass_x)
+        if 2 <= k <= Z_CHIPS + 1:
+
+            def pass_y(zs):
+                self.over_in(zs).wait_recv()
+                self.share(2, zs, self.c).start()
+
+            self.each(k - 2, pass_y)
+
+    stages = Z_CHIPS + 2
+
+    def finish(self):
+        for kind in range(3):
+            for k in range(1 if kind == 0 else 0, Z_CHIPS):
+                self.each(k, lambda zs, kind=kind: self.share(kind, zs, 1 - self.c).wait_recv())
+
+    def settle(self):
+        for k in range(Z_CHIPS):
+
+            @pl.when((self.z >= k) & (self.z < Z_CHIPS - 1))
+            def _():
+                self.up(self.z - k, k == 0).wait_send()
+
+            @pl.when((self.z + k < Z_CHIPS) & (self.z > 0))
+            def _():
+                self.down(self.z + k, k == 0).wait_send()
+
+            self.each(k, lambda zs, k=k: self.across(zs, k == 0).wait_send())
+            self.each(k, lambda zs: self.over(zs).wait_send())
+            for kind in range(3):
+                if kind > 0 or k > 0:
+                    self.each(k, lambda zs, kind=kind: self.share(kind, zs, self.c).wait_send())
+
+
+class Tokens:
+    def __init__(self, long_ref, short_ref, out, send, recv, local):
+        self.long_ref, self.short_ref, self.out, self.send, self.recv, self.local = long_ref, short_ref, out, send, recv, local
+        self.dp, self.s = lax.axis_index("dp"), lax.axis_index("seq")
+
+    def pieces(self, target, source):
+        yield self.long_ref.at[target // 2, target % 2], self.out.at[source, pl.ds(0, 128)]
+        yield self.short_ref.at[0, target], self.out.at[source, pl.ds(128, 64)]
+        yield self.short_ref.at[1, target], self.out.at[source, pl.ds(192, 64)]
+
+    def copies(self, k):
+        target = (self.s + k) % 4
+        for j, (src, dst) in enumerate(self.pieces(target, self.s)):
+            yield remote(src, dst, self.send.at[k, j], self.recv.at[k, j], (self.dp, target))
+
+    def own(self):
+        for j, (src, dst) in enumerate(self.pieces(self.s, self.s)):
+            yield pltpu.make_async_copy(src, dst, self.local.at[j])
+
+    def start(self):
+        for k in range(1, 4):
+            for copy in self.copies(k):
+                copy.start()
+        for copy in self.own():
+            copy.start()
+
+    def finish(self):
+        for copy in self.own():
+            copy.wait()
+        for k in range(1, 4):
+            source = (self.s + 4 - k) % 4
+            for j, (src, dst) in enumerate(self.pieces(self.s, source)):
+                remote(src, dst, self.send.at[k, j], self.recv.at[k, j], (self.dp, self.s)).wait_recv()
+
+    def settle(self):
+        for k in range(1, 4):
+            for copy in self.copies(k):
+                copy.wait_send()
+
+
+def gather_kernel(
+    wide_ref,
+    down_ref,
+    vec_ref,
+    long_in,
+    short_in,
+    long_cot,
+    short_cot,
+    qkv_out,
+    wo_out,
+    w1_out,
+    w2_out,
+    vec_out,
+    tok_out,
+    cot_out,
+    own_wide,
+    own_down,
+    z_send,
+    z_recv,
+    x_send,
+    x_recv,
+    y_send,
+    y_recv,
+    c_send,
+    c_recv,
+    v_send,
+    v_recv,
+    t_send,
+    t_recv,
+    local,
+):
+    dp, s, z, x, y, c = place()
+    greet()
+    tokens = Tokens(long_in, short_in, tok_out, t_send.at[0], t_recv.at[0], local.at[0])
+    cots = Tokens(long_cot, short_cot, cot_out, t_send.at[1], t_recv.at[1], local.at[1])
+    tokens.start()
+    own_wide[...] = wide_ref[...].astype(bf16)
+    own_down[...] = down_ref[...].astype(bf16)
+
+    def vec_copy(k, source, target):
+        return remote(vec_ref, vec_out.at[source], v_send.at[k], v_recv.at[k], (target, s))
+
+    sems = lambda i: [
+        r.at[i] for r in (z_send, z_recv, x_send, x_recv, y_send, y_recv, c_send, c_recv)
+    ]
+    parts = [
+        Part(own_wide.at[:, pl.ds(0, 3 * D)], qkv_out, sems(0)),
+        Part(own_wide.at[:, pl.ds(3 * D, D)], wo_out, sems(1)),
+        Part(own_wide.at[:, pl.ds(4 * D, FF)], w1_out, sems(2)),
+        Part(own_down, w2_out, sems(3)),
+    ]
+    parts[0].stage(0)
+    for k in range(1, 8):
+        vec_copy(k, dp, (dp + k) % 8).start()
+    own_copies = [
+        pltpu.make_async_copy(part.own, part.out.at[dp], local.at[2, i]) for i, part in enumerate(parts)
+    ]
+    own_copies.append(pltpu.make_async_copy(vec_ref, vec_out.at[dp], local.at[2, 4]))
+    for copy in own_copies:
+        copy.start()
+    for t in range(1, Part.stages + len(parts) - 1):
+        for i, part in enumerate(parts):
+            if 0 <= t - i < Part.stages:
+                part.stage(t - i)
+        if t == 4:
+            cots.start()
+    for copy in own_copies:
+        copy.wait()
+    for part in parts:
+        part.finish()
+    tokens.finish()
+    cots.finish()
+    for k in range(1, 8):
+        vec_copy(k, (dp + 8 - k) % 8, dp).wait_recv()
+    for k in range(1, 8):
+        vec_copy(k, dp, (dp + k) % 8).wait_send()
+    for part in parts:
+        part.settle()
+    tokens.settle()
+    cots.settle()
+
+
+def gather(wide_master, down_master, vec_block, long_in, short_in, long_cot, short_cot):
+    any_spec = pl.BlockSpec(memory_space=pl.ANY)
+    vmem = pl.BlockSpec(memory_space=pltpu.VMEM)
+    shape = jax.ShapeDtypeStruct
+    rows, down_rows = wide_master.shape[0], down_master.shape[0]
+    dma = pltpu.SemaphoreType.DMA
+    return pl.pallas_call(
+        gather_kernel,
+        in_specs=[vmem, vmem, vmem] + [any_spec] * 4,
+        out_specs=[any_spec] * 7,
+        out_shape=[
+            shape((8, rows, 3 * D), bf16),
+            shape((8, rows, D), bf16),
+            shape((8, rows, FF), bf16),
+            shape((8, down_rows, D), bf16),
+            shape((8, 16, 128), f32),
+            shape((4, 256, D), bf16),
+            shape((4, 256, D), bf16),
+        ],
+        scratch_shapes=[
+            pltpu.VMEM((rows, 4 * D + FF), bf16),
+            pltpu.VMEM((down_rows, D), bf16),
+            dma((4, 4, 2)),
+            dma((4, 4)),
+            dma((4, 4)),
+            dma((4, 4)),
+            dma((4, 4)),
+            dma((4, 4)),
+            dma((4, 12)),
+            dma((4, 12)),
+            dma((8,)),
+            dma((8,)),
+            dma((2, 4, 3)),
+            dma((2, 4, 3)),
+            dma((3, 5)),
+        ],
+        compiler_params=pltpu.CompilerParams(
+            vmem_limit_bytes=VMEM_BYTES, collective_id=0, has_side_effects=True
+        ),
+        name="gather",
+    )(wide_master, down_master, vec_block, long_in, short_in, long_cot, short_cot)
+
+
 def transpose_dot(left, right):
     return jnp.einsum("ra,rb->ab", left, right, preferred_element_type=f32)
 
@@ -393,15 +733,24 @@
 ):
     s = lax.axis_index("seq")
     lens = jnp.stack([long_len[s // 2, 0, s % 2], short_len[0, 0, s], short_len[1, 0, s]])
-    tokens = exchange(spread_rows(long_in, short_in))
-    cotangent = exchange(spread_rows(long_cot, short_cot))
-    wide_w = lax.all_gather(wide_master.astype(bf16), "dp", axis=0, tiled=True)
-    down_w = lax.all_gather(down_master.astype(bf16), "dp", axis=0, tiled=True)
-    vector_w = lax.all_gather(vector_master.astype(bf16), "dp", axis=0, tiled=True)
-    vec = jnp.transpose(vector_w.astype(f32))
-    w_qkv = wide_w[:, : 3 * D]
-    w_o = wide_w[:, 3 * D : 4 * D]
-    w_1 = wide_w[:, 4 * D :]
+    if lax.axis_size("dp") == 8:
+        vec_own = jnp.transpose(vector_master).astype(bf16).astype(f32)
+        vec_block = jnp.pad(vec_own, ((0, 4), (0, 128 - vec_own.shape[1])))
+        w_qkv, w_o, w_1, w_2, vec_blocks, tokens, cotangent = gather(
+            wide_master, down_master, vec_block, long_in, short_in, long_cot, short_cot
+        )
+        w_qkv, w_o, w_1, w_2 = [w.reshape(-1, w.shape[2]) for w in (w_qkv, w_o, w_1, w_2)]
+        vec = jnp.transpose(vec_blocks[:, :12, : vec_own.shape[1]], (1, 0, 2)).reshape(12, D)
+    else:
+        tokens = exchange(spread_rows(long_in, short_in))
+        cotangent = exchange(spread_rows(long_cot, short_cot))
+        wide_w = lax.all_gather(wide_master.astype(bf16), "dp", axis=0, tiled=True)
+        w_2 = lax.all_gather(down_master.astype(bf16), "dp", axis=0, tiled=True)
+        vector_w = lax.all_gather(vector_master.astype(bf16), "dp", axis=0, tiled=True)
+        vec = jnp.transpose(vector_w.astype(f32))
+        w_qkv = wide_w[:, : 3 * D]
+        w_o = wide_w[:, 3 * D : 4 * D]
+        w_1 = wide_w[:, 4 * D :]
 
     rows = tokens.reshape(1024, D)
     proj_bias = jnp.concatenate([vec[0], jnp.zeros((D,), f32), vec[1]])
@@ -410,7 +759,7 @@
     attended, long_probs, short_probs = attn_forward(lens, qkv)
     flat_attended = attended.reshape(1024, D)
     out, y1b, act, dfb, dub, dab, dob, dh, sums = middle(
-        lens, flat_attended, rows, cotangent.reshape(1024, D), w_o, w_1, down_w, vec
+        lens, flat_attended, rows, cotangent.reshape(1024, D), w_o, w_1, w_2, vec
     )
     d_down = transpose_dot(act, dfb).astype(bf16)
     d_one = transpose_dot(y1b, dub).astype(bf16)

time: 576 us -> 481 us (0.84)
  waiting for transfers between devices: 230 us -> 92.4 us
  Pallas kernels: 78.9 us -> 173 us
  blocking collectives: 84.8 us -> 51.5 us
  between operations: 15.3 us -> 1.51 us
  matrix products: 34.5 us -> 43.9 us
  starting transfers between devices: 41.9 us -> 32.7 us
    all_gather x2 -> x0, waiting for transfers between devices: 136 us -> none  [the longest x1 89.5 us: body(): wide_w = lax.all_gather(wide_master.astype(bf16), 'dp', axis=0, tiled=True)]
    pallas_call x0 -> x1, Pallas kernels: none -> 94.9 us  [gather(): pl.pallas_call(gather_kernel, in_specs=[vmem, vmem, vmem] + [any_spec] *...]
    all_gather x1 -> x0, blocking collectives: 32.3 us -> none  [body(): lax.all_gather(vector_master.astype(bf16), 'dp', axis=0, tiled=True)]
    all_to_all x4 -> x2, starting transfers between devices: 16.7 us -> 9.01 us  [exchange(): return lax.all_to_all(v, 'seq', split_axis=0, concat_axis=0, tiled=True)]
    slice x2 -> x0, local copies, waits for them, and re-layouts: 7.22 us -> none  [the longest x1 4.86 us: body(): w_1 = wide_w[:, 4 * D:]]
    dot_general x4, matrix products: 19.1 us -> 26.1 us  [transpose_dot(): return jnp.einsum('ra,rb->ab', left, right, preferred_element_type=f32)]
    unnamed x96 -> x73, local copies, waits for them, and re-layouts: 20 us -> 20.9 us
  transfers between devices with their start and end apart: 34 -> 30, of which waited for: 18 -> 16; matrix products, arithmetic and copies ran while one was open for 15% -> 16% of each run, Pallas kernels for 6% -> 4%
where the time goes in v2:
time: 481 us; the launch traced here: 475 us
  Pallas kernels  173 us (36%)
  waiting for transfers between devices  92.4 us (19%)
  blocking collectives  51.5 us (11%)
  local copies, waits for them, and re-layouts  44.2 us (9%)
  matrix products  43.9 us (9%)
  other arithmetic  34.9 us (7%)
  starting transfers between devices  32.7 us (7%)
    pallas_call x1, Pallas kernels, gather(): pl.pallas_call(gather_kernel, in_specs=[vmem, vmem, vmem] + [any_spec] *...  94.9 us
    ppermute x28, waiting for transfers between devices, flip(): return lax.ppermute(v, axis, [(i, i ^ bit) for i in range(n)])  88.3 us
    psum x1, blocking collectives, body(): vector_sum = jnp.transpose(lax.psum(vector_total, ('dp', 'seq')))  51.5 us
    pallas_call x1, Pallas kernels, middle(): pl.pallas_call(middle_kernel, grid=(n // rows,), in_specs=[pl.BlockSpec(m...  43 us
    dot_general x4, matrix products, transpose_dot(): return jnp.einsum('ra,rb->ab', left, right, preferred_element_type=f32)  26.1 us
    ppermute x28, starting transfers between devices, flip(): return lax.ppermute(v, axis, [(i, i ^ bit) for i in range(n)])  23.7 us
    unnamed x73, local copies, waits for them, and re-layouts  20.9 us
    convert_element_type x16, other arithmetic, halve(): return (half_of(v, dim, mine).astype(f32) + other.astype(f32)).astype(bf16)  19.2 us
  transfers between devices with their start and end apart: 30, of which 16 were waited for; matrix products, arithmetic and copies ran while one was open for 16% of the time, Pallas kernels for 4%

profile of v2, /device:TPU:0, one launch (start us, length us, event | category | flops | bytes accessed | tf_op | source)
XLA Modules:
  0.0 474.5 jit_solution(17921312652606006491)
XLA Ops:
  2.0 94.9 %gather.1 = (bf16[8,96,2304]{2,1,0:T(8,128)(2,1)}, bf16[8,96,768]{2,1,0:T(8,128)(2,1)}, bf16[8,96,3072]{2,1,0:T(8,128)(2,1)}, bf16[8,384,768]{2,1,0:T(8,128)(2,1...) custom-call(f32[96,6144]{1,0:T(8,128)} %wide_ref.1, f32[384,768]{1,0:T(8,128)} %down_ref.1, ...), custom_call_target="tpu_custom_call" | custom-call | tf_op jit(solution)/shard_map/gather/pallas_call | solution.py:606
  99.8 2.5 pad_add_fusion.lens_ref
  102.4 8.4 %add_convert_fusion = bf16[1024,2304]{1,0:T(8,128)(2,1)} fusion(bf16[1024,768]{1,0:T(8,128)(2,1)} %bitcast.104, bf16[768,2304]{1,0:T(8,128)(2,1)} %bitcast.119, f32[2304]{0:T(1024)S(1)} %pad_maximum_fusion.1), kind=kOutput, calls=%fused_computation | convolution fusion | flops 3628597248 | bytes 9839616 | tf_op jit(solution)/shard_map/dot_general | solution.py:757
  110.8 18.8 %attn_forward.1 = (bf16[4,256,768]{2,1,0:T(8,128)(2,1)}, bf16[12,512,512]{2,1,0:T(8,128)(2,1)}, bf16[12,2,256,256]{3,2,1,0:T(8,128)(2,1)}) custom-call(s32[3]{0:T(128)} %pad_add_fusion.lens_ref, bf16[4,256,2304]{2,1,0:T(8,128)(2,1)} %bitcast.76, bf16[4,256,2304]{2,1,0:T(8,128)(2,1)} %bitcast.77, bf16[4,256,2304]{2,1,0:T(8,128)(2,1)} %bitcast.78), custom_call_target="tpu_custom_call" | custom-call | tf_op jit(solution)/shard_map/attn_forward/pallas_call | solution.py:70
  129.6 43.0 %middle.1 = (bf16[1024,768]{1,0:T(8,128)(2,1)}, bf16[1024,768]{1,0:T(8,128)(2,1)}, bf16[1024,3072]{1,0:T(8,128)(2,1)}, bf16[1024,768]{1,0:T(8,128)(2,1)}, bf16[1...) custom-call(s32[3]{0:T(128)} %pad_add_fusion.lens_ref, ...), custom_call_target="tpu_custom_call" | custom-call | tf_op jit(solution)/shard_map/middle/pallas_call | solution.py:262
  172.7 9.3 %convolution_convert_fusion = bf16[3072,768]{1,0:T(8,128)(2,1)} fusion(bf16[1024,3072]{1,0:T(8,128)(2,1)} %get-tuple-element.61, bf16[1024,768]{1,0:T(8,128)(2,1)} %get-tuple-element.62), kind=kOutput, calls=%fused_computation.2 | convolution fusion | flops 4834197504 | bytes 12582912 | tf_op jit(solution)/shard_map/ra,rb->ab/dot_general | solution.py:644
  182.0 4.4 constant_dynamic-slice_fusion.7
  186.4 4.3 copy.78
  191.2 16.7 %attn_backward.1 = (bf16[4,256,768]{2,1,0:T(8,128)(2,1)}, bf16[4,256,768]{2,1,0:T(8,128)(2,1)}, bf16[4,256,768]{2,1,0:T(8,128)(2,1)}, f32[8,768]{1,0:T(8,128)}) custom-call(s32[3]{0:T(128)} %pad_add_fusion.lens_ref, bf16[4,256,2304]{2,1,0:T(8,128)(2,1)} %bitcast.79, bf16[4,256,2304]{2,1,0:T(8,128)(2,1)} %bitcast.80, bf16[4,256,2304]{2,1,0:T(8,128)(2,1)} %bitcast.81, ...), custom_call_target="tpu_custom_call" | custom-call | tf_op jit(solution)/shard_map/attn_backward/pallas_call | solution.py:140
  207.9 1.6 constant_dynamic-update-slice_fusion.2
  211.2 2.1 copy-done.22
  213.3 5.4 %bitcast_convert_fusion = bf16[768,2304]{1,0:T(8,128)(2,1)} fusion(bf16[4,256,768]{2,1,0:T(8,128)(2,1)S(1)} %copy-done.16, bf16[4,256,2304]{2,1,0:T(8,128)(2,1)S(1)} %constant_dynamic-update-slice_fusion), kind=kOutput, calls=%fused_computation.1 | convolution fusion | flops 3625648128 | bytes 9830400 | tf_op jit(solution)/shard_map/ra,rb->ab/dot_general | solution.py:644
  218.6 3.0 constant_dynamic-slice_fusion.19
  221.6 1.4 convolution_convert_fusion.2
  224.7 9.9 %convolution_convert_fusion.1 = bf16[768,3072]{1,0:T(8,128)(2,1)} fusion(bf16[1024,768]{1,0:T(8,128)(2,1)S(1)} %copy-done.29, bf16[1024,3072]{1,0:T(8,128)(2,1)} %get-tuple-element.60), kind=kOutput, calls=%fused_computation.3 | convolution fusion | flops 4834197504 | bytes 12582912 | tf_op jit(solution)/shard_map/ra,rb->ab/dot_general | solution.py:644
  234.6 1.2 add_convert_fusion.10
  236.7 3.2 constant_dynamic-slice_fusion.11
  239.9 7.4 %collective-permute-done.8 = bf16[8,96,192]{2,1,0:T(8,128)(2,1)} collective-permute-done((bf16[8,96,192]{2,1,0:T(8,128)(2,1)S(1)}, bf16[8,96,192]{2,1,0:T(8,128)(2,1)}, u32[]{:S(2)}, u32[]{:S(2)}) %collective-permute-start.8) | collective-permute-done | bytes 294944 | tf_op jit(solution)/shard_map/ppermute | solution.py:653
  247.3 1.2 add_convert_fusion.13
  249.4 9.4 %add_convert_fusion.4 = bf16[1024,768]{1,0:T(8,128)(2,1)} fusion(f32[1024,768]{1,0:T(8,128)} %get-tuple-element.51, bf16[1024,2304]{1,0:T(8,128)(2,1)} %bitcast.118, bf16[768,2304]{1,0:T(8,128)(2,1)} %bitcast.120), kind=kOutput, calls=%fused_computation.7 | convolution fusion | flops 3625451520 | bytes 12976128 | tf_op jit(solution)/shard_map/ra,ba->rb/dot_general | solution.py:648
  258.8 4.5 all-to-all-start.1
  264.1 51.5 %psum.7 = f32[12,768]{1,0:T(8,128)S(1)} all-reduce(f32[12,768]{1,0:T(8,128)S(1)} %pad_maximum_fusion), channel_id=1, replica_groups=mesh['dp'=8,'seq'=4] {'dp','seq'}, use_global_device_ids=true, to_apply=%region_0.1 | all-reduce | flops 9216 | bytes 73728 | tf_op jit(solution)/shard_map/psum | solution.py:775
  316.5 3.9 collective-permute-done.10
  322.0 2.6 copy.77
  325.6 2.3 collective-permute-start.12
  327.9 2.4 add_convert_fusion.3
  330.4 1.2 copy-done.7
  331.6 1.4 constant_dynamic-slice_fusion.18
  333.2 4.5 all-to-all-start
  337.7 2.5 fusion.11
  340.2 2.5 add_convert_fusion.1
  342.7 1.2 constant_dynamic-slice_fusion.5
  343.8 2.0 collective-permute-start.22
  345.8 12.1 %collective-permute-done.1 = bf16[8,96,576]{2,1,0:T(8,128)(2,1)} collective-permute-done((bf16[8,96,576]{2,1,0:T(8,128)(2,1)}, bf16[8,96,576]{2,1,0:T(8,128)(2,1)}, u32[]{:S(2)}, u32[]{:S(2)}) %collective-permute-start.1) | collective-permute-done | bytes 884768 | tf_op jit(solution)/shard_map/ppermute | solution.py:653
  358.0 1.8 add_convert_fusion.7
  359.8 1.7 collective-permute-start.2
  361.5 3.0 add_convert_fusion.2
  364.6 1.4 copy-done.5
  367.4 1.3 collective-permute-done.2
  369.6 1.1 collective-permute-start.3
  370.8 4.0 all-to-all-done
  374.8 2.4 fusion.12
  380.1 1.2 collective-permute-start.4
  381.3 5.9 %collective-permute-done.4 = bf16[1,1,96,576]{3,2,1,0:T(8,128)(2,1)S(1)} collective-permute-done((bf16[1,1,96,576]{3,2,1,0:T(8,128)(2,1)S(1)}, bf16[1,1,96,576]{3,2,1,0:T(8,128)(2,1)S(1)}, u32[]{:S(2)}, u32[]{:S(2)}) %collective-permute-start.4) | collective-permute-done | bytes 110624 | tf_op jit(solution)/shard_map/ppermute | solution.py:653
  387.4 12.7 %collective-permute-done.22 = bf16[8,384,192]{1,2,0:T(8,128)(2,1)} collective-permute-done((bf16[8,384,192]{1,2,0:T(8,128)(2,1)}, bf16[8,384,192]{1,2,0:T(8,128)(2,1)}, u32[]{:S(2)}, u32[]{:S(2)}) %collective-permute-start.22) | collective-permute-done | bytes 1179680 | tf_op jit(solution)/shard_map/ppermute | solution.py:653
  400.1 1.7 add_convert_fusion.5
  401.8 1.7 collective-permute-start.23
  403.5 19.0 %collective-permute-done.15 = bf16[8,96,768]{2,1,0:T(8,128)(2,1)} collective-permute-done((bf16[8,96,768]{2,1,0:T(8,128)(2,1)}, bf16[8,96,768]{2,1,0:T(8,128)(2,1)}, u32[]{:S(2)}, u32[]{:S(2)}) %collective-permute-start.15) | collective-permute-done | bytes 1179680 | tf_op jit(solution)/shard_map/ppermute | solution.py:653
  422.5 1.6 add_convert_fusion.6
  425.2 1.7 collective-permute-start.24
  427.2 7.0 %collective-permute-done.16 = bf16[4,1,96,768]{3,2,0,1:T(8,128)(2,1)} collective-permute-done((bf16[4,1,96,768]{3,2,0,1:T(8,128)(2,1)S(1)}, bf16[4,1,96,768]{3,2,0,1:T(8,128)(2,1)}, u32[]{:S(2)}, u32[]{:S(2)}) %collective-permute-start.16) | collective-permute-done | bytes 589856 | tf_op jit(solution)/shard_map/ppermute | solution.py:653
  434.2 1.2 add_convert_fusion.9
  438.5 1.8 collective-permute-start.25
  440.3 5.7 %collective-permute-done.17 = bf16[2,1,96,768]{3,2,1,0:T(8,128)(2,1)S(1)} collective-permute-done((bf16[2,1,96,768]{3,2,1,0:T(8,128)(2,1)S(1)}, bf16[2,1,96,768]{3,2,1,0:T(8,128)(2,1)S(1)}, u32[]{:S(2)}, u32[]{:S(2)}) %collective-permute-start.17) | collective-permute-done | bytes 294944 | tf_op jit(solution)/shard_map/ppermute | solution.py:653
  446.9 7.5 %collective-permute-done.25 = bf16[1,1,384,192]{3,2,1,0:T(8,128)(2,1)S(1)} collective-permute-done((bf16[1,1,384,192]{3,2,1,0:T(8,128)(2,1)S(1)}, bf16[1,1,384,192]{3,2,1,0:T(8,128)(2,1)S(1)}, u32[]{:S(2)}, u32[]{:S(2)}) %collective-permute-start.25) | collective-permute-done | bytes 147488 | tf_op jit(solution)/shard_map/ppermute | solution.py:653
  454.5 1.4 collective-permute-start.26
  456.2 1.7 collective-permute-start.19
  457.9 3.6 collective-permute-done.26
  461.8 1.2 maximum_select_fusion.2
  463.7 1.9 fusion.8
  465.6 1.2 multiply_add_fusion.3
  467.0 1.1 copy-done.3
  468.8 3.4 fusion.10
  472.2 2.0 multiply_add_fusion
  (149 shorter events, 27.4 us)
Async XLA Ops:
  0.7 98.6 %copy-start = (s32[2,1,2]{2,1,0:T(1,128)S(1)}, s32[2,1,2]{2,1,0:T(1,128)}, u32[]{:S(2)}) copy-start(s32[2,1,2]{2,1,0:T(1,128)} %param.20) | copy-start | bytes 52
  2.0 96.6 %copy-start.28 = (s32[2,1,4]{2,1,0:T(1,128)S(1)}, s32[2,1,4]{2,1,0:T(1,128)}, u32[]{:S(2)}) copy-start(s32[2,1,4]{2,1,0:T(1,128)} %param.19) | copy-start | bytes 100
  190.6 149.6 %collective-permute-start.21 = (bf16[8,384,384]{1,2,0:T(8,128)(2,1)}, bf16[8,384,384]{1,2,0:T(8,128)(2,1)}, u32[]{:S(2)}, u32[]{:S(2)}) collective-permute-start(bf16[8,384,384]{1,2,0:T(8,128)(2,1)} %copy.78), channel_id=1, source_target_pairs={{0,1},{1,0},{2,3},{3,2},{4,5},{5,4},{6,7},{7,6},{8,9},{9,8},{10,11... | collective-permute-start | bytes 7077896 | tf_op jit(solution)/shard_map/ppermute | solution.py:653
  207.9 1.9 copy-start.18
  209.6 1.5 copy-start.17
  209.9 3.3 copy-start.16
  211.1 2.1 copy-start.22
  218.6 3.0 copy-start.9
  218.6 3.0 copy-start.30
  221.6 106.3 %collective-permute-start = (bf16[8,96,1152]{2,1,0:T(8,128)(2,1)}, bf16[8,96,1152]{2,1,0:T(8,128)(2,1)}, u32[]{:S(2)}, u32[]{:S(2)}) collective-permute-start(bf16[8,96,1152]{2,1,0:T(8,128)(2,1)} %constant_dynamic-slice_fusion.19), channel_id=1, source_target_pairs={{0,1},{1,0},{2,3},{3,2},{4,5},{5,4},{6,7},{7,6},{8,9},{9,8},{10,11... | collective-permute-start | bytes 5308424 | tf_op jit(solution)/shard_map/ppermute | solution.py:653
  221.6 3.1 copy-start.29
  223.1 1.0 copy-start.21
  224.2 10.5 %collective-permute-start.7 = (bf16[8,96,384]{2,1,0:T(8,128)(2,1)S(1)}, bf16[8,96,384]{2,1,0:T(8,128)(2,1)S(1)}, u32[]{:S(2)}, u32[]{:S(2)}) collective-permute-start(bf16[8,96,384]{2,1,0:T(8,128)(2,1)S(1)} %constant_dynamic-slice_fusion.15), channel_id=1, source_target_pairs={{0,1},{1,0},{2,3},{3,2},{4,5},{5,4},{6,7},{7,6},{8,9},{9,8},{10,11... | collective-permute-start | bytes 1769480 | tf_op jit(solution)/shard_map/ppermute | solution.py:653
  236.1 11.2 %collective-permute-start.8 = (bf16[8,96,192]{2,1,0:T(8,128)(2,1)S(1)}, bf16[8,96,192]{2,1,0:T(8,128)(2,1)}, u32[]{:S(2)}, u32[]{:S(2)}) collective-permute-start(bf16[8,96,192]{2,1,0:T(8,128)(2,1)S(1)} %constant_dynamic-slice_fusion.14), channel_id=1, source_target_pairs={{0,2},{1,3},{2,0},{3,1},{4,6},{5,7},{6,4},{7,5},{8,10},{9,11},{10,... | collective-permute-start | bytes 884744 | tf_op jit(solution)/shard_map/ppermute | solution.py:653
  239.9 121.6 %collective-permute-start.14 = (bf16[8,96,1536]{2,1,0:T(8,128)(2,1)}, bf16[8,96,1536]{2,1,0:T(8,128)(2,1)}, u32[]{:S(2)}, u32[]{:S(2)}) collective-permute-start(bf16[8,96,1536]{2,1,0:T(8,128)(2,1)} %constant_dynamic-slice_fusion.11), channel_id=1, source_target_pairs={{0,1},{1,0},{2,3},{3,2},{4,5},{5,4},{6,7},{7,6},{8,9},{9,8},{10,11... | collective-permute-start | bytes 7077896 | tf_op jit(solution)/shard_map/ppermute | solution.py:653
  248.5 67.1 %collective-permute-start.9 = (bf16[4,1,96,192]{3,2,0,1:T(8,128)(2,1)S(1)}, bf16[4,1,96,192]{3,2,0,1:T(8,128)(2,1)S(1)}, u32[]{:S(2)}, u32[]{:S(2)}) collective-permute-start(bf16[4,1,96,192]{3,2,0,1:T(8,128)(2,1)S(1)} %dynamic-slice_bitcast_fusion.2), channel_id=1, source_target_pairs={{0,4},{4,0},{8,12},{12,8},{16,20},{20,16},{24,28},{28,24},{1,5},{5... | collective-permute-start | bytes 442376 | tf_op jit(solution)/shard_map/ppermute | solution.py:653
  258.8 5.3 %copy-start.23 = (f32[16,768]{1,0:T(8,128)S(1)}, f32[16,768]{1,0:T(8,128)}, u32[]{:S(2)}) copy-start(f32[16,768]{1,0:T(8,128)} %get-tuple-element.64) | copy-start | bytes 147460
  258.8 57.1 %copy-start.25 = (f32[96,12]{0,1:T(8,128)S(1)}, f32[96,12]{0,1:T(8,128)}, u32[]{:S(2)}) copy-start(f32[96,12]{0,1:T(8,128)} %param.23) | copy-start | bytes 13828
  258.8 57.1 %copy-start.27 = (f32[96,12]{0,1:T(8,128)S(1)}, f32[96,12]{0,1:T(8,128)}, u32[]{:S(2)}) copy-start(f32[96,12]{0,1:T(8,128)} %param.26) | copy-start | bytes 13828
  258.8 62.6 %copy-start.26 = (f32[96,12]{0,1:T(8,128)S(1)}, f32[96,12]{0,1:T(8,128)}, u32[]{:S(2)}) copy-start(f32[96,12]{0,1:T(8,128)} %param.29) | copy-start | bytes 13828
  258.8 74.4 %all-to-all-start.1 = ((bf16[4,256,768]{2,1,0:T(8,128)(2,1)}), bf16[4,256,768]{2,1,0:T(8,128)(2,1)}, u32[]{:S(2)}, u32[]{:S(2)}) async-start(bf16[4,256,768]{2,1,0:T(8,128)(2,1)} %bitcast.108), calls=%async_computation.1 | async-start | bytes 3145728 | tf_op jit(solution)/shard_map/all_to_all | solution.py:708
  315.8 4.7 collective-permute-start.10
  316.5 8.0 %copy-start.24 = (f32[96,12]{0,1:T(8,128)}, f32[96,12]{0,1:T(8,128)S(1)}, u32[]{:S(2)}) copy-start(f32[96,12]{0,1:T(8,128)S(1)} %get-tuple-element.106) | copy-start | bytes 13828
  320.5 5.1 %collective-permute-start.11 = (bf16[1,1,96,192]{3,2,1,0:T(8,128)(2,1)S(1)}, bf16[1,1,96,192]{3,2,1,0:T(8,128)(2,1)S(1)}, u32[]{:S(2)}, u32[]{:S(2)}) collective-permute-start(bf16[1,1,96,192]{3,2,1,0:T(8,128)(2,1)S(1)} %constant_dynamic-slice_fusion.12), channel_id=1, source_target_pairs={{0,16},{4,20},{8,24},{12,28},{16,0},{20,4},{24,8},{28,12},{1,17},{... | collective-permute-start | bytes 110600 | tf_op jit(solution)/shard_map/ppermute | solution.py:653
  325.6 7.4 %collective-permute-start.12 = (bf16[96,192]{1,0:T(8,128)(2,1)S(1)}, bf16[96,192]{1,0:T(8,128)(2,1)S(1)}, u32[]{:S(2)}, u32[]{:S(2)}) collective-permute-start(bf16[96,192]{1,0:T(8,128)(2,1)S(1)} %fusion.4), channel_id=1, source_target_pairs={{0,2},{1,3},{2,0},{3,1},{4,6},{5,7},{6,4},{7,5},{8,10},{9,11},{10,... | collective-permute-start | bytes 110600 | tf_op jit(solution)/shard_map/ppermute | solution.py:653
  330.4 1.2 copy-start.7
  332.9 25.0 %collective-permute-start.1 = (bf16[8,96,576]{2,1,0:T(8,128)(2,1)}, bf16[8,96,576]{2,1,0:T(8,128)(2,1)}, u32[]{:S(2)}, u32[]{:S(2)}) collective-permute-start(bf16[8,96,576]{2,1,0:T(8,128)(2,1)} %constant_dynamic-slice_fusion.18), channel_id=1, source_target_pairs={{0,2},{1,3},{2,0},{3,1},{4,6},{5,7},{6,4},{7,5},{8,10},{9,11},{10,... | collective-permute-start | bytes 2654216 | tf_op jit(solution)/shard_map/ppermute | solution.py:653
  333.1 48.2 %collective-permute-start.13 = (bf16[96,384]{1,0:T(8,128)(2,1)S(1)}, bf16[96,384]{1,0:T(8,128)(2,1)S(1)}, u32[]{:S(2)}, u32[]{:S(2)}) collective-permute-start(bf16[96,384]{1,0:T(8,128)(2,1)S(1)} %maximum_select_fusion.7), channel_id=1, source_target_pairs={{0,1},{1,0},{2,3},{3,2},{4,5},{5,4},{6,7},{7,6},{8,9},{9,8},{10,11... | collective-permute-start | bytes 221192 | tf_op jit(solution)/shard_map/ppermute | solution.py:653
  333.2 41.6 %all-to-all-start = ((bf16[4,256,768]{2,1,0:T(8,128)(2,1)}), bf16[4,256,768]{2,1,0:T(8,128)(2,1)}, u32[]{:S(2)}, u32[]{:S(2)}) async-start(bf16[4,256,768]{2,1,0:T(8,128)(2,1)} %bitcast.13), calls=%async_computation | async-start | bytes 3145728 | tf_op jit(solution)/shard_map/all_to_all | solution.py:708
  337.7 2.5 copy-start.4
  342.7 15.3 %copy-start.8 = (bf16[8,96,1152]{2,1,0:T(8,128)(2,1)S(1)}, bf16[8,96,1152]{2,1,0:T(8,128)(2,1)}, u32[]{:S(2)}) copy-start(bf16[8,96,1152]{2,1,0:T(8,128)(2,1)} %copy-done.7) | copy-start | bytes 5308420
  343.8 56.2 %collective-permute-start.22 = (bf16[8,384,192]{1,2,0:T(8,128)(2,1)}, bf16[8,384,192]{1,2,0:T(8,128)(2,1)}, u32[]{:S(2)}, u32[]{:S(2)}) collective-permute-start(bf16[8,384,192]{1,2,0:T(8,128)(2,1)} %constant_dynamic-slice_fusion.5), channel_id=1, source_target_pairs={{0,2},{1,3},{2,0},{3,1},{4,6},{5,7},{6,4},{7,5},{8,10},{9,11},{10,... | collective-permute-start | bytes 3538952 | tf_op jit(solution)/shard_map/ppermute | solution.py:653
  359.8 8.9 %collective-permute-start.2 = (bf16[4,1,96,576]{3,2,0,1:T(8,128)(2,1)S(1)}, bf16[4,1,96,576]{3,2,0,1:T(8,128)(2,1)S(1)}, u32[]{:S(2)}, u32[]{:S(2)}) collective-permute-start(bf16[4,1,96,576]{3,2,0,1:T(8,128)(2,1)S(1)} %dynamic-slice_bitcast_fusion.1), channel_id=1, source_target_pairs={{0,4},{4,0},{8,12},{12,8},{16,20},{20,16},{24,28},{28,24},{1,5},{5... | collective-permute-start | bytes 1327112 | tf_op jit(solution)/shard_map/ppermute | solution.py:653
  364.5 1.4 copy-start.5
  367.1 55.4 %collective-permute-start.15 = (bf16[8,96,768]{2,1,0:T(8,128)(2,1)}, bf16[8,96,768]{2,1,0:T(8,128)(2,1)}, u32[]{:S(2)}, u32[]{:S(2)}) collective-permute-start(bf16[8,96,768]{2,1,0:T(8,128)(2,1)} %constant_dynamic-slice_fusion.10), channel_id=1, source_target_pairs={{0,2},{1,3},{2,0},{3,1},{4,6},{5,7},{6,4},{7,5},{8,10},{9,11},{10,... | collective-permute-start | bytes 3538952 | tf_op jit(solution)/shard_map/ppermute | solution.py:653
  368.8 0.8 copy-start.14
  369.6 9.4 %collective-permute-start.3 = (bf16[2,1,96,576]{3,2,1,0:T(8,128)(2,1)S(1)}, bf16[2,1,96,576]{3,2,1,0:T(8,128)(2,1)}, u32[]{:S(2)}, u32[]{:S(2)}) collective-permute-start(bf16[2,1,96,576]{3,2,1,0:T(8,128)(2,1)S(1)} %constant_dynamic-slice_fusion.17), channel_id=1, source_target_pairs={{0,8},{4,12},{8,0},{12,4},{16,24},{20,28},{24,16},{28,20},{1,9},{5... | collective-permute-start | bytes 663560 | tf_op jit(solution)/shard_map/ppermute | solution.py:653
  377.2 1.9 copy-start.15
  380.1 7.2 %collective-permute-start.4 = (bf16[1,1,96,576]{3,2,1,0:T(8,128)(2,1)S(1)}, bf16[1,1,96,576]{3,2,1,0:T(8,128)(2,1)S(1)}, u32[]{:S(2)}, u32[]{:S(2)}) collective-permute-start(bf16[1,1,96,576]{3,2,1,0:T(8,128)(2,1)S(1)} %constant_dynamic-slice_fusion.16), channel_id=1, source_target_pairs={{0,16},{4,20},{8,24},{12,28},{16,0},{20,4},{24,8},{28,12},{1,17},{... | collective-permute-start | bytes 331784 | tf_op jit(solution)/shard_map/ppermute | solution.py:653
  387.3 35.2 %copy-start.6 = (bf16[8,96,1536]{2,1,0:T(8,128)(2,1)S(1)}, bf16[8,96,1536]{2,1,0:T(8,128)(2,1)}, u32[]{:S(2)}) copy-start(bf16[8,96,1536]{2,1,0:T(8,128)(2,1)} %copy-done.5) | copy-start | bytes 7077892
  387.3 37.3 %collective-permute-start.5 = (bf16[96,576]{1,0:T(8,128)(2,1)S(1)}, bf16[96,576]{1,0:T(8,128)(2,1)S(1)}, u32[]{:S(2)}, u32[]{:S(2)}) collective-permute-start(bf16[96,576]{1,0:T(8,128)(2,1)S(1)} %fusion.3), channel_id=1, source_target_pairs={{0,2},{1,3},{2,0},{3,1},{4,6},{5,7},{6,4},{7,5},{8,10},{9,11},{10,... | collective-permute-start | bytes 331784 | tf_op jit(solution)/shard_map/ppermute | solution.py:653
  401.8 23.0 %collective-permute-start.23 = (bf16[4,1,384,192]{2,3,1,0:T(8,128)(2,1)S(1)}, bf16[4,1,384,192]{2,3,1,0:T(8,128)(2,1)S(1)}, u32[]{:S(2)}, u32[]{:S(2)}) collective-permute-start(bf16[4,1,384,192]{2,3,1,0:T(8,128)(2,1)S(1)} %constant_dynamic-slice_fusion.4), channel_id=1, source_target_pairs={{0,4},{4,0},{8,12},{12,8},{16,20},{20,16},{24,28},{28,24},{1,5},{5... | collective-permute-start | bytes 1769480 | tf_op jit(solution)/shard_map/ppermute | solution.py:653
  424.1 10.1 %collective-permute-start.16 = (bf16[4,1,96,768]{3,2,0,1:T(8,128)(2,1)S(1)}, bf16[4,1,96,768]{3,2,0,1:T(8,128)(2,1)}, u32[]{:S(2)}, u32[]{:S(2)}) collective-permute-start(bf16[4,1,96,768]{3,2,0,1:T(8,128)(2,1)S(1)} %dynamic-slice_bitcast_fusion), channel_id=1, source_target_pairs={{0,4},{4,0},{8,12},{12,8},{16,20},{20,16},{24,28},{28,24},{1,5},{5... | collective-permute-start | bytes 1769480 | tf_op jit(solution)/shard_map/ppermute | solution.py:653
  424.7 37.1 %collective-permute-start.6 = (bf16[96,1152]{1,0:T(8,128)(2,1)S(1)}, bf16[96,1152]{1,0:T(8,128)(2,1)}, u32[]{:S(2)}, u32[]{:S(2)}) collective-permute-start(bf16[96,1152]{1,0:T(8,128)(2,1)S(1)} %maximum_select_fusion.5), channel_id=1, source_target_pairs={{0,1},{1,0},{2,3},{3,2},{4,5},{5,4},{6,7},{7,6},{8,9},{9,8},{10,11... | collective-permute-start | bytes 663560 | tf_op jit(solution)/shard_map/ppermute | solution.py:653
  425.2 12.1 %collective-permute-start.24 = (bf16[2,1,384,192]{3,2,1,0:T(8,128)(2,1)S(1)}, bf16[2,1,384,192]{3,2,1,0:T(8,128)(2,1)}, u32[]{:S(2)}, u32[]{:S(2)}) collective-permute-start(bf16[2,1,384,192]{3,2,1,0:T(8,128)(2,1)S(1)} %copy.80), channel_id=1, source_target_pairs={{0,8},{4,12},{8,0},{12,4},{16,24},{20,28},{24,16},{28,20},{1,9},{5... | collective-permute-start | bytes 884744 | tf_op jit(solution)/shard_map/ppermute | solution.py:653
  435.4 10.6 %collective-permute-start.17 = (bf16[2,1,96,768]{3,2,1,0:T(8,128)(2,1)S(1)}, bf16[2,1,96,768]{3,2,1,0:T(8,128)(2,1)S(1)}, u32[]{:S(2)}, u32[]{:S(2)}) collective-permute-start(bf16[2,1,96,768]{3,2,1,0:T(8,128)(2,1)S(1)} %constant_dynamic-slice_fusion.9), channel_id=1, source_target_pairs={{0,8},{4,12},{8,0},{12,4},{16,24},{20,28},{24,16},{28,20},{1,9},{5... | collective-permute-start | bytes 884744 | tf_op jit(solution)/shard_map/ppermute | solution.py:653
  438.4 25.2 %copy-start.10 = (f32[384,768]{1,0:T(8,128)S(1)}, f32[384,768]{1,0:T(8,128)}, u32[]{:S(2)}) copy-start(f32[384,768]{1,0:T(8,128)} %down_ref.1) | copy-start | bytes 3538948
  438.4 25.2 %copy-start.19 = (f32[384,768]{1,0:T(8,128)S(1)}, f32[384,768]{1,0:T(8,128)}, u32[]{:S(2)}) copy-start(f32[384,768]{1,0:T(8,128)} %param.25) | copy-start | bytes 3538948
  438.5 15.9 %collective-permute-start.25 = (bf16[1,1,384,192]{3,2,1,0:T(8,128)(2,1)S(1)}, bf16[1,1,384,192]{3,2,1,0:T(8,128)(2,1)S(1)}, u32[]{:S(2)}, u32[]{:S(2)}) collective-permute-start(bf16[1,1,384,192]{3,2,1,0:T(8,128)(2,1)S(1)} %constant_dynamic-slice_fusion.1), channel_id=1, source_target_pairs={{0,16},{4,20},{8,24},{12,28},{16,0},{20,4},{24,8},{28,12},{1,17},{... | collective-permute-start | bytes 442376 | tf_op jit(solution)/shard_map/ppermute | solution.py:653
  446.1 10.0 %collective-permute-start.18 = (bf16[1,1,96,768]{3,2,1,0:T(8,128)(2,1)S(1)}, bf16[1,1,96,768]{3,2,1,0:T(8,128)(2,1)S(1)}, u32[]{:S(2)}, u32[]{:S(2)}) collective-permute-start(bf16[1,1,96,768]{3,2,1,0:T(8,128)(2,1)S(1)} %constant_dynamic-slice_fusion.8), channel_id=1, source_target_pairs={{0,16},{4,20},{8,24},{12,28},{16,0},{20,4},{24,8},{28,12},{1,17},{... | collective-permute-start | bytes 442376 | tf_op jit(solution)/shard_map/ppermute | solution.py:653
  454.5 7.0 %collective-permute-start.26 = (bf16[384,192]{1,0:T(8,128)(2,1)S(1)}, bf16[384,192]{1,0:T(8,128)(2,1)S(1)}, u32[]{:S(2)}, u32[]{:S(2)}) collective-permute-start(bf16[384,192]{1,0:T(8,128)(2,1)S(1)} %fusion.1), channel_id=1, source_target_pairs={{0,2},{1,3},{2,0},{3,1},{4,6},{5,7},{6,4},{7,5},{8,10},{9,11},{10,... | collective-permute-start | bytes 442376 | tf_op jit(solution)/shard_map/ppermute | solution.py:653
  456.2 6.9 %collective-permute-start.19 = (bf16[96,768]{1,0:T(8,128)(2,1)S(1)}, bf16[96,768]{1,0:T(8,128)(2,1)S(1)}, u32[]{:S(2)}, u32[]{:S(2)}) collective-permute-start(bf16[96,768]{1,0:T(8,128)(2,1)S(1)} %fusion.2), channel_id=1, source_target_pairs={{0,2},{1,3},{2,0},{3,1},{4,6},{5,7},{6,4},{7,5},{8,10},{9,11},{10,... | collective-permute-start | bytes 442376 | tf_op jit(solution)/shard_map/ppermute | solution.py:653
  461.7 1.9 collective-permute-start.27
  463.1 2.5 copy-start.20
  463.1 3.7 collective-permute-start.20
  465.6 1.4 copy-start.11
  465.6 2.5 copy-start.3
  465.6 3.2 copy-start.12
  468.8 3.4 copy-start.13
  472.2 2.2 copy-start.2
  472.2 2.2 copy-start.1

commit v3 on v2

--- a/solution.py
+++ b/solution.py
@@ -640,6 +640,305 @@
     )(wide_master, down_master, vec_block, long_in, short_in, long_cot, short_cot)
 
 
+class Grad:
+    def __init__(self, src, acc, cbuf, xbuf, ybuf, zbuf, fin, sems, order):
+        self.src, self.acc, self.cbuf, self.xbuf, self.ybuf, self.zbuf, self.fin = src, acc, cbuf, xbuf, ybuf, zbuf, fin
+        self.c_send, self.c_recv, self.x_send, self.x_recv, self.y_send, self.y_recv = sems[:6]
+        self.z_send, self.z_recv, self.f_send, self.f_recv, self.local = sems[6:]
+        self.order = order
+        self.dp, self.s, self.z, self.x, self.y, self.c = place()
+        self.rows, cols = src.shape[2:]
+        self.half_rows, self.half_cols = self.rows // 2, cols // 2
+
+    def cols(self, core):
+        return pl.ds(pl.multiple_of(core * self.half_cols, 128), self.half_cols)
+
+    def some(self, q):
+        return pl.ds(pl.multiple_of(q * self.half_rows, 16), self.half_rows)
+
+    def core_copy(self, j):
+        xd = (1 - self.x) if j == 0 else self.x
+        return remote(
+            self.src.at[:, xd, :, self.cols(1 - self.c)],
+            self.cbuf.at[:, xd],
+            self.c_send.at[j],
+            self.c_recv.at[j],
+            (self.dp, self.s + 1 - 2 * self.c),
+        )
+
+    def own_copy(self, j):
+        xd = (1 - self.x) if j == 0 else self.x
+        return pltpu.make_async_copy(self.src.at[:, xd, :, self.cols(self.c)], self.acc.at[:, xd], self.local.at[j])
+
+    def x_copy(self, zd):
+        device = (self.z * 2 + 1 - self.x, self.s)
+        return remote(
+            self.acc.at[zd, 1 - self.x], self.xbuf.at[zd], self.x_send.at[zd], self.x_recv.at[zd], device
+        )
+
+    def y_copy(self, zd):
+        device = (self.dp, (1 - self.y) * 2 + self.c)
+        return remote(
+            self.acc.at[zd, self.x, self.some(1 - self.y)],
+            self.ybuf.at[zd],
+            self.y_send.at[zd],
+            self.y_recv.at[zd],
+            device,
+        )
+
+    def z_copy(self, k):
+        zd = (self.z + k) % Z_CHIPS
+        src = self.acc.at[zd, self.x, self.some(self.y)] if self.order == "xyz" else self.acc.at[zd]
+        return remote(
+            src, self.zbuf.at[k], self.z_send.at[k], self.z_recv.at[k], (zd * 2 + self.x, self.s)
+        )
+
+    def fin_quarter(self, s):
+        return self.fin.at[self.some(s // 2), self.cols(s % 2)]
+
+    def fin_copy(self, k):
+        return remote(
+            self.fin_quarter(self.s),
+            self.fin_quarter(self.s),
+            self.f_send.at[k],
+            self.f_recv.at[k],
+            (self.dp, (self.s + k) % 4),
+        )
+
+    def fin_in(self, k):
+        ref = self.fin_quarter((self.s + 4 - k) % 4)
+        return remote(ref, ref, self.f_send.at[k], self.f_recv.at[k], (self.dp, self.s))
+
+    def core_add(self, j):
+        xd = (1 - self.x) if j == 0 else self.x
+        self.core_copy(j).wait_recv()
+        self.own_copy(j).wait()
+
+        def one(zd, carry):
+            self.acc[zd, xd] = (self.acc[zd, xd].astype(f32) + self.cbuf[zd, xd].astype(f32)).astype(bf16)
+            return carry
+
+        lax.fori_loop(0, Z_CHIPS, one, 0)
+
+    def publish(self, total):
+        self.fin[self.some(self.y), self.cols(self.c)] = total.astype(bf16)
+        for k in range(1, 4):
+            self.fin_copy(k).start()
+
+    stages = 7
+
+    def stage(self, i):
+        if i == 0:
+            for j in range(2):
+                self.core_copy(j).start()
+                self.own_copy(j).start()
+        elif self.order == "xyz":
+            if i == 1:
+                self.core_add(0)
+                for k in range(Z_CHIPS):
+                    self.x_copy((self.z + k) % Z_CHIPS).start()
+            elif i == 2:
+                self.core_add(1)
+            elif i == 3:
+                for k in range(Z_CHIPS):
+                    zd = (self.z + k) % Z_CHIPS
+                    self.x_copy(zd).wait_recv()
+                    self.acc[zd, self.x] = (self.acc[zd, self.x].astype(f32) + self.xbuf[zd].astype(f32)).astype(bf16)
+                    self.y_copy(zd).start()
+            elif i == 4:
+                for k in (1, 2, 3, 0):
+                    zd = (self.z + k) % Z_CHIPS
+                    self.y_copy(zd).wait_recv()
+                    rows = self.some(self.y)
+                    self.acc[zd, self.x, rows] = (
+                        self.acc[zd, self.x, rows].astype(f32) + self.ybuf[zd].astype(f32)
+                    ).astype(bf16)
+                    if k:
+                        self.z_copy(k).start()
+            elif i == 5:
+                total = self.acc[self.z, self.x, self.some(self.y)].astype(f32)
+                for k in range(1, Z_CHIPS):
+                    self.z_copy(k).wait_recv()
+                    total = total + self.zbuf[k].astype(f32)
+                self.publish(total)
+        else:
+            if i == 1:
+                self.core_add(0)
+                self.core_add(1)
+                for k in range(1, Z_CHIPS):
+                    self.z_copy(k).start()
+            elif i == 3:
+                for k in range(1, Z_CHIPS):
+                    self.z_copy(k).wait_recv()
+                for xd in range(2):
+                    total = self.acc[self.z, xd].astype(f32)
+                    for k in range(1, Z_CHIPS):
+                        total = total + self.zbuf[k, xd].astype(f32)
+                    self.acc[self.z, xd] = total.astype(bf16)
+                self.x_copy(self.z).start()
+            elif i == 4:
+                self.x_copy(self.z).wait_recv()
+                total = self.acc[self.z, self.x].astype(f32) + self.xbuf[self.z].astype(f32)
+                self.acc[self.z, self.x] = total.astype(bf16)
+                self.y_copy(self.z).start()
+            elif i == 5:
+                self.y_copy(self.z).wait_recv()
+                self.publish(self.acc[self.z, self.x, self.some(self.y)].astype(f32) + self.ybuf[self.z].astype(f32))
+        if i == 6:
+            for k in range(1, 4):
+                self.fin_in(k).wait_recv()
+
+    def settle(self):
+        for j in range(2):
+            self.core_copy(j).wait_send()
+        for k in range(1, Z_CHIPS):
+            self.z_copy(k).wait_send()
+        for k in range(1, 4):
+            self.fin_copy(k).wait_send()
+        for k in range(Z_CHIPS if self.order == "xyz" else 1):
+            self.x_copy((self.z + k) % Z_CHIPS).wait_send()
+            self.y_copy((self.z + k) % Z_CHIPS).wait_send()
+
+
+class Returns:
+    def __init__(self, rows_ref, long_out, short_out, send, recv, local):
+        self.rows_ref, self.long_out, self.short_out = rows_ref, long_out, short_out
+        self.send, self.recv, self.local = send, recv, local
+        self.dp, self.s = lax.axis_index("dp"), lax.axis_index("seq")
+
+    def pieces(self, target, source):
+        yield self.rows_ref.at[target, pl.ds(0, 128)], self.long_out.at[source // 2, source % 2]
+        yield self.rows_ref.at[target, pl.ds(128, 64)], self.short_out.at[0, source]
+        yield self.rows_ref.at[target, pl.ds(192, 64)], self.short_out.at[1, source]
+
+    copies, own, start, finish, settle = Tokens.copies, Tokens.own, Tokens.start, Tokens.finish, Tokens.settle
+
+
+class Sums:
+    def __init__(self, src, sbuf, part, dbuf, out, sems):
+        self.src, self.sbuf, self.part, self.dbuf, self.out = src, sbuf, part, dbuf, out
+        self.s_send, self.s_recv, self.d_send, self.d_recv = sems
+        self.dp, self.s = lax.axis_index("dp"), lax.axis_index("seq")
+
+    def s_copy(self, k, source):
+        return remote(self.src, self.sbuf.at[source], self.s_send.at[k], self.s_recv.at[k], (self.dp, (self.s + k) % 4))
+
+    def d_copy(self, k, source):
+        target = (self.dp + k) % 8
+        return remote(
+            self.part.at[target], self.dbuf.at[source], self.d_send.at[k], self.d_recv.at[k], (target, self.s)
+        )
+
+    def stage(self, i):
+        if i == 0:
+            for k in range(1, 4):
+                self.s_copy(k, self.s).start()
+            self.sbuf[self.s] = self.src[...]
+        elif i == 1:
+            for k in range(1, 4):
+                self.s_copy(k, (self.s + 4 - k) % 4).wait_recv()
+            self.part[...] = (self.sbuf[0] + self.sbuf[1]) + (self.sbuf[2] + self.sbuf[3])
+            for k in range(1, 8):
+                self.d_copy(k, self.dp).start()
+            self.dbuf[self.dp] = self.part[self.dp]
+        elif i == 2:
+            for k in range(1, 8):
+                self.d_copy(k, (self.dp + 8 - k) % 8).wait_recv()
+            total = self.dbuf[0]
+            for d in range(1, 8):
+                total = total + self.dbuf[d]
+            self.out[...] = total
+
+    def settle(self):
+        for k in range(1, 4):
+            self.s_copy(k, self.s).wait_send()
+        for k in range(1, 8):
+            self.d_copy(k, self.dp).wait_send()
+
+
+ORDERS = ("zxy", "xyz", "xyz", "xyz")
+
+
+def reduce_kernel(count, *refs):
+    grads, refs = refs[:count], refs[count:]
+    sums_ref, out_rows, back_rows, refs = refs[0], refs[1], refs[2], refs[3:]
+    fins, refs = refs[:count], refs[count:]
+    (sums_out, short_out, long_out, short_back, long_back), refs = refs[:5], refs[5:]
+    bufs, refs = refs[: 5 * count], refs[5 * count :]
+    (sbuf, part, dbuf), refs = refs[:3], refs[3:]
+    sems, refs = refs[:11], refs[11:]
+    s_sems, (t_send, t_recv, local) = refs[:4], refs[4:]
+    greet()
+    pieces = []
+    for i in range(count):
+        acc, cbuf, xbuf, ybuf, zbuf = bufs[5 * i : 5 * i + 5]
+        pieces.append(
+            Grad(grads[i], acc, cbuf, xbuf, ybuf, zbuf, fins[i], [r.at[i] for r in sems], ORDERS[i])
+        )
+    sums = Sums(sums_ref, sbuf, part, dbuf, sums_out, s_sems)
+    outs = Returns(out_rows, long_out, short_out, t_send.at[0], t_recv.at[0], local.at[0])
+    backs = Returns(back_rows, long_back, short_back, t_send.at[1], t_recv.at[1], local.at[1])
+    outs.start()
+    for t in range(Grad.stages + count - 1):
+        for i, piece in enumerate(pieces):
+            if 0 <= t - i < Grad.stages:
+                piece.stage(t - i)
+        if t < 3:
+            sums.stage(t)
+        if t == 2:
+            backs.start()
+    outs.finish()
+    backs.finish()
+    for piece in pieces:
+        piece.settle()
+    sums.settle()
+    outs.settle()
+    backs.settle()
+
+
+def reduce_all(grads, sums, out_rows, back_rows):
+    count = len(grads)
+    any_spec = pl.BlockSpec(memory_space=pl.ANY)
+    vmem = pl.BlockSpec(memory_space=pltpu.VMEM)
+    shape = jax.ShapeDtypeStruct
+    dma = pltpu.SemaphoreType.DMA
+    bufs = []
+    for g, order in zip(grads, ORDERS):
+        rows, cols = g.shape[2:]
+        half, cut = cols // 2, rows // 2
+        bufs += [
+            pltpu.VMEM((4, 2, rows, half), bf16),
+            pltpu.VMEM((4, 2, rows, half), bf16),
+            pltpu.VMEM((4, rows, half), bf16),
+            pltpu.VMEM((4, cut, half), bf16),
+            pltpu.VMEM((4, cut, half) if order == "xyz" else (4, 2, rows, half), bf16),
+        ]
+    return pl.pallas_call(
+        lambda *refs: reduce_kernel(count, *refs),
+        in_specs=[any_spec] * count + [vmem, any_spec, any_spec],
+        out_specs=[vmem] * count + [vmem] + [any_spec] * 4,
+        out_shape=[shape(g.shape[2:], bf16) for g in grads]
+        + [
+            shape((16, 128), f32),
+            shape((2, 4, 64, D), bf16),
+            shape((2, 2, 128, D), bf16),
+            shape((2, 4, 64, D), bf16),
+            shape((2, 2, 128, D), bf16),
+        ],
+        scratch_shapes=bufs
+        + [pltpu.VMEM((4, 8, 16, 128), f32), pltpu.VMEM((8, 16, 128), f32), pltpu.VMEM((8, 16, 128), f32)]
+        + [dma((count, 2))] * 2
+        + [dma((count, 4))] * 8
+        + [dma((count, 2))]
+        + [dma((4,)), dma((4,)), dma((8,)), dma((8,))]
+        + [dma((2, 4, 3)), dma((2, 4, 3)), dma((2, 3))],
+        compiler_params=pltpu.CompilerParams(
+            vmem_limit_bytes=VMEM_BYTES, collective_id=1, has_side_effects=True
+        ),
+        name="reduce",
+    )(*grads, sums, out_rows, back_rows)
+
+
 def transpose_dot(left, right):
     return jnp.einsum("ra,rb->ab", left, right, preferred_element_type=f32)
 
@@ -772,14 +1071,24 @@
     back = (dh + right_dot(d_qkv, w_qkv)).astype(bf16).reshape(4, 256, D)
 
     vector_total = jnp.concatenate([qv_sums[:2], sums[2:12]], axis=0)
-    vector_sum = jnp.transpose(lax.psum(vector_total, ("dp", "seq")))
     own_rows = vector_master.shape[0]
-    vector_reduced = lax.dynamic_slice_in_dim(vector_sum, lax.axis_index("dp") * own_rows, own_rows, 0)
-    wide_reduced = jnp.concatenate([reduce_rows(d_wqkv), reduce_rows(d_o), reduce_rows(d_one)], axis=1)
-    down_reduced = reduce_rows(d_down)
-
-    short_out, long_out = collect_rows(exchange(out.reshape(4, 256, D)))
-    short_back, long_back = collect_rows(exchange(back))
+    if lax.axis_size("dp") == 8:
+        blocks = lambda g: g.reshape(4, 2, g.shape[0] // 8, g.shape[1])
+        spread = jnp.transpose(vector_total.reshape(12, 8, own_rows), (1, 0, 2))
+        spread = jnp.pad(spread, ((0, 0), (0, 4), (0, 128 - own_rows)))
+        down_low, one_low, o_low, qkv_low, sums_own, short_out, long_out, short_back, long_back = reduce_all(
+            [blocks(g) for g in (d_down, d_one, d_o, d_wqkv)], spread, out.reshape(4, 256, D), back
+        )
+        vector_reduced = jnp.transpose(sums_own[:12, :own_rows])
+        wide_reduced = jnp.concatenate([qkv_low, o_low, one_low], axis=1).astype(f32)
+        down_reduced = down_low.astype(f32)
+    else:
+        vector_sum = jnp.transpose(lax.psum(vector_total, ("dp", "seq")))
+        vector_reduced = lax.dynamic_slice_in_dim(vector_sum, lax.axis_index("dp") * own_rows, own_rows, 0)
+        wide_reduced = jnp.concatenate([reduce_rows(d_wqkv), reduce_rows(d_o), reduce_rows(d_one)], axis=1)
+        down_reduced = reduce_rows(d_down)
+        short_out, long_out = collect_rows(exchange(out.reshape(4, 256, D)))
+        short_back, long_back = collect_rows(exchange(back))
     wide_new = update(wide_master, wide_reduced, wide_moment, wide_average)
     down_new = update(down_master, down_reduced, down_moment, down_average)
     vector_new = update(vector_master, vector_reduced, vector_moment, vector_average)

time: 481 us -> 379 us (0.79); the launches traced: 475 us -> 378 us
  Pallas kernels: 173 us -> 311 us
  waiting for transfers between devices: 92.4 us -> 0 us
  blocking collectives: 51.5 us -> 0 us
  starting transfers between devices: 32.7 us -> 0 us
  local copies, waits for them, and re-layouts: 44.2 us -> 15.5 us
  other arithmetic: 34.9 us -> 15.2 us
  matrix products: 43.9 us -> 35.3 us
    pallas_call x0 -> x1, Pallas kernels: none -> 137 us  [reduce_all(): pl.pallas_call(lambda *refs: reduce_kernel(count, *refs), in_specs=[any_s...]
    ppermute x28 -> x0, waiting for transfers between devices: 88.3 us -> none  [flip(): return lax.ppermute(v, axis, [(i, i ^ bit) for i in range(n)])]
    psum x1 -> x0, blocking collectives: 51.5 us -> none  [body(): vector_sum = jnp.transpose(lax.psum(vector_total, ('dp', 'seq')))]
    ppermute x28 -> x0, starting transfers between devices: 23.7 us -> none  [flip(): return lax.ppermute(v, axis, [(i, i ^ bit) for i in range(n)])]
    convert_element_type x16 -> x0, other arithmetic: 19.2 us -> none  [halve(): return (half_of(v, dim, mine).astype(f32) + other.astype(f32)).astype(bf16)]
    dynamic_slice x17 -> x0, local copies, waits for them, and re-layouts: 14.7 us -> none  [half_of(): return lax.dynamic_slice_in_dim(v, which * size, size, dim)]
    unnamed x73 -> x76, local copies, waits for them, and re-layouts: 20.9 us -> 10.2 us
    all_to_all x2 -> x0, starting transfers between devices: 9.01 us -> none  [exchange(): return lax.all_to_all(v, 'seq', split_axis=0, concat_axis=0, tiled=True)]
  transfers between devices with their start and end apart: 30 -> 0, of which waited for: 16 -> 0; matrix products, arithmetic and copies ran while one was open for 16% -> 0% of each run, Pallas kernels for 4% -> 0%
where the time goes in v3:
time: 379 us; the launch traced here: 378 us
  Pallas kernels  311 us (82%)
  matrix products  35.3 us (9%)
  local copies, waits for them, and re-layouts  15.5 us (4%)
  other arithmetic  15.2 us (4%)
    pallas_call x1, Pallas kernels, reduce_all(): pl.pallas_call(lambda *refs: reduce_kernel(count, *refs), in_specs=[any_s...  137 us
    pallas_call x1, Pallas kernels, gather(): pl.pallas_call(gather_kernel, in_specs=[vmem, vmem, vmem] + [any_spec] *...  94.9 us
    pallas_call x1, Pallas kernels, middle(): pl.pallas_call(middle_kernel, grid=(n // rows,), in_specs=[pl.BlockSpec(m...  43 us
    dot_general x4, matrix products, transpose_dot(): return jnp.einsum('ra,rb->ab', left, right, preferred_element_type=f32)  22 us
    pallas_call x1, Pallas kernels, attn_forward(): pl.pallas_call(attn_forward_kernel, grid=(pairs,), in_specs=[pl.BlockSpec...  18.7 us
    pallas_call x1, Pallas kernels, attn_backward(): pl.pallas_call(attn_backward_kernel, grid=(pairs,), in_specs=[pl.BlockSpe...  17.2 us
    unnamed x76, local copies, waits for them, and re-layouts  10.2 us
    dot_general x1, matrix products, body(): jnp.dot(rows, w_qkv, preferred_element_type=f32) + proj_bias  8.4 us

profile of v3, /device:TPU:0, one launch (start us, length us, event | category | flops | bytes accessed | tf_op | source)
XLA Modules:
  0.0 377.5 jit_solution(14722390455789144011)
XLA Ops:
  0.7 0.0 copy-start
  0.7 0.6 copy-done
  1.3 0.6 constant_dynamic-slice_fusion.2
  1.9 1.3 constant_dynamic-slice_fusion.1
  3.2 2.5 pad_add_fusion.lens_ref
  5.7 0.7 convert_bitcast_fusion
  6.4 0.6 pad_convert_fusion.vec_ref
  7.0 94.9 %gather.1 = (bf16[8,96,2304]{2,1,0:T(8,128)(2,1)}, bf16[8,96,768]{2,1,0:T(8,128)(2,1)}, bf16[8,96,3072]{2,1,0:T(8,128)(2,1)}, bf16[8,384,768]{2,1,0:T(8,128)(2,1...) custom-call(f32[96,6144]{1,0:T(8,128)} %wide_ref.1, f32[384,768]{1,0:T(8,128)} %down_ref.1, ...), custom_call_target="tpu_custom_call" | custom-call | tf_op jit(solution)/shard_map/gather/pallas_call | solution.py:606
  101.9 0.8 slice_bitcast_fusion
  102.8 0.7 reshape.105.vec_ref
  103.5 0.1 squeeze.6
  103.6 0.1 squeeze.7
  103.6 8.4 %add_convert_fusion = bf16[1024,2304]{1,0:T(8,128)(2,1)} fusion(bf16[1024,768]{1,0:T(8,128)(2,1)} %bitcast.56, bf16[768,2304]{1,0:T(8,128)(2,1)} %bitcast.68, f32[2304]{0:T(1024)S(1)} %pad_maximum_fusion.1), kind=kOutput, calls=%fused_computation | convolution fusion | flops 3628597248 | bytes 9839616 | tf_op jit(solution)/shard_map/dot_general | solution.py:1056
  112.0 18.7 %attn_forward.1 = (bf16[4,256,768]{2,1,0:T(8,128)(2,1)}, bf16[12,512,512]{2,1,0:T(8,128)(2,1)}, bf16[12,2,256,256]{3,2,1,0:T(8,128)(2,1)}) custom-call(s32[3]{0:T(128)} %pad_add_fusion.lens_ref, bf16[4,256,2304]{2,1,0:T(8,128)(2,1)} %bitcast.43, bf16[4,256,2304]{2,1,0:T(8,128)(2,1)} %bitcast.44, bf16[4,256,2304]{2,1,0:T(8,128)(2,1)} %bitcast.45), custom_call_target="tpu_custom_call" | custom-call | tf_op jit(solution)/shard_map/attn_forward/pallas_call | solution.py:70
  130.7 43.0 %middle.1 = (bf16[1024,768]{1,0:T(8,128)(2,1)}, bf16[1024,768]{1,0:T(8,128)(2,1)}, bf16[1024,3072]{1,0:T(8,128)(2,1)}, bf16[1024,768]{1,0:T(8,128)(2,1)}, bf16[1...) custom-call(s32[3]{0:T(128)} %pad_add_fusion.lens_ref, ...), custom_call_target="tpu_custom_call" | custom-call | tf_op jit(solution)/shard_map/middle/pallas_call | solution.py:262
  173.7 0.0 copy-start.4
  173.8 0.0 copy-start.32
  173.8 0.0 copy-start.31
  173.8 17.2 %attn_backward.1 = (bf16[4,256,768]{2,1,0:T(8,128)(2,1)}, bf16[4,256,768]{2,1,0:T(8,128)(2,1)}, bf16[4,256,768]{2,1,0:T(8,128)(2,1)}, f32[8,768]{1,0:T(8,128)}) custom-call(s32[3]{0:T(128)} %pad_add_fusion.lens_ref, bf16[4,256,2304]{2,1,0:T(8,128)(2,1)} %bitcast.46, bf16[4,256,2304]{2,1,0:T(8,128)(2,1)} %bitcast.47, bf16[4,256,2304]{2,1,0:T(8,128)(2,1)} %bitcast.48, ...), custom_call_target="tpu_custom_call" | custom-call | tf_op jit(solution)/shard_map/attn_backward/pallas_call | solution.py:140
  190.9 0.0 copy-done.4
  191.0 0.0 copy-done.32
  191.0 0.0 copy-start.27
  191.0 2.5 convolution_convert_fusion.2
  193.4 0.0 copy-done.31
  193.4 0.7 copy-done.27
  194.2 7.0 %convolution_convert_fusion.1 = bf16[3072,768]{1,0:T(8,128)(2,1)} fusion(bf16[1024,3072]{1,0:T(8,128)(2,1)S(1)} %copy-done.27, bf16[1024,768]{1,0:T(8,128)(2,1)S(1)} %copy-done.31), kind=kOutput, calls=%fused_computation.3 | convolution fusion | flops 4834197504 | bytes 12582912 | tf_op jit(solution)/shard_map/ra,rb->ab/dot_general | solution.py:943
  201.1 0.9 slice.23
  202.0 0.0 copy-done.22
  202.0 0.1 reshape.111
  202.1 0.6 pad.12.refs_4_
  202.8 0.0 copy-done.12
  202.8 0.1 constant_dynamic-update-slice_fusion.2
  202.9 0.0 copy-done.11
  202.9 0.0 copy-start.10
  202.9 0.1 constant_dynamic-update-slice_fusion.1
  203.0 1.4 copy-done.10
  204.5 0.1 constant_dynamic-update-slice_fusion
  204.6 0.6 copy-done.29
  205.1 1.1 copy-done.28
  206.2 4.9 %add_convert_fusion.1 = bf16[1024,768]{1,0:T(8,128)(2,1)} fusion(f32[1024,768]{1,0:T(8,128)S(1)} %copy-done.29, bf16[1024,2304]{1,0:T(8,128)(2,1)S(1)} %bitcast.64, bf16[768,2304]{1,0:T(8,128)(2,1)S(1)} %bitcast.69), kind=kOutput, calls=%fused_computation.4 | convolution fusion | flops 3625451520 | bytes 12976128 | tf_op jit(solution)/shard_map/ra,ba->rb/dot_general | solution.py:947
  211.2 5.4 %bitcast_convert_fusion = bf16[768,2304]{1,0:T(8,128)(2,1)} fusion(bf16[4,256,768]{2,1,0:T(8,128)(2,1)S(1)} %copy-done.9, bf16[4,256,2304]{2,1,0:T(8,128)(2,1)S(1)} %constant_dynamic-update-slice_fusion), kind=kOutput, calls=%fused_computation.1 | convolution fusion | flops 3625648128 | bytes 9830400 | tf_op jit(solution)/shard_map/ra,rb->ab/dot_general | solution.py:943
  216.5 0.0 slice-done
  216.5 7.2 %convolution_convert_fusion = bf16[768,3072]{1,0:T(8,128)(2,1)} fusion(bf16[1024,768]{1,0:T(8,128)(2,1)S(1)} %copy-done.30, bf16[1024,3072]{1,0:T(8,128)(2,1)S(1)} %bitcast.67), kind=kOutput, calls=%fused_computation.2 | convolution fusion | flops 4834197504 | bytes 12582912 | tf_op jit(solution)/shard_map/ra,rb->ab/dot_general | solution.py:943
  223.8 0.0 copy-start.13
  223.8 136.8 %reduce.9 = (bf16[384,768]{1,0:T(8,128)(2,1)}, bf16[96,3072]{1,0:T(8,128)(2,1)}, bf16[96,768]{1,0:T(8,128)(2,1)}, bf16[96,2304]{1,0:T(8,128)(2,1)}, f32[16,128]{...) custom-call(bf16[4,2,384,768]{3,2,1,0:T(8,128)(2,1)} %bitcast.51, ...), custom_call_target="tpu_custom_call" | custom-call | tf_op jit(solution)/shard_map/reduce/pallas_call | solution.py:916
  360.6 1.3 fusion
  361.9 0.6 multiply_add_fusion.6
  362.5 0.0 copy-done.5
  362.5 3.1 fusion.1
  365.7 1.2 multiply_add_fusion.3
  366.9 1.3 copy-done.3
  368.2 0.1 copy-done.19
  368.3 0.1 copy-done.20
  368.4 0.0 copy-done.21
  368.4 3.4 fusion.2
  371.8 0.0 copy-done.8
  371.8 1.8 multiply_add_fusion
  373.6 0.4 copy-done.2
  374.0 0.9 copy.48
  374.9 0.9 copy.49
  375.7 0.0 copy-done.16
  375.8 0.9 copy.50
  376.6 0.9 copy.51
  377.5 0.0 copy-done.1
  (50 shorter events, 0.2 us)
Async XLA Ops:
  0.7 0.7 copy-start
  173.7 17.2 %copy-start.4 = (bf16[4,256,768]{2,1,0:T(8,128)(2,1)S(1)}, bf16[4,256,768]{2,1,0:T(8,128)(2,1)}, u32[]{:S(2)}) copy-start(bf16[4,256,768]{2,1,0:T(8,128)(2,1)} %get-tuple-element.54.o_ref) | copy-start | bytes 4718596
  173.8 17.2 %copy-start.32 = (bf16[1024,768]{1,0:T(8,128)(2,1)S(1)}, bf16[1024,768]{1,0:T(8,128)(2,1)}, u32[]{:S(2)}) copy-start(bf16[1024,768]{1,0:T(8,128)(2,1)} %get-tuple-element.63) | copy-start | bytes 4718596
  173.8 19.7 %copy-start.31 = (bf16[1024,768]{1,0:T(8,128)(2,1)S(1)}, bf16[1024,768]{1,0:T(8,128)(2,1)}, u32[]{:S(2)}) copy-start(bf16[1024,768]{1,0:T(8,128)(2,1)} %get-tuple-element.60) | copy-start | bytes 4718596
  191.0 3.2 copy-start.27
  194.2 7.8 %copy-start.22 = (f32[16,768]{1,0:T(8,128)S(1)}, f32[16,768]{1,0:T(8,128)}, u32[]{:S(2)}) copy-start(f32[16,768]{1,0:T(8,128)} %get-tuple-element.71) | copy-start | bytes 147460
  194.2 8.6 %copy-start.12 = (bf16[4,256,768]{2,1,0:T(8,128)(2,1)S(1)}, bf16[4,256,768]{2,1,0:T(8,128)(2,1)}, u32[]{:S(2)}) copy-start(bf16[4,256,768]{2,1,0:T(8,128)(2,1)} %get-tuple-element.67) | copy-start | bytes 4718596
  201.1 1.7 copy-start.11
  202.8 2.4 copy-start.29
  202.9 1.6 copy-start.10
  202.9 3.3 copy-start.28
  204.5 12.1 %slice-start = ((s8[6291456]{0:T(1024)(128)(4,1)}), s8[4194304]{0:T(1024)(128)(4,1)S(1)}, s32[]{:S(2)}) async-start(s8[6291456]{0:T(1024)(128)(4,1)} %bitcast.66), calls=%async_computation | async-start | bytes 8388608
  206.2 4.9 %copy-start.9 = (bf16[4,256,768]{2,1,0:T(8,128)(2,1)S(1)}, bf16[4,256,768]{2,1,0:T(8,128)(2,1)}, u32[]{:S(2)}) copy-start(bf16[4,256,768]{2,1,0:T(8,128)(2,1)} %get-tuple-element.51) | copy-start | bytes 4718596
  206.2 10.3 %slice-start.1 = ((s8[6291456]{0:T(1024)(128)(4,1)}), s8[2097152]{0:T(1024)(128)(4,1)S(1)}, s32[]{:S(2)}) async-start(s8[6291456]{0:T(1024)(128)(4,1)} %bitcast.66), calls=%async_computation.1 | async-start | bytes 4194304
  211.2 5.4 %copy-start.30 = (bf16[1024,768]{1,0:T(8,128)(2,1)S(1)}, bf16[1024,768]{1,0:T(8,128)(2,1)}, u32[]{:S(2)}) copy-start(bf16[1024,768]{1,0:T(8,128)(2,1)} %get-tuple-element.61) | copy-start | bytes 4718596
  223.7 136.8 %copy-start.24 = (f32[96,12]{0,1:T(8,128)S(1)}, f32[96,12]{0,1:T(8,128)}, u32[]{:S(2)}) copy-start(f32[96,12]{0,1:T(8,128)} %param.23) | copy-start | bytes 13828
  223.7 136.8 %copy-start.26 = (f32[96,12]{0,1:T(8,128)S(1)}, f32[96,12]{0,1:T(8,128)}, u32[]{:S(2)}) copy-start(f32[96,12]{0,1:T(8,128)} %param.26) | copy-start | bytes 13828
  223.7 138.2 %copy-start.25 = (f32[96,12]{0,1:T(8,128)S(1)}, f32[96,12]{0,1:T(8,128)}, u32[]{:S(2)}) copy-start(f32[96,12]{0,1:T(8,128)} %param.29) | copy-start | bytes 13828
  223.8 138.8 %copy-start.5 = (f32[384,768]{1,0:T(8,128)S(1)}, f32[384,768]{1,0:T(8,128)}, u32[]{:S(2)}) copy-start(f32[384,768]{1,0:T(8,128)} %down_ref.1) | copy-start | bytes 3538948
  223.8 138.8 %copy-start.13 = (f32[384,768]{1,0:T(8,128)S(1)}, f32[384,768]{1,0:T(8,128)}, u32[]{:S(2)}) copy-start(f32[384,768]{1,0:T(8,128)} %param.25) | copy-start | bytes 3538948
  361.9 3.8 copy-start.23
  362.5 3.2 copy-start.14
  362.5 4.4 %copy-start.7 = (f32[96,6144]{1,0:T(8,128)S(1)}, f32[96,6144]{1,0:T(8,128)}, u32[]{:S(2)}) copy-start(f32[96,6144]{1,0:T(8,128)} %param.24) | copy-start | bytes 7077892
  365.6 6.1 %copy-start.6 = (f32[384,768]{1,0:T(8,128)}, f32[384,768]{1,0:T(8,128)S(1)}, u32[]{:S(2)}) copy-start(f32[384,768]{1,0:T(8,128)S(1)} %get-tuple-element.132) | copy-start | bytes 3538948
  365.7 2.5 copy-start.3
  365.7 2.6 copy-start.19
  365.7 2.7 copy-start.20
  365.7 2.8 copy-start.21
  368.4 3.4 copy-start.8
  371.8 2.2 copy-start.2
  371.8 2.2 copy-start.18
  371.8 3.1 copy-start.17
  374.0 1.8 copy-start.16
  374.0 2.7 copy-start.15
  374.0 3.5 copy-start.1

commit v4 on v3

--- a/solution.py
+++ b/solution.py
@@ -39,29 +39,36 @@
 SEQS = ((0, 128, LONG_L, 0), (128, 64, SHORT_L, 1), (192, 64, SHORT_L, 2))
 
 
+def attend(q, k, v, limit, keep_probs):
+    length = q.shape[0]
+    v_t = jnp.transpose(v)
+    head_lane = lax.broadcasted_iota(jnp.int32, (length, PAIR), 1) // HEAD_DIM
+    live = lax.broadcasted_iota(jnp.int32, (length, length), 0) < limit
+    parts = []
+    for h in range(2):
+        k_h = jnp.where(head_lane == h, k, jnp.zeros_like(k))
+        scores = jnp.where(live, dot_nt(k_h, q) * score_scale, mask_fill)
+        top = jnp.max(scores, axis=0, keepdims=True)
+        exponent = jnp.exp(scores - top)
+        total = jnp.sum(exponent, axis=0, keepdims=True)
+        probs = (exponent * (1.0 / total)).astype(bf16)
+        keep_probs(h, probs)
+        parts.append(dot_nn(v_t[h * HEAD_DIM : (h + 1) * HEAD_DIM], probs))
+    return jnp.transpose(jnp.concatenate(parts, axis=0)).astype(bf16)
+
+
 def attn_forward_kernel(lens_ref, q_ref, k_ref, v_ref, o_ref, long_ref, short_ref):
     for first, rows, length, index in SEQS:
-        q = q_ref[:, first : first + rows, :].reshape(length, PAIR)
-        k = k_ref[:, first : first + rows, :].reshape(length, PAIR)
-        v = v_ref[:, first : first + rows, :].reshape(length, PAIR)
-        v_t = jnp.transpose(v)
-        head_lane = lax.broadcasted_iota(jnp.int32, (length, PAIR), 1) // HEAD_DIM
-        live = lax.broadcasted_iota(jnp.int32, (length, length), 0) < lens_ref[index]
-        parts = []
-        for h in range(2):
-            k_h = jnp.where(head_lane == h, k, jnp.zeros_like(k))
-            scores = jnp.where(live, dot_nt(k_h, q) * score_scale, mask_fill)
-            top = jnp.max(scores, axis=0, keepdims=True)
-            exponent = jnp.exp(scores - top)
-            total = jnp.sum(exponent, axis=0, keepdims=True)
-            probs = (exponent * (1.0 / total)).astype(bf16)
+        q, k, v = [r[:, first : first + rows, :].reshape(length, PAIR) for r in (q_ref, k_ref, v_ref)]
+
+        def keep_probs(h, probs, index=index):
             if index == 0:
                 long_ref[h] = probs
             else:
                 short_ref[h, index - 1] = probs
-            parts.append(dot_nn(v_t[h * HEAD_DIM : (h + 1) * HEAD_DIM], probs))
-        o = jnp.transpose(jnp.concatenate(parts, axis=0))
-        o_ref[:, first : first + rows, :] = o.astype(bf16).reshape(4, rows, PAIR)
+
+        o = attend(q, k, v, lens_ref[index], keep_probs)
+        o_ref[:, first : first + rows, :] = o.reshape(4, rows, PAIR)
 
 
 def attn_forward(lens, qkv):
@@ -327,8 +334,8 @@
 
 
 class Part:
-    def __init__(self, own, out, sems):
-        self.own, self.out = own, out
+    def __init__(self, own, out, sems, direct=False):
+        self.own, self.out, self.direct = own, out, direct
         self.z_send, self.z_recv, self.x_send, self.x_recv, self.y_send, self.y_recv, self.c_send, self.c_recv = sems
         self.dp, self.s, self.z, self.x, self.y, self.c = place()
         self.rows, cols = own.shape
@@ -359,12 +366,13 @@
         return remote(self.source(zs, own), dst, self.z_send.at[zs, 1], self.z_recv.at[zs], (self.dp - 2, self.s))
 
     def across(self, zs, own=False):
-        dst = self.block(zs, self.x, self.c, self.y)
+        q = None if self.direct else self.y
+        dst = self.block(zs, self.x, self.c, q)
         device = (self.z * 2 + 1 - self.x, self.s)
-        return remote(self.source(zs, own, self.y), dst, self.x_send.at[zs], self.x_recv.at[zs], device)
+        return remote(self.source(zs, own, q), dst, self.x_send.at[zs], self.x_recv.at[zs], device)
 
     def across_in(self, zs):
-        ref = self.block(zs, 1 - self.x, self.c, self.y)
+        ref = self.block(zs, 1 - self.x, self.c, None if self.direct else self.y)
         return remote(ref, ref, self.x_send.at[zs], self.x_recv.at[zs], (self.dp, self.s))
 
     def over(self, zs):
@@ -379,7 +387,8 @@
         if kind == 0:
             ref = self.block(zs, self.x, core)
         else:
-            ref = self.block(zs, 1 - self.x, core, self.y if kind == 1 else 1 - self.y)
+            q = self.y if kind == 1 else 1 - self.y
+            ref = self.block(zs, 1 - self.x, core, None if self.direct else q)
         j = kind * Z_CHIPS + zs
         return remote(ref, ref, self.c_send.at[j], self.c_recv.at[j], (self.dp, self.s + 1 - 2 * self.c))
 
@@ -438,11 +447,12 @@
 
             def pass_x(zs):
                 self.across_in(zs).wait_recv()
-                self.over(zs).start()
+                if not self.direct:
+                    self.over(zs).start()
                 self.share(1, zs, self.c).start()
 
             self.each(k - 1, pass_x)
-        if 2 <= k <= Z_CHIPS + 1:
+        if 2 <= k <= Z_CHIPS + 1 and not self.direct:
 
             def pass_y(zs):
                 self.over_in(zs).wait_recv()
@@ -453,7 +463,7 @@
     stages = Z_CHIPS + 2
 
     def finish(self):
-        for kind in range(3):
+        for kind in range(2 if self.direct else 3):
             for k in range(1 if kind == 0 else 0, Z_CHIPS):
                 self.each(k, lambda zs, kind=kind: self.share(kind, zs, 1 - self.c).wait_recv())
 
@@ -469,8 +479,9 @@
                 self.down(self.z + k, k == 0).wait_send()
 
             self.each(k, lambda zs, k=k: self.across(zs, k == 0).wait_send())
-            self.each(k, lambda zs: self.over(zs).wait_send())
-            for kind in range(3):
+            if not self.direct:
+                self.each(k, lambda zs: self.over(zs).wait_send())
+            for kind in range(2 if self.direct else 3):
                 if kind > 0 or k > 0:
                     self.each(k, lambda zs, kind=kind: self.share(kind, zs, self.c).wait_send())
 
@@ -515,7 +526,8 @@
                 copy.wait_send()
 
 
-def gather_kernel(
+def forward_kernel(
+    lens_ref,
     wide_ref,
     down_ref,
     vec_ref,
@@ -523,15 +535,26 @@
     short_in,
     long_cot,
     short_cot,
-    qkv_out,
+    qkv_w_out,
     wo_out,
     w1_out,
     w2_out,
     vec_out,
     tok_out,
     cot_out,
+    qkv_out,
+    att_out,
+    long_probs,
+    short_probs,
     own_wide,
     own_down,
+    w_s,
+    x_s,
+    qkv_s,
+    vec_s,
+    bias_s,
+    long_s,
+    short_s,
     z_send,
     z_recv,
     x_send,
@@ -545,50 +568,144 @@
     t_send,
     t_recv,
     local,
+    p_sem,
 ):
     dp, s, z, x, y, c = place()
     greet()
-    tokens = Tokens(long_in, short_in, tok_out, t_send.at[0], t_recv.at[0], local.at[0])
+    tokens = Tokens(long_in, short_in, x_s, t_send.at[0], t_recv.at[0], local.at[0])
     cots = Tokens(long_cot, short_cot, cot_out, t_send.at[1], t_recv.at[1], local.at[1])
     tokens.start()
     own_wide[...] = wide_ref[...].astype(bf16)
-    own_down[...] = down_ref[...].astype(bf16)
 
     def vec_copy(k, source, target):
-        return remote(vec_ref, vec_out.at[source], v_send.at[k], v_recv.at[k], (target, s))
+        return remote(vec_ref, vec_s.at[source], v_send.at[k], v_recv.at[k], (target, s))
 
     sems = lambda i: [
         r.at[i] for r in (z_send, z_recv, x_send, x_recv, y_send, y_recv, c_send, c_recv)
     ]
     parts = [
-        Part(own_wide.at[:, pl.ds(0, 3 * D)], qkv_out, sems(0)),
+        Part(own_wide.at[:, pl.ds(0, 3 * D)], w_s, sems(0)),
         Part(own_wide.at[:, pl.ds(3 * D, D)], wo_out, sems(1)),
         Part(own_wide.at[:, pl.ds(4 * D, FF)], w1_out, sems(2)),
-        Part(own_down, w2_out, sems(3)),
+        Part(own_down, w2_out, sems(3), direct=True),
     ]
-    parts[0].stage(0)
+    first, others = parts[0], parts[1:]
+    first.stage(0)
     for k in range(1, 8):
         vec_copy(k, dp, (dp + k) % 8).start()
+    own_down[...] = down_ref[...].astype(bf16)
     own_copies = [
         pltpu.make_async_copy(part.own, part.out.at[dp], local.at[2, i]) for i, part in enumerate(parts)
     ]
-    own_copies.append(pltpu.make_async_copy(vec_ref, vec_out.at[dp], local.at[2, 4]))
+    own_copies.append(pltpu.make_async_copy(vec_ref, vec_s.at[dp], local.at[2, 4]))
     for copy in own_copies:
         copy.start()
-    for t in range(1, Part.stages + len(parts) - 1):
-        for i, part in enumerate(parts):
-            if 0 <= t - i < Part.stages:
-                part.stage(t - i)
-        if t == 4:
-            cots.start()
+    first.stage(1)
+    parts[1].stage(0)
+    first.stage(2)
+    parts[2].stage(0)
+    first.stage(3)
+    first.stage(4)
+    parts[3].stage(0)
+    first.stage(5)
+    cots.start()
     for copy in own_copies:
         copy.wait()
-    for part in parts:
-        part.finish()
-    tokens.finish()
-    cots.finish()
     for k in range(1, 8):
         vec_copy(k, (dp + 8 - k) % 8, dp).wait_recv()
+    vec = vec_s[0].astype(f32)
+    for d in range(1, 8):
+        vec = vec + vec_s[d].astype(f32)
+    vec_out[...] = vec
+    bias_s[:, 0:D] = jnp.broadcast_to(vec[0:1, :], (8, D))
+    bias_s[:, D : 2 * D] = jnp.zeros((8, D), f32)
+    bias_s[:, 2 * D : 3 * D] = jnp.broadcast_to(vec[1:2, :], (8, D))
+    tokens.finish()
+    first.finish()
+    keep_tokens = pltpu.make_async_copy(x_s, tok_out, local.at[3, 0])
+    keep_weights = pltpu.make_async_copy(w_s, qkv_w_out, local.at[3, 1])
+    keep_tokens.start()
+    keep_weights.start()
+
+    def during(i, plan):
+        for when, jobs in plan:
+
+            @pl.when(i == when)
+            def _():
+                for index, stage in jobs:
+                    parts[index].stage(stage)
+
+    def project(j, carry):
+        during(j, ((2, ((1, 1),)), (4, ((2, 1),)), (6, ((1, 2),)), (8, ((3, 1),))))
+        cols = pl.ds(pl.multiple_of(j * 256, 256), 256)
+        w = w_s[:, :, cols].reshape(D, 256)
+        rows = x_s[...].reshape(1024, D)
+        qkv_s[:, :, cols] = (dot_nn(rows, w) + bias_s[0:1, cols]).astype(bf16).reshape(4, 256, 256)
+        return carry
+
+    lax.fori_loop(0, 3 * D // 256, project, 0)
+    keep_qkv = pltpu.make_async_copy(qkv_s, qkv_out, local.at[3, 2])
+    keep_qkv.start()
+    pairs = D // PAIR
+
+    def keep_probs_copies(i, slot):
+        return (
+            pltpu.make_async_copy(long_s.at[slot], long_probs.at[pl.ds(2 * i, 2)], p_sem.at[0, slot]),
+            pltpu.make_async_copy(short_s.at[slot], short_probs.at[pl.ds(2 * i, 2)], p_sem.at[1, slot]),
+        )
+
+    def attention(i, carry):
+        during(
+            i,
+            (
+                (0, ((2, 2), (1, 3))),
+                (1, ((3, 2), (1, 4))),
+                (2, ((2, 3), (1, 5))),
+                (3, ((3, 3),)),
+                (4, ((2, 4),)),
+                (5, ((3, 4), (2, 5))),
+            ),
+        )
+        slot = i % 2
+
+        @pl.when(i >= 2)
+        def _():
+            for copy in keep_probs_copies(i - 2, slot):
+                copy.wait()
+
+        for first_row, rows, length, index in SEQS:
+            q, k, v = [
+                qkv_s[:, first_row : first_row + rows, pl.ds(pl.multiple_of(base + i * PAIR, PAIR), PAIR)].reshape(
+                    length, PAIR
+                )
+                for base in (0, D, 2 * D)
+            ]
+
+            def keep_probs(h, probs, index=index):
+                if index == 0:
+                    long_s[slot, h] = probs
+                else:
+                    short_s[slot, h, index - 1] = probs
+
+            o = attend(q, k, v, lens_ref[index], keep_probs)
+            att_out[:, first_row : first_row + rows, pl.ds(pl.multiple_of(i * PAIR, PAIR), PAIR)] = o.reshape(
+                4, rows, PAIR
+            )
+        for copy in keep_probs_copies(i, slot):
+            copy.start()
+        return carry
+
+    lax.fori_loop(0, pairs, attention, 0)
+    parts[3].stage(5)
+    for part in others:
+        part.finish()
+    cots.finish()
+    keep_tokens.wait()
+    keep_weights.wait()
+    keep_qkv.wait()
+    for i in (pairs - 2, pairs - 1):
+        for copy in keep_probs_copies(i, i % 2):
+            copy.wait()
     for k in range(1, 8):
         vec_copy(k, dp, (dp + k) % 8).wait_send()
     for part in parts:
@@ -597,28 +714,41 @@
     cots.settle()
 
 
-def gather(wide_master, down_master, vec_block, long_in, short_in, long_cot, short_cot):
+def forward(lens, wide_master, down_master, vec_block, long_in, short_in, long_cot, short_cot):
     any_spec = pl.BlockSpec(memory_space=pl.ANY)
     vmem = pl.BlockSpec(memory_space=pltpu.VMEM)
+    smem = pl.BlockSpec(memory_space=pltpu.SMEM)
     shape = jax.ShapeDtypeStruct
     rows, down_rows = wide_master.shape[0], down_master.shape[0]
     dma = pltpu.SemaphoreType.DMA
+    heads = D // HEAD_DIM
     return pl.pallas_call(
-        gather_kernel,
-        in_specs=[vmem, vmem, vmem] + [any_spec] * 4,
-        out_specs=[any_spec] * 7,
+        forward_kernel,
+        in_specs=[smem, vmem, vmem, vmem] + [any_spec] * 4,
+        out_specs=[any_spec] * 4 + [vmem] + [any_spec] * 3 + [vmem] + [any_spec] * 2,
         out_shape=[
             shape((8, rows, 3 * D), bf16),
             shape((8, rows, D), bf16),
             shape((8, rows, FF), bf16),
             shape((8, down_rows, D), bf16),
-            shape((8, 16, 128), f32),
+            shape((16, D), f32),
             shape((4, 256, D), bf16),
             shape((4, 256, D), bf16),
+            shape((4, 256, 3 * D), bf16),
+            shape((4, 256, D), bf16),
+            shape((heads, LONG_L, LONG_L), bf16),
+            shape((heads, 2, SHORT_L, SHORT_L), bf16),
         ],
         scratch_shapes=[
             pltpu.VMEM((rows, 4 * D + FF), bf16),
             pltpu.VMEM((down_rows, D), bf16),
+            pltpu.VMEM((8, rows, 3 * D), bf16),
+            pltpu.VMEM((4, 256, D), bf16),
+            pltpu.VMEM((4, 256, 3 * D), bf16),
+            pltpu.VMEM((8, 16, D), bf16),
+            pltpu.VMEM((8, 3 * D), f32),
+            pltpu.VMEM((2, 2, LONG_L, LONG_L), bf16),
+            pltpu.VMEM((2, 2, 2, SHORT_L, SHORT_L), bf16),
             dma((4, 4, 2)),
             dma((4, 4)),
             dma((4, 4)),
@@ -631,13 +761,14 @@
             dma((8,)),
             dma((2, 4, 3)),
             dma((2, 4, 3)),
-            dma((3, 5)),
+            dma((4, 5)),
+            dma((2, 2)),
         ],
         compiler_params=pltpu.CompilerParams(
             vmem_limit_bytes=VMEM_BYTES, collective_id=0, has_side_effects=True
         ),
-        name="gather",
-    )(wide_master, down_master, vec_block, long_in, short_in, long_cot, short_cot)
+        name="forward",
+    )(lens, wide_master, down_master, vec_block, long_in, short_in, long_cot, short_cot)
 
 
 class Grad:
@@ -1033,13 +1164,16 @@
     s = lax.axis_index("seq")
     lens = jnp.stack([long_len[s // 2, 0, s % 2], short_len[0, 0, s], short_len[1, 0, s]])
     if lax.axis_size("dp") == 8:
-        vec_own = jnp.transpose(vector_master).astype(bf16).astype(f32)
-        vec_block = jnp.pad(vec_own, ((0, 4), (0, 128 - vec_own.shape[1])))
-        w_qkv, w_o, w_1, w_2, vec_blocks, tokens, cotangent = gather(
-            wide_master, down_master, vec_block, long_in, short_in, long_cot, short_cot
+        own = vector_master.shape[0]
+        vec_own = jnp.pad(jnp.transpose(vector_master).astype(bf16), ((0, 4), (0, 0)))
+        vec_block = lax.dynamic_update_slice(
+            jnp.zeros((16, D), bf16), vec_own, (0, lax.axis_index("dp") * own)
+        )
+        w_qkv, w_o, w_1, w_2, vec, tokens, cotangent, qkv, attended, long_probs, short_probs = forward(
+            lens, wide_master, down_master, vec_block, long_in, short_in, long_cot, short_cot
         )
         w_qkv, w_o, w_1, w_2 = [w.reshape(-1, w.shape[2]) for w in (w_qkv, w_o, w_1, w_2)]
-        vec = jnp.transpose(vec_blocks[:, :12, : vec_own.shape[1]], (1, 0, 2)).reshape(12, D)
+        rows = tokens.reshape(1024, D)
     else:
         tokens = exchange(spread_rows(long_in, short_in))
         cotangent = exchange(spread_rows(long_cot, short_cot))
@@ -1050,12 +1184,12 @@
         w_qkv = wide_w[:, : 3 * D]
         w_o = wide_w[:, 3 * D : 4 * D]
         w_1 = wide_w[:, 4 * D :]
-
-    rows = tokens.reshape(1024, D)
-    proj_bias = jnp.concatenate([vec[0], jnp.zeros((D,), f32), vec[1]])
-    qkv = (jnp.dot(rows, w_qkv, preferred_element_type=f32) + proj_bias).astype(bf16)
-    qkv = qkv.reshape(4, 256, 3 * D)
-    attended, long_probs, short_probs = attn_forward(lens, qkv)
+        rows = tokens.reshape(1024, D)
+        proj_bias = jnp.concatenate([vec[0], jnp.zeros((D,), f32), vec[1]])
+        qkv = (jnp.dot(rows, w_qkv, preferred_element_type=f32) + proj_bias).astype(bf16)
+        qkv = qkv.reshape(4, 256, 3 * D)
+        attended, long_probs, short_probs = attn_forward(lens, qkv)
+
     flat_attended = attended.reshape(1024, D)
     out, y1b, act, dfb, dub, dab, dob, dh, sums = middle(
         lens, flat_attended, rows, cotangent.reshape(1024, D), w_o, w_1, w_2, vec

time: 379 us -> 349 us (0.921)
  Pallas kernels: 311 us -> 291 us
  matrix products: 35.3 us -> 26.6 us
    pallas_call x2 -> x1, Pallas kernels: 114 us -> 92.9 us  [forward(): pl.pallas_call(forward_kernel, in_specs=[smem, vmem, vmem, vmem] + [any_s...]
    dot_general x1 -> x0, matrix products: 8.4 us -> none  [body(): jnp.dot(rows, w_qkv, preferred_element_type=f32) + proj_bias]
    unnamed x76 -> x78, local copies, waits for them, and re-layouts: 10.2 us -> 10.8 us
where the time goes in v4:
time: 349 us; the launch traced here: 348 us
  Pallas kernels  291 us (83%)
  matrix products  26.6 us (8%)
  local copies, waits for them, and re-layouts  14.6 us (4%)
  other arithmetic  14.6 us (4%)
    pallas_call x1, Pallas kernels, reduce_all(): pl.pallas_call(lambda *refs: reduce_kernel(count, *refs), in_specs=[any_s...  138 us
    pallas_call x1, Pallas kernels, forward(): pl.pallas_call(forward_kernel, in_specs=[smem, vmem, vmem, vmem] + [any_s...  92.9 us
    pallas_call x1, Pallas kernels, middle(): pl.pallas_call(middle_kernel, grid=(n // rows,), in_specs=[pl.BlockSpec(m...  43.3 us
    dot_general x4, matrix products, transpose_dot(): return jnp.einsum('ra,rb->ab', left, right, preferred_element_type=f32)  21.7 us
    pallas_call x1, Pallas kernels, attn_backward(): pl.pallas_call(attn_backward_kernel, grid=(pairs,), in_specs=[pl.BlockSpe...  16.9 us
    unnamed x78, local copies, waits for them, and re-layouts  10.8 us
    convert_element_type x3, other arithmetic, update(): return (velocity, averaged, updated, updated.astype(jnp.bfloat16))  7.78 us

profile of v4, /device:TPU:0, one launch (start us, length us, event | category | flops | bytes accessed | tf_op | source)
XLA Modules:
  0.0 347.9 jit_solution(7734887102576334272)
XLA Ops:
  0.7 0.0 copy-start
  0.7 0.6 copy-done
  1.3 0.6 constant_dynamic-slice_fusion.2
  1.9 1.3 constant_dynamic-slice_fusion.1
  3.2 2.5 pad_add_fusion.lens_ref
  5.7 0.7 convert_bitcast_fusion
  6.4 0.2 dynamic_update_slice.3.vec_ref
  6.6 0.0 copy-start.22
  6.6 0.6 copy-done.22
  7.2 92.9 %forward.1 = (bf16[8,96,2304]{2,1,0:T(8,128)(2,1)}, bf16[8,96,768]{2,1,0:T(8,128)(2,1)}, bf16[8,96,3072]{2,1,0:T(8,128)(2,1)}, bf16[8,384,768]{2,1,0:T(8,128)(2,...) custom-call(s32[3]{0:T(128)} %pad_add_fusion.lens_ref, ...), custom_call_target="tpu_custom_call" | custom-call | tf_op jit(solution)/shard_map/forward/pallas_call | solution.py:725
  100.2 43.3 %middle.1 = (bf16[1024,768]{1,0:T(8,128)(2,1)}, bf16[1024,768]{1,0:T(8,128)(2,1)}, bf16[1024,3072]{1,0:T(8,128)(2,1)}, bf16[1024,768]{1,0:T(8,128)(2,1)}, bf16[1...) custom-call(s32[3]{0:T(128)} %pad_add_fusion.lens_ref, ...), custom_call_target="tpu_custom_call" | custom-call | tf_op jit(solution)/shard_map/middle/pallas_call | solution.py:269
  143.4 0.0 copy-start.4
  143.4 0.0 copy-start.33
  143.5 0.0 copy-start.32
  143.5 16.9 %attn_backward.1 = (bf16[4,256,768]{2,1,0:T(8,128)(2,1)}, bf16[4,256,768]{2,1,0:T(8,128)(2,1)}, bf16[4,256,768]{2,1,0:T(8,128)(2,1)}, f32[8,768]{1,0:T(8,128)}) custom-call(s32[3]{0:T(128)} %pad_add_fusion.lens_ref, bf16[4,256,2304]{2,1,0:T(8,128)(2,1)} %get-tuple-element.64.q_ref.k_ref.v_ref, bf16[4,256,2304]{2,1,0:T(8,128)(2,1)} %get-tuple-element.64.q_ref.k_ref.v_ref, ...), custom_call_target="tpu_custom_call" | custom-call | tf_op jit(solution)/shard_map/attn_backward/pallas_call | solution.py:147
  160.4 0.0 copy-done.4
  160.4 0.0 copy-done.33
  160.4 0.0 copy-start.28
  160.4 2.5 convolution_convert_fusion.2
  162.9 0.0 copy-done.32
  162.9 0.7 copy-done.28
  163.6 6.9 %convolution_convert_fusion.1 = bf16[3072,768]{1,0:T(8,128)(2,1)} fusion(bf16[1024,3072]{1,0:T(8,128)(2,1)S(1)} %copy-done.28, bf16[1024,768]{1,0:T(8,128)(2,1)S(1)} %copy-done.32), kind=kOutput, calls=%fused_computation.2 | convolution fusion | flops 4834197504 | bytes 12582912 | tf_op jit(solution)/shard_map/ra,rb->ab/dot_general | solution.py:1074
  170.5 0.9 slice.9
  171.4 0.0 copy-done.23
  171.4 0.1 reshape.97
  171.5 0.6 pad.9.refs_4_
  172.1 0.0 copy-done.12
  172.1 0.1 constant_dynamic-update-slice_fusion.2
  172.3 0.0 copy-done.11
  172.3 0.0 copy-start.10
  172.3 0.0 copy-start.29
  172.3 0.1 constant_dynamic-update-slice_fusion.1
  172.4 1.4 copy-done.10
  173.8 0.1 constant_dynamic-update-slice_fusion
  173.9 0.6 copy-done.30
  174.5 1.1 copy-done.29
  175.6 4.9 %add_convert_fusion = bf16[1024,768]{1,0:T(8,128)(2,1)} fusion(f32[1024,768]{1,0:T(8,128)S(1)} %copy-done.30, bf16[1024,2304]{1,0:T(8,128)(2,1)S(1)} %bitcast.52, bf16[768,2304]{1,0:T(8,128)(2,1)S(1)} %bitcast.56), kind=kOutput, calls=%fused_computation.3 | convolution fusion | flops 3625451520 | bytes 12976128 | tf_op jit(solution)/shard_map/ra,ba->rb/dot_general | solution.py:1078
  180.5 0.0 copy-done.9
  180.5 5.4 %bitcast_convert_fusion = bf16[768,2304]{1,0:T(8,128)(2,1)} fusion(bf16[4,256,768]{2,1,0:T(8,128)(2,1)S(1)} %copy-done.9, bf16[4,256,2304]{2,1,0:T(8,128)(2,1)S(1)} %constant_dynamic-update-slice_fusion), kind=kOutput, calls=%fused_computation | convolution fusion | flops 3625648128 | bytes 9830400 | tf_op jit(solution)/shard_map/ra,rb->ab/dot_general | solution.py:1074
  185.9 0.0 slice-done
  185.9 0.0 slice-done.1
  186.0 7.0 %convolution_convert_fusion = bf16[768,3072]{1,0:T(8,128)(2,1)} fusion(bf16[1024,768]{1,0:T(8,128)(2,1)S(1)} %copy-done.31, bf16[1024,3072]{1,0:T(8,128)(2,1)S(1)} %bitcast.55), kind=kOutput, calls=%fused_computation.1 | convolution fusion | flops 4834197504 | bytes 12582912 | tf_op jit(solution)/shard_map/ra,rb->ab/dot_general | solution.py:1074
  192.9 0.0 copy-start.13
  192.9 138.0 %reduce.1 = (bf16[384,768]{1,0:T(8,128)(2,1)}, bf16[96,3072]{1,0:T(8,128)(2,1)}, bf16[96,768]{1,0:T(8,128)(2,1)}, bf16[96,2304]{1,0:T(8,128)(2,1)}, f32[16,128]{...) custom-call(bf16[4,2,384,768]{3,2,1,0:T(8,128)(2,1)} %bitcast.40, ...), custom_call_target="tpu_custom_call" | custom-call | tf_op jit(solution)/shard_map/reduce/pallas_call | solution.py:1047
  330.9 1.3 fusion
  332.3 0.6 multiply_add_fusion.6
  332.9 0.0 copy-done.6
  332.9 3.1 fusion.1
  336.0 0.0 copy-done.24
  336.0 1.2 multiply_add_fusion.3
  337.2 1.3 copy-done.3
  338.5 0.1 copy-done.19
  338.6 0.1 copy-done.20
  338.8 0.0 copy-done.21
  338.8 3.4 fusion.2
  342.1 0.0 copy-done.5
  342.2 1.8 multiply_add_fusion
  343.9 0.4 copy-done.2
  344.3 0.9 copy.47
  345.2 0.0 copy-done.17
  345.2 0.9 copy.48
  346.1 0.9 copy.49
  347.0 0.0 copy-done.15
  347.0 0.9 copy.50
  (44 shorter events, 0.1 us)
Async XLA Ops:
  0.7 0.7 copy-start
  6.6 0.6 copy-start.22
  143.4 17.0 %copy-start.4 = (bf16[4,256,768]{2,1,0:T(8,128)(2,1)S(1)}, bf16[4,256,768]{2,1,0:T(8,128)(2,1)}, u32[]{:S(2)}) copy-start(bf16[4,256,768]{2,1,0:T(8,128)(2,1)} %get-tuple-element.52.o_ref) | copy-start | bytes 4718596
  143.4 17.0 %copy-start.33 = (bf16[1024,768]{1,0:T(8,128)(2,1)S(1)}, bf16[1024,768]{1,0:T(8,128)(2,1)}, u32[]{:S(2)}) copy-start(bf16[1024,768]{1,0:T(8,128)(2,1)} %get-tuple-element.63) | copy-start | bytes 4718596
  143.5 19.4 %copy-start.32 = (bf16[1024,768]{1,0:T(8,128)(2,1)S(1)}, bf16[1024,768]{1,0:T(8,128)(2,1)}, u32[]{:S(2)}) copy-start(bf16[1024,768]{1,0:T(8,128)(2,1)} %get-tuple-element.60) | copy-start | bytes 4718596
  160.4 3.2 copy-start.28
  163.6 7.7 %copy-start.23 = (f32[16,768]{1,0:T(8,128)S(1)}, f32[16,768]{1,0:T(8,128)}, u32[]{:S(2)}) copy-start(f32[16,768]{1,0:T(8,128)} %get-tuple-element.72) | copy-start | bytes 147460
  163.6 8.5 %copy-start.12 = (bf16[4,256,768]{2,1,0:T(8,128)(2,1)S(1)}, bf16[4,256,768]{2,1,0:T(8,128)(2,1)}, u32[]{:S(2)}) copy-start(bf16[4,256,768]{2,1,0:T(8,128)(2,1)} %get-tuple-element.68) | copy-start | bytes 4718596
  170.5 1.7 copy-start.11
  172.1 2.4 copy-start.30
  172.3 1.6 copy-start.10
  172.3 3.3 copy-start.29
  173.8 12.1 %slice-start = ((s8[6291456]{0:T(1024)(128)(4,1)}), s8[4194304]{0:T(1024)(128)(4,1)S(1)}, s32[]{:S(2)}) async-start(s8[6291456]{0:T(1024)(128)(4,1)} %bitcast.54), calls=%async_computation | async-start | bytes 8388608
  175.6 4.9 %copy-start.9 = (bf16[4,256,768]{2,1,0:T(8,128)(2,1)S(1)}, bf16[4,256,768]{2,1,0:T(8,128)(2,1)}, u32[]{:S(2)}) copy-start(bf16[4,256,768]{2,1,0:T(8,128)(2,1)} %get-tuple-element.53) | copy-start | bytes 4718596
  175.6 10.4 %slice-start.1 = ((s8[6291456]{0:T(1024)(128)(4,1)}), s8[2097152]{0:T(1024)(128)(4,1)S(1)}, s32[]{:S(2)}) async-start(s8[6291456]{0:T(1024)(128)(4,1)} %bitcast.54), calls=%async_computation.1 | async-start | bytes 4194304
  180.5 5.4 %copy-start.31 = (bf16[1024,768]{1,0:T(8,128)(2,1)S(1)}, bf16[1024,768]{1,0:T(8,128)(2,1)}, u32[]{:S(2)}) copy-start(bf16[1024,768]{1,0:T(8,128)(2,1)} %get-tuple-element.61) | copy-start | bytes 4718596
  192.9 138.0 %copy-start.25 = (f32[96,12]{0,1:T(8,128)S(1)}, f32[96,12]{0,1:T(8,128)}, u32[]{:S(2)}) copy-start(f32[96,12]{0,1:T(8,128)} %param.23) | copy-start | bytes 13828
  192.9 138.0 %copy-start.27 = (f32[96,12]{0,1:T(8,128)S(1)}, f32[96,12]{0,1:T(8,128)}, u32[]{:S(2)}) copy-start(f32[96,12]{0,1:T(8,128)} %param.26) | copy-start | bytes 13828
  192.9 139.3 %copy-start.26 = (f32[96,12]{0,1:T(8,128)S(1)}, f32[96,12]{0,1:T(8,128)}, u32[]{:S(2)}) copy-start(f32[96,12]{0,1:T(8,128)} %param.29) | copy-start | bytes 13828
  192.9 139.9 %copy-start.6 = (f32[384,768]{1,0:T(8,128)S(1)}, f32[384,768]{1,0:T(8,128)}, u32[]{:S(2)}) copy-start(f32[384,768]{1,0:T(8,128)} %down_ref.1) | copy-start | bytes 3538948
  192.9 139.9 %copy-start.13 = (f32[384,768]{1,0:T(8,128)S(1)}, f32[384,768]{1,0:T(8,128)}, u32[]{:S(2)}) copy-start(f32[384,768]{1,0:T(8,128)} %param.25) | copy-start | bytes 3538948
  332.2 3.7 %copy-start.24 = (f32[96,12]{0,1:T(8,128)}, f32[96,12]{0,1:T(8,128)S(1)}, u32[]{:S(2)}) copy-start(f32[96,12]{0,1:T(8,128)S(1)} %get-tuple-element.133) | copy-start | bytes 13828
  332.9 3.2 copy-start.14
  332.9 4.4 %copy-start.7 = (f32[96,6144]{1,0:T(8,128)S(1)}, f32[96,6144]{1,0:T(8,128)}, u32[]{:S(2)}) copy-start(f32[96,6144]{1,0:T(8,128)} %param.24) | copy-start | bytes 7077892
  336.0 6.1 %copy-start.5 = (f32[384,768]{1,0:T(8,128)}, f32[384,768]{1,0:T(8,128)S(1)}, u32[]{:S(2)}) copy-start(f32[384,768]{1,0:T(8,128)S(1)} %get-tuple-element.132) | copy-start | bytes 3538948
  336.0 2.5 copy-start.3
  336.0 2.6 copy-start.19
  336.0 2.7 copy-start.20
  336.0 2.8 copy-start.21
  338.8 3.4 copy-start.8
  342.1 2.2 copy-start.2
  342.1 2.2 copy-start.18
  342.1 3.1 copy-start.17
  344.3 1.8 copy-start.16
  344.3 2.7 copy-start.15
  344.3 3.5 %copy-start.1 = (s32[2,1,2]{2,1,0:T(1,128)S(1)}, s32[2,1,2]{2,1,0:T(1,128)}, u32[]{:S(2)}) copy-start(s32[2,1,2]{2,1,0:T(1,128)} %param.20) | copy-start | bytes 52

commit v5 on v4

--- a/solution.py
+++ b/solution.py
@@ -11,7 +11,7 @@
 PAIR = 128
 LONG_L = 512
 SHORT_L = 256
-VMEM_BYTES = 56 * 1024 * 1024
+VMEM_BYTES = 62 * 1024 * 1024
 
 norm_eps = 1e-12
 mask_fill = -10000.0
@@ -98,44 +98,42 @@
     )(lens, qkv, qkv, qkv)
 
 
+def attend_back(q, k, v, do, o, limit, kept_probs):
+    length = q.shape[0]
+    k_t = jnp.transpose(k)
+    inner = jnp.transpose(do.astype(f32) * o.astype(f32))
+    head_lane = lax.broadcasted_iota(jnp.int32, (length, PAIR), 1) // HEAD_DIM
+    live = lax.broadcasted_iota(jnp.int32, (length, length), 0) < limit
+    dq_parts = []
+    dk = jnp.zeros((length, PAIR), f32)
+    dv = jnp.zeros((length, PAIR), f32)
+    for h in range(2):
+        keep = head_lane == h
+        v_h, do_h, q_h = [jnp.where(keep, m, jnp.zeros_like(m)) for m in (v, do, q)]
+        probs = kept_probs(h)
+        delta = jnp.sum(inner[h * HEAD_DIM : (h + 1) * HEAD_DIM], axis=0, keepdims=True)
+        d_probs = dot_nt(v_h, do)
+        d_scores = jnp.where(live, probs.astype(f32) * (d_probs - delta), 0.0).astype(bf16)
+        dv = dv + dot_nn(probs, do_h)
+        dk = dk + dot_nn(d_scores, q_h)
+        dq_parts.append(dot_nn(k_t[h * HEAD_DIM : (h + 1) * HEAD_DIM], d_scores))
+    dq = jnp.transpose(jnp.concatenate(dq_parts, axis=0)) * score_scale
+    return dq.astype(bf16), (dk * score_scale).astype(bf16), dv.astype(bf16)
+
+
 def attn_backward_kernel(
     lens_ref, q_ref, k_ref, v_ref, do_ref, o_ref, long_ref, short_ref, dq_ref, dk_ref, dv_ref, sum_ref
 ):
     sum_q = jnp.zeros((1, PAIR), f32)
     sum_v = jnp.zeros((1, PAIR), f32)
     for first, rows, length, index in SEQS:
-        q = q_ref[:, first : first + rows, :].reshape(length, PAIR)
-        k = k_ref[:, first : first + rows, :].reshape(length, PAIR)
-        v = v_ref[:, first : first + rows, :].reshape(length, PAIR)
-        do = do_ref[:, first : first + rows, :].reshape(length, PAIR)
-        o = o_ref[:, first : first + rows, :].reshape(length, PAIR)
-        k_t = jnp.transpose(k)
-        inner = jnp.transpose(do.astype(f32) * o.astype(f32))
-        head_lane = lax.broadcasted_iota(jnp.int32, (length, PAIR), 1) // HEAD_DIM
-        live = lax.broadcasted_iota(jnp.int32, (length, length), 0) < lens_ref[index]
-        dq_parts = []
-        dk = jnp.zeros((length, PAIR), f32)
-        dv = jnp.zeros((length, PAIR), f32)
-        for h in range(2):
-            keep = head_lane == h
-            v_h = jnp.where(keep, v, jnp.zeros_like(v))
-            do_h = jnp.where(keep, do, jnp.zeros_like(do))
-            q_h = jnp.where(keep, q, jnp.zeros_like(q))
-            probs = long_ref[h] if index == 0 else short_ref[h, index - 1]
-            delta = jnp.sum(inner[h * HEAD_DIM : (h + 1) * HEAD_DIM], axis=0, keepdims=True)
-            d_probs = dot_nt(v_h, do)
-            d_scores = jnp.where(live, probs.astype(f32) * (d_probs - delta), 0.0).astype(bf16)
-            dv = dv + dot_nn(probs, do_h)
-            dk = dk + dot_nn(d_scores, q_h)
-            dq_parts.append(dot_nn(k_t[h * HEAD_DIM : (h + 1) * HEAD_DIM], d_scores))
-        dq = (jnp.transpose(jnp.concatenate(dq_parts, axis=0)) * score_scale).astype(bf16)
-        dk = (dk * score_scale).astype(bf16)
-        dv = dv.astype(bf16)
+        args = [r[:, first : first + rows, :].reshape(length, PAIR) for r in (q_ref, k_ref, v_ref, do_ref, o_ref)]
+        kept = lambda h, index=index: long_ref[h] if index == 0 else short_ref[h, index - 1]
+        dq, dk, dv = attend_back(*args, lens_ref[index], kept)
         sum_q = sum_q + jnp.sum(dq.astype(f32), axis=0, keepdims=True)
         sum_v = sum_v + jnp.sum(dv.astype(f32), axis=0, keepdims=True)
-        dq_ref[:, first : first + rows, :] = dq.reshape(4, rows, PAIR)
-        dk_ref[:, first : first + rows, :] = dk.reshape(4, rows, PAIR)
-        dv_ref[:, first : first + rows, :] = dv.reshape(4, rows, PAIR)
+        for ref, v in ((dq_ref, dq), (dk_ref, dk), (dv_ref, dv)):
+            ref[:, first : first + rows, :] = v.reshape(4, rows, PAIR)
     sum_ref[0:1, :] = sum_q
     sum_ref[1:2, :] = sum_v
     sum_ref[2:8, :] = jnp.zeros((6, PAIR), f32)
@@ -772,14 +770,15 @@
 
 
 class Grad:
-    def __init__(self, src, acc, cbuf, xbuf, ybuf, zbuf, fin, sems, order):
-        self.src, self.acc, self.cbuf, self.xbuf, self.ybuf, self.zbuf, self.fin = src, acc, cbuf, xbuf, ybuf, zbuf, fin
+    def __init__(self, theirs, acc, cbuf, xbuf, ybuf, zbuf, quarter, fin, sems, order):
+        self.theirs, self.acc, self.cbuf, self.xbuf, self.ybuf, self.zbuf = theirs, acc, cbuf, xbuf, ybuf, zbuf
+        self.quarter, self.fin, self.order = quarter, fin, order
         self.c_send, self.c_recv, self.x_send, self.x_recv, self.y_send, self.y_recv = sems[:6]
         self.z_send, self.z_recv, self.f_send, self.f_recv, self.local = sems[6:]
-        self.order = order
         self.dp, self.s, self.z, self.x, self.y, self.c = place()
-        self.rows, cols = src.shape[2:]
+        self.rows, cols = fin.shape
         self.half_rows, self.half_cols = self.rows // 2, cols // 2
+        self.core_pieces = 4 if order == "zxy" else 2
 
     def cols(self, core):
         return pl.ds(pl.multiple_of(core * self.half_cols, 128), self.half_cols)
@@ -787,41 +786,36 @@
     def some(self, q):
         return pl.ds(pl.multiple_of(q * self.half_rows, 16), self.half_rows)
 
+    def core_view(self, ref, j):
+        if self.order == "zxy":
+            return ref.at[j]
+        return ref.at[:, (1 - self.x) if j == 0 else self.x]
+
     def core_copy(self, j):
-        xd = (1 - self.x) if j == 0 else self.x
         return remote(
-            self.src.at[:, xd, :, self.cols(1 - self.c)],
-            self.cbuf.at[:, xd],
+            self.core_view(self.theirs, j),
+            self.core_view(self.cbuf, j),
             self.c_send.at[j],
             self.c_recv.at[j],
             (self.dp, self.s + 1 - 2 * self.c),
         )
 
-    def own_copy(self, j):
-        xd = (1 - self.x) if j == 0 else self.x
-        return pltpu.make_async_copy(self.src.at[:, xd, :, self.cols(self.c)], self.acc.at[:, xd], self.local.at[j])
-
     def x_copy(self, zd):
         device = (self.z * 2 + 1 - self.x, self.s)
-        return remote(
-            self.acc.at[zd, 1 - self.x], self.xbuf.at[zd], self.x_send.at[zd], self.x_recv.at[zd], device
-        )
+        j = zd if self.order == "xyz" else 0
+        return remote(self.acc.at[zd, 1 - self.x], self.xbuf.at[j], self.x_send.at[j], self.x_recv.at[j], device)
 
     def y_copy(self, zd):
         device = (self.dp, (1 - self.y) * 2 + self.c)
-        return remote(
-            self.acc.at[zd, self.x, self.some(1 - self.y)],
-            self.ybuf.at[zd],
-            self.y_send.at[zd],
-            self.y_recv.at[zd],
-            device,
-        )
+        j = zd if self.order == "xyz" else 0
+        src = self.acc.at[zd, self.x, self.some(1 - self.y)]
+        return remote(src, self.ybuf.at[j], self.y_send.at[j], self.y_recv.at[j], device)
 
     def z_copy(self, k):
         zd = (self.z + k) % Z_CHIPS
         src = self.acc.at[zd, self.x, self.some(self.y)] if self.order == "xyz" else self.acc.at[zd]
         return remote(
-            src, self.zbuf.at[k], self.z_send.at[k], self.z_recv.at[k], (zd * 2 + self.x, self.s)
+            src, self.zbuf.at[k - 1], self.z_send.at[k], self.z_recv.at[k], (zd * 2 + self.x, self.s)
         )
 
     def fin_quarter(self, s):
@@ -829,7 +823,7 @@
 
     def fin_copy(self, k):
         return remote(
-            self.fin_quarter(self.s),
+            self.quarter,
             self.fin_quarter(self.s),
             self.f_send.at[k],
             self.f_recv.at[k],
@@ -838,12 +832,30 @@
 
     def fin_in(self, k):
         ref = self.fin_quarter((self.s + 4 - k) % 4)
-        return remote(ref, ref, self.f_send.at[k], self.f_recv.at[k], (self.dp, self.s))
+        return remote(self.quarter, ref, self.f_send.at[k], self.f_recv.at[k], (self.dp, self.s))
+
+    def fin_own(self):
+        return pltpu.make_async_copy(self.quarter, self.fin_quarter(self.s), self.local)
+
+    def core_start(self, j):
+        self.core_copy(j).start()
+
+    def core_sent(self):
+        for j in range(self.core_pieces):
+            self.core_copy(j).wait_send()
+
+    def z_block(self, k):
+        zd = (self.z + k) % Z_CHIPS
+        self.core_copy(zd).wait_recv()
+        for xd in range(2):
+            self.acc[zd, xd] = (self.acc[zd, xd].astype(f32) + self.cbuf[zd, xd].astype(f32)).astype(bf16)
+
+        if k % Z_CHIPS:
+            self.z_copy(k % Z_CHIPS).start()
 
     def core_add(self, j):
         xd = (1 - self.x) if j == 0 else self.x
         self.core_copy(j).wait_recv()
-        self.own_copy(j).wait()
 
         def one(zd, carry):
             self.acc[zd, xd] = (self.acc[zd, xd].astype(f32) + self.cbuf[zd, xd].astype(f32)).astype(bf16)
@@ -851,36 +863,40 @@
 
         lax.fori_loop(0, Z_CHIPS, one, 0)
 
+    def pass_x(self, k):
+        zd = (self.z + k + 1) % Z_CHIPS
+        self.x_copy(zd).wait_recv()
+        self.acc[zd, self.x] = (self.acc[zd, self.x].astype(f32) + self.xbuf[zd].astype(f32)).astype(bf16)
+        self.y_copy(zd).start()
+
     def publish(self, total):
-        self.fin[self.some(self.y), self.cols(self.c)] = total.astype(bf16)
+        self.quarter[...] = total.astype(bf16)
+        self.fin_own().start()
         for k in range(1, 4):
             self.fin_copy(k).start()
 
-    stages = 7
-
     def stage(self, i):
-        if i == 0:
-            for j in range(2):
-                self.core_copy(j).start()
-                self.own_copy(j).start()
+        if not isinstance(i, int) or i >= 30:
+            self.pass_x(i - 30)
         elif self.order == "xyz":
             if i == 1:
                 self.core_add(0)
                 for k in range(Z_CHIPS):
-                    self.x_copy((self.z + k) % Z_CHIPS).start()
+                    self.x_copy((self.z + k + 1) % Z_CHIPS).start()
             elif i == 2:
                 self.core_add(1)
             elif i == 3:
-                for k in range(Z_CHIPS):
-                    zd = (self.z + k) % Z_CHIPS
-                    self.x_copy(zd).wait_recv()
-                    self.acc[zd, self.x] = (self.acc[zd, self.x].astype(f32) + self.xbuf[zd].astype(f32)).astype(bf16)
-                    self.y_copy(zd).start()
+
+                def pass_x(k, carry):
+                    self.pass_x(k)
+                    return carry
+
+                lax.fori_loop(0, Z_CHIPS, pass_x, 0)
             elif i == 4:
+                rows = self.some(self.y)
                 for k in (1, 2, 3, 0):
                     zd = (self.z + k) % Z_CHIPS
                     self.y_copy(zd).wait_recv()
-                    rows = self.some(self.y)
                     self.acc[zd, self.x, rows] = (
                         self.acc[zd, self.x, rows].astype(f32) + self.ybuf[zd].astype(f32)
                     ).astype(bf16)
@@ -890,38 +906,32 @@
                 total = self.acc[self.z, self.x, self.some(self.y)].astype(f32)
                 for k in range(1, Z_CHIPS):
                     self.z_copy(k).wait_recv()
-                    total = total + self.zbuf[k].astype(f32)
+                    total = total + self.zbuf[k - 1].astype(f32)
                 self.publish(total)
         else:
-            if i == 1:
-                self.core_add(0)
-                self.core_add(1)
-                for k in range(1, Z_CHIPS):
-                    self.z_copy(k).start()
-            elif i == 3:
+            if i == 3:
                 for k in range(1, Z_CHIPS):
                     self.z_copy(k).wait_recv()
                 for xd in range(2):
                     total = self.acc[self.z, xd].astype(f32)
                     for k in range(1, Z_CHIPS):
-                        total = total + self.zbuf[k, xd].astype(f32)
+                        total = total + self.zbuf[k - 1, xd].astype(f32)
                     self.acc[self.z, xd] = total.astype(bf16)
                 self.x_copy(self.z).start()
             elif i == 4:
                 self.x_copy(self.z).wait_recv()
-                total = self.acc[self.z, self.x].astype(f32) + self.xbuf[self.z].astype(f32)
+                total = self.acc[self.z, self.x].astype(f32) + self.xbuf[0].astype(f32)
                 self.acc[self.z, self.x] = total.astype(bf16)
                 self.y_copy(self.z).start()
             elif i == 5:
                 self.y_copy(self.z).wait_recv()
-                self.publish(self.acc[self.z, self.x, self.some(self.y)].astype(f32) + self.ybuf[self.z].astype(f32))
+                self.publish(self.acc[self.z, self.x, self.some(self.y)].astype(f32) + self.ybuf[0].astype(f32))
         if i == 6:
+            self.fin_own().wait()
             for k in range(1, 4):
                 self.fin_in(k).wait_recv()
 
     def settle(self):
-        for j in range(2):
-            self.core_copy(j).wait_send()
         for k in range(1, Z_CHIPS):
             self.z_copy(k).wait_send()
         for k in range(1, 4):
@@ -945,6 +955,10 @@
     copies, own, start, finish, settle = Tokens.copies, Tokens.own, Tokens.start, Tokens.finish, Tokens.settle
 
 
+def sums_window(d):
+    return jnp.minimum(d * 96 // 128, 4) * 128
+
+
 class Sums:
     def __init__(self, src, sbuf, part, dbuf, out, sems):
         self.src, self.sbuf, self.part, self.dbuf, self.out = src, sbuf, part, dbuf, out
@@ -954,11 +968,12 @@
     def s_copy(self, k, source):
         return remote(self.src, self.sbuf.at[source], self.s_send.at[k], self.s_recv.at[k], (self.dp, (self.s + k) % 4))
 
+    def window(self, d):
+        return self.part.at[:, pl.ds(pl.multiple_of(sums_window(d), 128), 256)]
+
     def d_copy(self, k, source):
         target = (self.dp + k) % 8
-        return remote(
-            self.part.at[target], self.dbuf.at[source], self.d_send.at[k], self.d_recv.at[k], (target, self.s)
-        )
+        return remote(self.window(target), self.dbuf.at[source], self.d_send.at[k], self.d_recv.at[k], (target, self.s))
 
     def stage(self, i):
         if i == 0:
@@ -971,7 +986,7 @@
             self.part[...] = (self.sbuf[0] + self.sbuf[1]) + (self.sbuf[2] + self.sbuf[3])
             for k in range(1, 8):
                 self.d_copy(k, self.dp).start()
-            self.dbuf[self.dp] = self.part[self.dp]
+            self.dbuf[self.dp] = self.window(self.dp)[...]
         elif i == 2:
             for k in range(1, 8):
                 self.d_copy(k, (self.dp + 8 - k) % 8).wait_recv()
@@ -987,87 +1002,327 @@
             self.d_copy(k, self.dp).wait_send()
 
 
-ORDERS = ("zxy", "xyz", "xyz", "xyz")
-
-
-def reduce_kernel(count, *refs):
-    grads, refs = refs[:count], refs[count:]
-    sums_ref, out_rows, back_rows, refs = refs[0], refs[1], refs[2], refs[3:]
-    fins, refs = refs[:count], refs[count:]
-    (sums_out, short_out, long_out, short_back, long_back), refs = refs[:5], refs[5:]
-    bufs, refs = refs[: 5 * count], refs[5 * count :]
-    (sbuf, part, dbuf), refs = refs[:3], refs[3:]
-    sems, refs = refs[:11], refs[11:]
-    s_sems, (t_send, t_recv, local) = refs[:4], refs[4:]
+PIECES = (
+    ("down", 384, D, "zxy"),
+    ("one", 96, FF, "xyz"),
+    ("o", 96, D, "xyz"),
+    ("qkv0", 96, D, "xyz"),
+    ("qkv1", 96, D, "xyz"),
+    ("qkv2", 96, D, "xyz"),
+)
+
+
+def backward_kernel(*refs):
+    refs = list(refs)
+
+    def take(n):
+        out = refs[:n]
+        del refs[:n]
+        return out
+
+    lens_ref, sums_in = take(2)
+    act_hbm, dfb_hbm, y1b_hbm, dub_hbm, att_hbm, dab_hbm, dob_hbm, qkv_hbm = take(8)
+    long_hbm, short_hbm, tok_hbm, dh_hbm, w_hbm, out_rows = take(6)
+    fins = take(len(PIECES))
+    (sums_out,) = take(1)
+    short_out, long_out, short_back, long_back = take(4)
+    theirs_a, theirs_b = take(2)
+    bufs = [take(6) for _ in PIECES]
+    big, dfb_s, y1b_s, att_s, at_s, qkv_s, dob_s, long_s, short_s, dh_s, w_s, dqkv_s, back_s = take(13)
+    sums_s, sbuf, part, dbuf = take(4)
+    sems = take(11)
+    s_sems = take(4)
+    t_send, t_recv, local, load_sem, big_sem, p_sem = take(6)
+
+    dp, s, z, x, y, c = place()
     greet()
+    outs = Returns(out_rows, long_out, short_out, t_send.at[0], t_recv.at[0], local.at[0])
+    backs = Returns(back_s, long_back, short_back, t_send.at[1], t_recv.at[1], local.at[1])
+
+    def load(i, src, dst):
+        copy = pltpu.make_async_copy(src, dst, load_sem.at[i])
+        copy.start()
+        return copy
+
+    def act_chunk(k):
+        zd = (z + k) % Z_CHIPS
+        return act_hbm.at[:, pl.ds(pl.multiple_of(zd * D, D), D)]
+
+    def dub_chunk(k):
+        first = jnp.where(k < 2, (1 - c) * 2 + k, c * 2 + k - 2)
+        return dub_hbm.at[:, pl.ds(pl.multiple_of(first * D, D), D)]
+
+    def big_copy(src, slot):
+        return pltpu.make_async_copy(src, big.at[slot], big_sem.at[slot])
+
+    big_copy(act_chunk(1), 1).start()
+    load_dfb = load(0, dfb_hbm, dfb_s)
+    load_y1b = load(1, y1b_hbm, y1b_s)
+    load_att = load(2, att_hbm, att_s)
+    load_qkv = load(3, qkv_hbm, qkv_s)
+    load_dob = load(4, dob_hbm, dob_s)
+    load_w = load(5, w_hbm, w_s)
+    load_dh = load(6, dh_hbm, dh_s)
+
     pieces = []
-    for i in range(count):
-        acc, cbuf, xbuf, ybuf, zbuf = bufs[5 * i : 5 * i + 5]
-        pieces.append(
-            Grad(grads[i], acc, cbuf, xbuf, ybuf, zbuf, fins[i], [r.at[i] for r in sems], ORDERS[i])
+    for i, (name, rows, cols, order) in enumerate(PIECES):
+        theirs = (theirs_a, theirs_b)[i] if i < 2 else theirs_a.at[:, :, pl.ds((i - 2) * 96, 96), :]
+        pieces.append(Grad(theirs, *bufs[i], fins[i], [r.at[i] for r in sems], order))
+    down, one, o_piece = pieces[:3]
+    sums = Sums(sums_s, sbuf, part, dbuf, sums_out, s_sems)
+    outs.start()
+
+    def columns(core, width):
+        return pl.ds(pl.multiple_of(core * width, 128), width)
+
+    load_dfb.wait()
+
+    def down_block(k, carry):
+        zd = (z + k) % Z_CHIPS
+        slot = k % 2
+        big_copy(act_chunk(k), slot).wait()
+
+        @pl.when(k < Z_CHIPS)
+        def _():
+            big_copy(act_chunk(k + 1), 1 - slot).start()
+
+        @pl.when(k == Z_CHIPS)
+        def _():
+            big_copy(dub_chunk(0), 1 - slot).start()
+
+        at_s[...] = jnp.transpose(big[slot])
+        theirs_a[zd] = dot_nn(at_s[...], dfb_s[:, columns(1 - c, D // 2)]).astype(bf16).reshape(2, 384, D // 2)
+        down.core_start(zd)
+        down.acc[zd] = dot_nn(at_s[...], dfb_s[:, columns(c, D // 2)]).astype(bf16).reshape(2, 384, D // 2)
+        for j in range(2, Z_CHIPS + 1):
+
+            @pl.when(k == j)
+            def _():
+                down.z_block(j - 1)
+
+        return carry
+
+    lax.fori_loop(1, Z_CHIPS + 1, down_block, 0)
+    load_dab = load(0, dab_hbm, dfb_s)
+
+    load_y1b.wait()
+    at_s[...] = jnp.transpose(y1b_s[...])
+    load_tok = load(1, tok_hbm, y1b_s)
+
+    def one_block(k, carry):
+        slot = (k + 1) % 2
+        big_copy(dub_chunk(k), slot).wait()
+
+        @pl.when(k < 3)
+        def _():
+            big_copy(dub_chunk(k + 1), 1 - slot).start()
+
+        grad = dot_nn(at_s[...], big[slot]).astype(bf16).reshape(4, 2, 96, D)
+        cols = pl.ds(pl.multiple_of((k % 2) * D, D), D)
+
+        @pl.when(k < 2)
+        def _():
+            theirs_b[:, :, :, cols] = grad
+
+        @pl.when(k >= 2)
+        def _():
+            one.acc[:, :, :, cols] = grad
+
+        @pl.when(k == 1)
+        def _():
+            one.core_start(0)
+            one.core_start(1)
+            down.z_block(Z_CHIPS)
+
+        return carry
+
+    lax.fori_loop(0, 4, one_block, 0)
+    one.stage(1)
+    down.core_sent()
+
+    def small_grad(piece, right):
+        piece.theirs[...] = dot_nn(at_s[...], right(1 - c)).astype(bf16).reshape(4, 2, 96, D // 2)
+        piece.core_start(0)
+        piece.core_start(1)
+        piece.acc[...] = dot_nn(at_s[...], right(c)).astype(bf16).reshape(4, 2, 96, D // 2)
+
+    load_att.wait()
+    at_s[...] = jnp.transpose(att_s[...].reshape(1024, D))
+    load_dab.wait()
+    small_grad(o_piece, lambda core: dfb_s[:, columns(core, D // 2)])
+    one.stage(2)
+    o_piece.stage(1)
+
+    load_tok.wait()
+    at_s[...] = jnp.transpose(y1b_s[...])
+    load_qkv.wait()
+    load_dob.wait()
+    load_w.wait()
+    load_dh.wait()
+    sums_s[...] = sums_in[...]
+    pairs = D // PAIR
+
+    def probs_copies(i, slot):
+        return (
+            pltpu.make_async_copy(long_hbm.at[pl.ds(2 * i, 2)], long_s.at[slot], p_sem.at[0, slot]),
+            pltpu.make_async_copy(short_hbm.at[pl.ds(2 * i, 2)], short_s.at[slot], p_sem.at[1, slot]),
         )
-    sums = Sums(sums_ref, sbuf, part, dbuf, sums_out, s_sems)
-    outs = Returns(out_rows, long_out, short_out, t_send.at[0], t_recv.at[0], local.at[0])
-    backs = Returns(back_rows, long_back, short_back, t_send.at[1], t_recv.at[1], local.at[1])
-    outs.start()
-    for t in range(Grad.stages + count - 1):
-        for i, piece in enumerate(pieces):
-            if 0 <= t - i < Grad.stages:
-                piece.stage(t - i)
-        if t < 3:
-            sums.stage(t)
-        if t == 2:
-            backs.start()
+
+    for copy in probs_copies(0, 0):
+        copy.start()
+
+    def run(jobs):
+        for index, stage in jobs:
+            pieces[index].stage(stage)
+
+    before = (
+        ((2, 2),),
+        ((1, 30),),
+        ((3, 2),),
+        ((1, 31),),
+        ((4, 2), (1, 32)),
+        ((1, 33),),
+    )
+    after = (
+        ((3, 1),),
+        ((4, 1),),
+        ((5, 1), (5, 2), (1, 4)),
+    )
+    tail = (
+        (2, 3), (2, 4), (1, 5), (0, 3), (3, 3), (3, 4), (2, 5), (0, 4), (4, 3), (4, 4), (3, 5), (0, 5),
+        (5, 3), (5, 4), (4, 5), (5, 5),
+    )
+    for g in range(3):
+
+        def pair(i, carry, g=g):
+            for j in range(2):
+
+                @pl.when(i == 2 * g + j)
+                def _():
+                    run(before[2 * g + j])
+
+            slot = i % 2
+            for copy in probs_copies(i, slot):
+                copy.wait()
+
+            @pl.when(i + 1 < pairs)
+            def _():
+                for copy in probs_copies(i + 1, 1 - slot):
+                    copy.start()
+
+            lanes = pl.ds(pl.multiple_of(i * PAIR, PAIR), PAIR)
+            sum_q = jnp.zeros((1, PAIR), f32)
+            sum_v = jnp.zeros((1, PAIR), f32)
+            for first, rows, length, index in SEQS:
+                q, k, v = [
+                    qkv_s[:, first : first + rows, pl.ds(pl.multiple_of(base + i * PAIR, PAIR), PAIR)].reshape(length, PAIR)
+                    for base in (0, D, 2 * D)
+                ]
+                do, o = [r[:, first : first + rows, lanes].reshape(length, PAIR) for r in (dob_s, att_s)]
+                kept = lambda h, index=index: long_s[slot, h] if index == 0 else short_s[slot, h, index - 1]
+                grads = attend_back(q, k, v, do, o, lens_ref[index], kept)
+                sum_q = sum_q + jnp.sum(grads[0].astype(f32), axis=0, keepdims=True)
+                sum_v = sum_v + jnp.sum(grads[2].astype(f32), axis=0, keepdims=True)
+                for j in range(3):
+                    dst = pl.ds(pl.multiple_of(j * 256 + (i % 2) * PAIR, PAIR), PAIR)
+                    dqkv_s[:, first : first + rows, dst] = grads[j].reshape(4, rows, PAIR)
+            sums_s[0:1, lanes] = sum_q
+            sums_s[1:2, lanes] = sum_v
+            return carry
+
+        lax.fori_loop(2 * g, 2 * g + 2, pair, 0)
+        small_grad(pieces[3 + g], lambda core: dqkv_s[:, :, columns(core, D // 2)].reshape(1024, D // 2))
+        run(after[g])
+        if g == 2:
+            sums.stage(0)
+        total = dh_s[...]
+        for j in range(3):
+            total = total + dot_nt(
+                dqkv_s[:, :, j * 256 : (j + 1) * 256].reshape(1024, 256), w_s[:, j * D + g * 256 : j * D + (g + 1) * 256]
+            )
+        if g < 2:
+            dh_s[...] = total
+        else:
+            back_s[...] = total.astype(bf16).reshape(4, 256, D)
+
+    backs.start()
+    sums.stage(1)
+    run(tail)
+    sums.stage(2)
+    run([(i, 6) for i in range(6)])
     outs.finish()
     backs.finish()
-    for piece in pieces:
+    for i, piece in enumerate(pieces):
+        if i > 0:
+            piece.core_sent()
         piece.settle()
     sums.settle()
     outs.settle()
     backs.settle()
 
 
-def reduce_all(grads, sums, out_rows, back_rows):
-    count = len(grads)
+def backward(lens, sums, arrays, out_rows):
     any_spec = pl.BlockSpec(memory_space=pl.ANY)
     vmem = pl.BlockSpec(memory_space=pltpu.VMEM)
+    smem = pl.BlockSpec(memory_space=pltpu.SMEM)
     shape = jax.ShapeDtypeStruct
     dma = pltpu.SemaphoreType.DMA
+    count = len(PIECES)
     bufs = []
-    for g, order in zip(grads, ORDERS):
-        rows, cols = g.shape[2:]
+    for name, rows, cols, order in PIECES:
         half, cut = cols // 2, rows // 2
+        blocks = 4 if order == "xyz" else 1
         bufs += [
             pltpu.VMEM((4, 2, rows, half), bf16),
             pltpu.VMEM((4, 2, rows, half), bf16),
-            pltpu.VMEM((4, rows, half), bf16),
-            pltpu.VMEM((4, cut, half), bf16),
-            pltpu.VMEM((4, cut, half) if order == "xyz" else (4, 2, rows, half), bf16),
+            pltpu.VMEM((blocks, rows, half), bf16),
+            pltpu.VMEM((blocks, cut, half), bf16),
+            pltpu.VMEM((3, cut, half) if order == "xyz" else (3, 2, rows, half), bf16),
+            pltpu.VMEM((cut, half), bf16),
         ]
+    n = 1024
     return pl.pallas_call(
-        lambda *refs: reduce_kernel(count, *refs),
-        in_specs=[any_spec] * count + [vmem, any_spec, any_spec],
-        out_specs=[vmem] * count + [vmem] + [any_spec] * 4,
-        out_shape=[shape(g.shape[2:], bf16) for g in grads]
+        backward_kernel,
+        in_specs=[smem, vmem] + [any_spec] * (len(arrays) + 1),
+        out_specs=[any_spec] * count + [vmem] + [any_spec] * 4,
+        out_shape=[shape((rows, cols), bf16) for _, rows, cols, _ in PIECES]
         + [
-            shape((16, 128), f32),
+            shape((16, 256), f32),
             shape((2, 4, 64, D), bf16),
             shape((2, 2, 128, D), bf16),
             shape((2, 4, 64, D), bf16),
             shape((2, 2, 128, D), bf16),
         ],
-        scratch_shapes=bufs
-        + [pltpu.VMEM((4, 8, 16, 128), f32), pltpu.VMEM((8, 16, 128), f32), pltpu.VMEM((8, 16, 128), f32)]
-        + [dma((count, 2))] * 2
-        + [dma((count, 4))] * 8
-        + [dma((count, 2))]
+        scratch_shapes=[pltpu.VMEM((4, 2, 384, D // 2), bf16), pltpu.VMEM((4, 2, 96, FF // 2), bf16)]
+        + bufs
+        + [
+            pltpu.VMEM((2, n, D), bf16),
+            pltpu.VMEM((n, D), bf16),
+            pltpu.VMEM((n, D), bf16),
+            pltpu.VMEM((4, 256, D), bf16),
+            pltpu.VMEM((D, n), bf16),
+            pltpu.VMEM((4, 256, 3 * D), bf16),
+            pltpu.VMEM((4, 256, D), bf16),
+            pltpu.VMEM((2, 2, LONG_L, LONG_L), bf16),
+            pltpu.VMEM((2, 2, 2, SHORT_L, SHORT_L), bf16),
+            pltpu.VMEM((n, D), f32),
+            pltpu.VMEM((D, 3 * D), bf16),
+            pltpu.VMEM((4, 256, D), bf16),
+            pltpu.VMEM((4, 256, D), bf16),
+            pltpu.VMEM((16, D), f32),
+            pltpu.VMEM((4, 16, D), f32),
+            pltpu.VMEM((16, D), f32),
+            pltpu.VMEM((8, 16, 256), f32),
+        ]
+        + [dma((count, 4))] * 10
+        + [dma((count,))]
         + [dma((4,)), dma((4,)), dma((8,)), dma((8,))]
-        + [dma((2, 4, 3)), dma((2, 4, 3)), dma((2, 3))],
+        + [dma((2, 4, 3)), dma((2, 4, 3)), dma((2, 3)), dma((7,)), dma((2,)), dma((2, 2))],
         compiler_params=pltpu.CompilerParams(
             vmem_limit_bytes=VMEM_BYTES, collective_id=1, has_side_effects=True
         ),
-        name="reduce",
-    )(*grads, sums, out_rows, back_rows)
+        name="backward",
+    )(lens, sums, *arrays, out_rows)
 
 
 def transpose_dot(left, right):
@@ -1194,29 +1449,31 @@
     out, y1b, act, dfb, dub, dab, dob, dh, sums = middle(
         lens, flat_attended, rows, cotangent.reshape(1024, D), w_o, w_1, w_2, vec
     )
-    d_down = transpose_dot(act, dfb).astype(bf16)
-    d_one = transpose_dot(y1b, dub).astype(bf16)
-    d_o = transpose_dot(flat_attended, dab).astype(bf16)
-    dq, dk, dv, qv_sums = attn_backward(
-        lens, qkv, dob.reshape(4, 256, D), attended, long_probs, short_probs
-    )
-    d_qkv = jnp.concatenate([dq, dk, dv], axis=2).reshape(1024, 3 * D)
-    d_wqkv = transpose_dot(rows, d_qkv).astype(bf16)
-    back = (dh + right_dot(d_qkv, w_qkv)).astype(bf16).reshape(4, 256, D)
-
-    vector_total = jnp.concatenate([qv_sums[:2], sums[2:12]], axis=0)
     own_rows = vector_master.shape[0]
     if lax.axis_size("dp") == 8:
-        blocks = lambda g: g.reshape(4, 2, g.shape[0] // 8, g.shape[1])
-        spread = jnp.transpose(vector_total.reshape(12, 8, own_rows), (1, 0, 2))
-        spread = jnp.pad(spread, ((0, 0), (0, 4), (0, 128 - own_rows)))
-        down_low, one_low, o_low, qkv_low, sums_own, short_out, long_out, short_back, long_back = reduce_all(
-            [blocks(g) for g in (d_down, d_one, d_o, d_wqkv)], spread, out.reshape(4, 256, D), back
+        arrays = (
+            act, dfb, y1b, dub, attended, dab, dob.reshape(4, 256, D), qkv, long_probs, short_probs, rows, dh, w_qkv
         )
-        vector_reduced = jnp.transpose(sums_own[:12, :own_rows])
-        wide_reduced = jnp.concatenate([qkv_low, o_low, one_low], axis=1).astype(f32)
+        down_low, one_low, o_low, low_0, low_1, low_2, sums_own, short_out, long_out, short_back, long_back = backward(
+            lens, sums, arrays, out.reshape(4, 256, D)
+        )
+        index = lax.axis_index("dp")
+        own_sums = lax.dynamic_slice(sums_own, (0, index * own_rows - sums_window(index)), (12, own_rows))
+        vector_reduced = jnp.transpose(own_sums)
+        lows = [low[:, j * 256 : (j + 1) * 256] for j in range(3) for low in (low_0, low_1, low_2)]
+        wide_reduced = jnp.concatenate(lows + [o_low, one_low], axis=1).astype(f32)
         down_reduced = down_low.astype(f32)
     else:
+        d_down = transpose_dot(act, dfb).astype(bf16)
+        d_one = transpose_dot(y1b, dub).astype(bf16)
+        d_o = transpose_dot(flat_attended, dab).astype(bf16)
+        dq, dk, dv, qv_sums = attn_backward(
+            lens, qkv, dob.reshape(4, 256, D), attended, long_probs, short_probs
+        )
+        d_qkv = jnp.concatenate([dq, dk, dv], axis=2).reshape(1024, 3 * D)
+        d_wqkv = transpose_dot(rows, d_qkv).astype(bf16)
+        back = (dh + right_dot(d_qkv, w_qkv)).astype(bf16).reshape(4, 256, D)
+        vector_total = jnp.concatenate([qv_sums[:2], sums[2:12]], axis=0)
         vector_sum = jnp.transpose(lax.psum(vector_total, ("dp", "seq")))
         vector_reduced = lax.dynamic_slice_in_dim(vector_sum, lax.axis_index("dp") * own_rows, own_rows, 0)
         wide_reduced = jnp.concatenate([reduce_rows(d_wqkv), reduce_rows(d_o), reduce_rows(d_one)], axis=1)

time: 349 us -> 306 us (0.88); the launches traced: 348 us -> 300 us
  matrix products: 26.6 us -> 0 us
  Pallas kernels: 291 us -> 265 us
  local copies, waits for them, and re-layouts: 14.6 us -> 19.5 us
    dot_general x5 -> x0, matrix products: 26.6 us -> none  [the longest x4 21.7 us: transpose_dot(): return jnp.einsum('ra,rb->ab', left, right, preferred_element_type=f32)]
    pallas_call x2 -> x1, Pallas kernels: 155 us -> 129 us  [backward(): pl.pallas_call(backward_kernel, in_specs=[smem, vmem] + [any_spec] * (len...]
    unnamed x78 -> x52, local copies, waits for them, and re-layouts: 10.8 us -> 16.4 us
where the time goes in v5:
time: 306 us; the launch traced here: 300 us
  Pallas kernels  265 us (87%)
  local copies, waits for them, and re-layouts  19.5 us (6%)
  other arithmetic  14.7 us (5%)
    pallas_call x1, Pallas kernels, backward(): pl.pallas_call(backward_kernel, in_specs=[smem, vmem] + [any_spec] * (len...  129 us
    pallas_call x1, Pallas kernels, forward(): pl.pallas_call(forward_kernel, in_specs=[smem, vmem, vmem, vmem] + [any_s...  92.9 us
    pallas_call x1, Pallas kernels, middle(): pl.pallas_call(middle_kernel, grid=(n // rows,), in_specs=[pl.BlockSpec(m...  43.2 us
    unnamed x52, local copies, waits for them, and re-layouts  16.4 us
    convert_element_type x3, other arithmetic, update(): return (velocity, averaged, updated, updated.astype(jnp.bfloat16))  7.85 us

profile of v5, /device:TPU:0, one launch (start us, length us, event | category | flops | bytes accessed | tf_op | source)
XLA Modules:
  0.0 300.2 jit_solution(3813490441339550204)
XLA Ops:
  0.7 0.0 copy-start
  0.7 0.6 copy-done
  1.3 0.6 constant_dynamic-slice_fusion.2
  1.9 1.3 constant_dynamic-slice_fusion.1
  3.2 2.5 pad_add_fusion.lens_ref.refs_0_
  5.7 0.7 convert_bitcast_fusion
  6.4 0.2 dynamic_update_slice.3.vec_ref
  6.6 0.0 copy-start.14
  6.6 0.6 copy-done.14
  7.2 92.9 %forward.1 = (bf16[8,96,2304]{2,1,0:T(8,128)(2,1)}, bf16[8,96,768]{2,1,0:T(8,128)(2,1)}, bf16[8,96,3072]{2,1,0:T(8,128)(2,1)}, bf16[8,384,768]{2,1,0:T(8,128)(2,...) custom-call(s32[3]{0:T(128)} %pad_add_fusion.lens_ref.refs_0_, ...), custom_call_target="tpu_custom_call" | custom-call | tf_op jit(solution)/shard_map/forward/pallas_call | solution.py:723
  100.2 43.2 %middle.1 = (bf16[1024,768]{1,0:T(8,128)(2,1)}, bf16[1024,768]{1,0:T(8,128)(2,1)}, bf16[1024,3072]{1,0:T(8,128)(2,1)}, bf16[1024,768]{1,0:T(8,128)(2,1)}, bf16[1...) custom-call(s32[3]{0:T(128)} %pad_add_fusion.lens_ref.refs_0_, ...), custom_call_target="tpu_custom_call" | custom-call | tf_op jit(solution)/shard_map/middle/pallas_call | solution.py:267
  143.4 0.0 copy-start.16
  143.4 0.0 copy-start.18
  143.4 0.0 copy-start.17
  143.5 128.6 %backward.1 = (bf16[384,768]{1,0:T(8,128)(2,1)}, bf16[96,3072]{1,0:T(8,128)(2,1)}, bf16[96,768]{1,0:T(8,128)(2,1)}, bf16[96,768]{1,0:T(8,128)(2,1)}, bf16[96,768...) custom-call(s32[3]{0:T(128)} %pad_add_fusion.lens_ref.refs_0_, ...), custom_call_target="tpu_custom_call" | custom-call | tf_op jit(solution)/shard_map/backward/pallas_call | solution.py:1284
  272.0 0.0 copy-done.16
  272.0 0.0 copy-done.18
  272.0 1.4 fusion
  273.5 0.0 copy-start.15
  273.5 0.0 copy-done.17
  273.5 0.0 copy-start.8
  273.5 0.6 multiply_add_fusion.6
  274.1 0.9 slice_dynamic-update-slice_fusion.8
  275.0 0.8 slice_dynamic-update-slice_fusion.7
  275.8 0.8 slice_dynamic-update-slice_fusion.6
  276.6 0.8 slice_dynamic-update-slice_fusion.5
  277.4 0.8 slice_dynamic-update-slice_fusion.4
  278.2 0.8 slice_dynamic-update-slice_fusion.3
  279.0 0.8 slice_dynamic-update-slice_fusion.2
  279.8 0.8 slice_dynamic-update-slice_fusion.1
  280.6 0.8 slice_dynamic-update-slice_fusion
  281.4 0.9 constant_dynamic-update-slice_fusion.1
  282.3 1.1 constant_dynamic-update-slice_fusion
  283.4 0.0 copy-done.15
  283.4 0.0 copy-done.8
  283.4 0.0 copy-done.5
  283.4 0.0 copy-start.9
  283.5 0.0 copy-start.6
  283.5 3.1 %fusion.1 = (bf16[384,768]{1,0:T(8,128)(2,1)}, f32[384,768]{1,0:T(8,128)S(1)}, f32[384,768]{1,0:T(8,128)}, f32[384,768]{1,0:T(8,128)}) fusion(f32[384,768]{1,0:T(8,128)S(1)} %copy-done.5, f32[384,768]{1,0:T(8,128)S(1)} %copy-done.8, bf16[384,768]{1,0:T(8,128)(2,1)} %get-tuple-element.79), kind=kLoop, calls=%fused_computation.30 | loop fusion | flops 2949120 | bytes 7077888 | tf_op jit(solution)/shard_map/convert_element_type | solution.py:1383
  286.6 0.0 copy-start.4
  286.6 0.0 copy-done.9
  286.6 0.0 copy-start.3
  286.6 1.2 multiply_add_fusion.3
  287.8 0.2 copy-done.4
  288.0 0.0 copy-done.6
  288.0 1.1 copy-done.3
  289.1 0.0 copy-start.7
  289.1 3.3 %fusion.2 = (bf16[96,6144]{1,0:T(8,128)(2,1)}, f32[96,6144]{1,0:T(8,128)S(1)}, f32[96,6144]{1,0:T(8,128)}, f32[96,6144]{1,0:T(8,128)}) fusion(f32[96,6144]{1,0:T(8,128)S(1)} %copy-done.3, f32[96,6144]{1,0:T(8,128)S(1)} %copy-done.6, bf16[96,6144]{1,0:T(8,128)(2,1)S(1)} %constant_dynamic-update-slice_fusion), kind=kLoop, calls=%fused_computation.31 | loop fusion | flops 5898240 | bytes 14155776 | tf_op jit(solution)/shard_map/convert_element_type | solution.py:1383
  292.4 0.0 copy-start.2
  292.5 0.0 copy-done.7
  292.5 1.8 multiply_add_fusion
  294.2 0.4 copy-done.2
  294.6 0.0 copy-done.13
  294.6 0.0 copy-start.12
  294.6 0.9 copy.49
  295.5 0.5 copy-done.12
  296.1 0.0 copy-start.11
  296.1 0.9 copy.50
  296.9 0.5 copy-done.11
  297.5 0.0 copy-start.10
  297.5 0.9 copy.51
  298.4 0.5 copy-done.10
  298.9 0.9 copy.52
  299.8 0.0 copy-done.1
  (5 shorter events, 0.0 us)
Async XLA Ops:
  0.7 0.7 copy-start
  6.6 0.6 copy-start.14
  143.4 128.6 %copy-start.16 = (f32[96,12]{0,1:T(8,128)S(1)}, f32[96,12]{0,1:T(8,128)}, u32[]{:S(2)}) copy-start(f32[96,12]{0,1:T(8,128)} %param.23) | copy-start | bytes 13828
  143.4 128.6 %copy-start.18 = (f32[96,12]{0,1:T(8,128)S(1)}, f32[96,12]{0,1:T(8,128)}, u32[]{:S(2)}) copy-start(f32[96,12]{0,1:T(8,128)} %param.26) | copy-start | bytes 13828
  143.4 130.0 %copy-start.17 = (f32[96,12]{0,1:T(8,128)S(1)}, f32[96,12]{0,1:T(8,128)}, u32[]{:S(2)}) copy-start(f32[96,12]{0,1:T(8,128)} %param.29) | copy-start | bytes 13828
  273.5 10.0 %copy-start.15 = (f32[96,12]{0,1:T(8,128)}, f32[96,12]{0,1:T(8,128)S(1)}, u32[]{:S(2)}) copy-start(f32[96,12]{0,1:T(8,128)S(1)} %get-tuple-element.129) | copy-start | bytes 13828
  273.5 10.0 %copy-start.8 = (f32[384,768]{1,0:T(8,128)S(1)}, f32[384,768]{1,0:T(8,128)}, u32[]{:S(2)}) copy-start(f32[384,768]{1,0:T(8,128)} %param.25) | copy-start | bytes 3538948
  274.1 9.4 %copy-start.5 = (f32[384,768]{1,0:T(8,128)S(1)}, f32[384,768]{1,0:T(8,128)}, u32[]{:S(2)}) copy-start(f32[384,768]{1,0:T(8,128)} %down_ref.1) | copy-start | bytes 3538948
  283.4 3.1 %copy-start.9 = (f32[384,768]{1,0:T(8,128)S(1)}, f32[384,768]{1,0:T(8,128)}, u32[]{:S(2)}) copy-start(f32[384,768]{1,0:T(8,128)} %param.28) | copy-start | bytes 3538948
  283.5 4.5 %copy-start.6 = (f32[96,6144]{1,0:T(8,128)S(1)}, f32[96,6144]{1,0:T(8,128)}, u32[]{:S(2)}) copy-start(f32[96,6144]{1,0:T(8,128)} %param.24) | copy-start | bytes 7077892
  286.6 1.4 copy-start.4
  286.6 2.5 copy-start.3
  289.1 3.3 %copy-start.7 = (f32[96,6144]{1,0:T(8,128)S(1)}, f32[96,6144]{1,0:T(8,128)}, u32[]{:S(2)}) copy-start(f32[96,6144]{1,0:T(8,128)} %param.27) | copy-start | bytes 7077892
  292.4 2.2 copy-start.2
  292.5 2.2 copy-start.13
  294.6 1.4 copy-start.12
  296.1 1.4 copy-start.11
  297.5 1.4 copy-start.10
  297.5 2.3 copy-start.1
